TPU v7x, 32 devices: a whole 2x2x4 slice. The times are simulated.
32 devices in a mesh: own: 8 (over y, x, core), dp: 4 (over z).
Axes of the slice: x: 2, y: 2, z: 4, core: 2. Of those that a mesh axis runs over, the one named last changes fastest.
Arguments:
- tokens: bfloat16 [8192, 640], P(('dp', 'own')), may hold values from -6 to 6
- cotangent: bfloat16 [8192, 640], P(('dp', 'own')), may hold values from -6 to 6
- lengths: int32 [4, 4], P('dp'), may hold values from 1 to 1024, 2048 in all within a row
- row_packed_slot: int32 [4, 2048], P('dp'), may hold values from 0 to 2047, as said below
- shared_attention_matrix: bfloat16 [640, 1536], P('own'), may hold values from -0.25 to 0.25
- shared_output_matrix: bfloat16 [1024, 640], P('own'), may hold values from -0.1875 to 0.1875
- shared_gate_up_matrix: bfloat16 [640, 4096], P('own'), may hold values from -0.25 to 0.25
- shared_down_matrix: bfloat16 [2048, 640], P('own'), may hold values from -0.125 to 0.125
- norm_gain_table: bfloat16 [4, 640], P(None, 'own'), may hold values from 0.25 to 1.75
- query_key_gains: bfloat16 [2, 256], P(None, 'own'), may hold values from 0.25 to 1.75
- adapter_attention_first: bfloat16 [2, 640, 768], P(None, 'own'), may hold values from -0.25 to 0.25
- adapter_query_second: bfloat16 [2, 256, 1024], P(None, 'own'), may hold values from -0.1875 to 0.1875
- adapter_key_value_second: bfloat16 [2, 2, 256, 256], P(None, None, 'own'), may hold values from -0.1875 to 0.1875
- adapter_output_first: bfloat16 [2, 1024, 256], P(None, 'own'), may hold values from -0.1875 to 0.1875
- adapter_output_second: bfloat16 [2, 256, 640], P(None, 'own'), may hold values from -0.1875 to 0.1875
- adapter_gate_first: bfloat16 [2, 640, 512], P(None, 'own'), may hold values from -0.25 to 0.25
- adapter_gate_second: bfloat16 [2, 2, 256, 2048], P(None, None, 'own'), may hold values from -0.1875 to 0.1875
- adapter_down_first: bfloat16 [2, 2048, 256], P(None, 'own'), may hold values from -0.125 to 0.125
- adapter_down_second: bfloat16 [2, 256, 640], P(None, 'own'), may hold values from -0.1875 to 0.1875
Outputs:
- mixed: bfloat16 [8192, 640], P(('dp', 'own'))
- tokens_grad: bfloat16 [8192, 640], P(('dp', 'own'))
- qkv_weight_grad: float32 [640, 1536], P('own')
- out_weight_grad: float32 [1024, 640], P('own')
- gate_up_weight_grad: float32 [640, 4096], P('own')
- down_weight_grad: float32 [2048, 640], P('own')
- norm_gains_grad: float32 [4, 640], P(None, 'own')
- qk_gains_grad: float32 [2, 256], P(None, 'own')
- lora_a_qkv_grad: float32 [2, 640, 768], P(None, 'own')
- lora_b_q_grad: float32 [2, 256, 1024], P(None, 'own')
- lora_b_kv_grad: float32 [2, 2, 256, 256], P(None, None, 'own')
- lora_a_out_grad: float32 [2, 1024, 256], P(None, 'own')
- lora_b_out_grad: float32 [2, 256, 640], P(None, 'own')
- lora_a_gu_grad: float32 [2, 640, 512], P(None, 'own')
- lora_b_gu_grad: float32 [2, 2, 256, 2048], P(None, None, 'own')
- lora_a_down_grad: float32 [2, 2048, 256], P(None, 'own')
- lora_b_down_grad: float32 [2, 256, 640], P(None, 'own')
Inputs may be any that keep to these rules, and one draw needn't show every extreme that they name: The lengths of a group sum to 2048; its sequences fill slots 0 to 2047 in order. Each slot of a group appears once in its row of row_packed_slot. Rows 256 * j to 256 * j + 255 of a group lie on index j of own, and their slots all leave the same remainder when divided by 8.
All inputs are finite; a program needn't handle non-finite values.
Results may differ from a plain program's by a relative error of at most 0.029.
Values may be sent and summed in bfloat16 or wider, within the bound.
No kernel may reach another device: no remote copies, remote signals or barrier semaphores. Data moves between devices by JAX's collectives and lax.ppermute only.
A program may use at most 192 MiB of HBM per device.

v0:
```python
import math

import jax
import jax.numpy as jnp
from jax import lax
from jax.sharding import PartitionSpec as P

HEAD_SIZE = 256


EPS = 1e-06
THETA = 1000000.0
MASKED = -1e30


def for_sending(value):

    def short(part):
        return part.astype(jnp.bfloat16) if part.dtype == jnp.float32 else part

    return jax.tree.map(short, value)


def matrix_product(left, right):
    return jnp.dot(left, right, preferred_element_type=jnp.float32)


def interior_rows(left, right):
    return lax.dot_general(
        left, right, (((0,), (0,)), ((), ())), preferred_element_type=jnp.float32
    )


def inner_cols(left, right):
    return lax.dot_general(
        left, right, (((1,), (1,)), ((), ())), preferred_element_type=jnp.float32
    )


def rms_gain(values, gain):
    return values * lax.rsqrt(jnp.mean(values * values, axis=-1, keepdims=True) + EPS) * gain


def gated_gelu(gate_up_output):
    half_width = gate_up_output.shape[-1] // 2
    return (
        jax.nn.gelu(gate_up_output[..., :half_width], approximate=True)
        * gate_up_output[..., half_width:]
    )


def locate(slots, seq_lengths):
    ends = jnp.cumsum(seq_lengths)
    starts = ends - seq_lengths
    segment = jnp.sum((slots[:, None] >= ends[None, :]).astype(jnp.int32), axis=1)
    tree_member = segment[:, None] == jnp.arange(seq_lengths.shape[0], dtype=jnp.int32)[None, :]
    position = slots - jnp.sum(jnp.where(tree_member, starts[None, :], 0), axis=1)
    return (segment, position)


def rotary(position, head_extent):
    inverse = THETA ** (-jnp.arange(head_extent // 2, dtype=jnp.float32) * 2.0 / head_extent)
    angles = position.astype(jnp.float32)[:, None] * inverse[None, :]
    return (jnp.cos(angles), jnp.sin(angles))


def rotate(values, cos_table, sin_table):
    half_width = values.shape[-1] // 2
    leading = values[..., :half_width]
    trailing = values[..., half_width:]
    return jnp.concatenate(
        [leading * cos_table - trailing * sin_table, trailing * cos_table + leading * sin_table],
        axis=-1,
    )


def split_heads(attention_projected, qk_gain, cos_table, sin_table):
    head_extent = qk_gain.shape[1]
    query_span_width = attention_projected.shape[1] - 2 * head_extent
    query = attention_projected[:, :query_span_width].reshape(
        attention_projected.shape[0], query_span_width // head_extent, head_extent
    )
    key_rows = attention_projected[:, query_span_width : query_span_width + head_extent]
    value_rows = attention_projected[:, query_span_width + head_extent :]
    query = rotate(rms_gain(query, qk_gain[0]), cos_table[:, None, :], sin_table[:, None, :])
    key_rows = rotate(rms_gain(key_rows, qk_gain[1]), cos_table, sin_table)
    return (query, key_rows, value_rows)


def scored(query, key_block, seg_block, pos_block, seg_query, pos_query):
    softmax_scale = query.shape[2] ** (-0.5)
    scores = (
        jnp.einsum("thd,kd->thk", query, key_block, preferred_element_type=jnp.float32)
        * softmax_scale
    )
    allowed = (
        (seg_query[:, None] == seg_block[None, :]) & (pos_block[None, :] <= pos_query[:, None])
    )[:, None, :]
    return (jnp.where(allowed, scores, MASKED), allowed)


def stacked_keys(keys_all, values_all, seg_all, pos_all):
    group_rows, head_extent = keys_all.shape
    block_rows = math.gcd(group_rows, 512)
    blocks = group_rows // block_rows
    return (
        keys_all.reshape(blocks, block_rows, head_extent),
        values_all.reshape(blocks, block_rows, head_extent),
        seg_all.reshape(blocks, block_rows),
        pos_all.reshape(blocks, block_rows),
    )


def attend(query, keys_all, values_all, context):
    seg_query, pos_query, seg_all, pos_all = context[:4]
    stacked = stacked_keys(keys_all, values_all, seg_all, pos_all)

    def measure(carry, pieces):
        highest, totals = carry
        scores, allowed = scored(query, pieces[0], pieces[2], pieces[3], seg_query, pos_query)
        newest = jnp.maximum(highest, jnp.max(scores, axis=-1))
        totals = totals * jnp.exp(highest - newest) + jnp.sum(
            jnp.where(allowed, jnp.exp(scores - newest[..., None]), 0.0), axis=-1
        )
        return ((newest, totals), None)

    start = jnp.full(query.shape[:2], MASKED, jnp.float32)
    (highest, totals), _ = lax.scan(
        measure, (start, jnp.zeros(query.shape[:2], jnp.float32)), stacked
    )
    logsum = highest + jnp.log(totals)

    def mixing(carry, pieces):
        scores, allowed = scored(query, pieces[0], pieces[2], pieces[3], seg_query, pos_query)
        probs = jnp.where(allowed, jnp.exp(scores - logsum[..., None]), 0.0).astype(jnp.bfloat16)
        return (
            carry + jnp.einsum("thk,kd->thd", probs, pieces[1], preferred_element_type=jnp.float32),
            None,
        )

    attended, _ = lax.scan(mixing, jnp.zeros(query.shape, jnp.float32), stacked)
    return (attended, logsum)


def attend_back(query, keys_all, values_all, context, logsum, attended, heads_grad):
    seg_query, pos_query, seg_all, pos_all = context[:4]
    group_rows, head_extent = keys_all.shape
    softmax_scale = head_extent ** (-0.5)
    stacked = stacked_keys(keys_all, values_all, seg_all, pos_all)
    row_dot = jnp.sum(heads_grad.astype(jnp.float32) * attended, axis=-1)

    def stepping(query_grad, pieces):
        scores, allowed = scored(query, pieces[0], pieces[2], pieces[3], seg_query, pos_query)
        probs = jnp.where(allowed, jnp.exp(scores - logsum[..., None]), 0.0)
        probs_grad = jnp.einsum(
            "thd,kd->thk", heads_grad, pieces[1], preferred_element_type=jnp.float32
        )
        scores_grad = (probs * (probs_grad - row_dot[..., None])).astype(jnp.bfloat16)
        query_grad = (
            query_grad
            + jnp.einsum("thk,kd->thd", scores_grad, pieces[0], preferred_element_type=jnp.float32)
            * softmax_scale
        )
        key_grad = (
            jnp.einsum("thk,thd->kd", scores_grad, query, preferred_element_type=jnp.float32)
            * softmax_scale
        )
        value_grad = jnp.einsum(
            "thk,thd->kd",
            probs.astype(jnp.bfloat16),
            heads_grad,
            preferred_element_type=jnp.float32,
        )
        return (query_grad, (key_grad, value_grad))

    query_grad, (key_parts, value_parts) = lax.scan(
        stepping, jnp.zeros(query.shape, jnp.float32), stacked
    )
    key_grad, value_grad = (
        lax.psum_scatter(
            key_parts.reshape(group_rows, head_extent).astype(jnp.bfloat16),
            "own",
            scatter_dimension=0,
            tiled=True,
        ).astype(jnp.float32),
        lax.psum_scatter(
            value_parts.reshape(group_rows, head_extent).astype(jnp.bfloat16),
            "own",
            scatter_dimension=0,
            tiled=True,
        ).astype(jnp.float32),
    )
    return (query_grad, key_grad, value_grad)


def block_forward(stream_in, params, context):
    (
        attention_matrix,
        out_w,
        gate_up_matrix,
        down_w,
        norm_gain,
        qk_gain,
        qkv_a,
        query_up_factor,
        key_value_factor,
        out_a,
        out_b,
        gate_a,
        gate_up_factor,
        down_a,
        down_b,
    ) = params
    cos_table, sin_table = (context[4], context[5])
    norm_scale = norm_gain.astype(jnp.float32)
    qk_scale = qk_gain.astype(jnp.float32)
    adapter_rank = query_up_factor.shape[0]
    count = stream_in.shape[0]
    attention_input = rms_gain(stream_in, norm_scale[0]).astype(jnp.bfloat16)
    attention_middle_part = matrix_product(attention_input, qkv_a).astype(jnp.bfloat16)
    attention_projected = matrix_product(attention_input, attention_matrix) + jnp.concatenate(
        [
            matrix_product(attention_middle_part[:, :adapter_rank], query_up_factor),
            matrix_product(
                attention_middle_part[:, adapter_rank : 2 * adapter_rank], key_value_factor[0]
            ),
            matrix_product(attention_middle_part[:, 2 * adapter_rank :], key_value_factor[1]),
        ],
        axis=1,
    )
    query, key_rows, value_rows = split_heads(attention_projected, qk_scale, cos_table, sin_table)
    query = query.astype(jnp.bfloat16)
    keys_all, values_all = (
        lax.all_gather(key_rows.astype(jnp.bfloat16), "own", axis=0, tiled=True),
        lax.all_gather(value_rows.astype(jnp.bfloat16), "own", axis=0, tiled=True),
    )
    attended, logsum = attend(query, keys_all, values_all, context)
    heads_out = attended.reshape(count, -1).astype(jnp.bfloat16)
    out_mid = matrix_product(heads_out, out_a).astype(jnp.bfloat16)
    branch = matrix_product(heads_out, out_w) + matrix_product(out_mid, out_b)
    middle = stream_in + rms_gain(branch, norm_scale[1])
    feedforward_input = rms_gain(middle, norm_scale[2]).astype(jnp.bfloat16)
    gate_middle_part = matrix_product(feedforward_input, gate_a).astype(jnp.bfloat16)
    gate_up_output = matrix_product(feedforward_input, gate_up_matrix) + jnp.concatenate(
        [
            matrix_product(gate_middle_part[:, :adapter_rank], gate_up_factor[0]),
            matrix_product(gate_middle_part[:, adapter_rank:], gate_up_factor[1]),
        ],
        axis=1,
    )
    hidden = gated_gelu(gate_up_output).astype(jnp.bfloat16)
    down_mid = matrix_product(hidden, down_a).astype(jnp.bfloat16)
    ffn_out = matrix_product(hidden, down_w) + matrix_product(down_mid, down_b)
    stream_out = middle + rms_gain(ffn_out, norm_scale[3])
    saved = (
        stream_in,
        attention_input,
        attention_middle_part,
        attention_projected,
        query,
        keys_all,
        values_all,
        attended,
        logsum,
        heads_out,
        out_mid,
        branch,
        middle,
        feedforward_input,
        gate_middle_part,
        gate_up_output,
        hidden,
        down_mid,
        ffn_out,
    )
    return (stream_out, saved)


def block_backward(out_grad, saved, params, context):
    (
        attention_matrix,
        out_w,
        gate_up_matrix,
        down_w,
        norm_gain,
        qk_gain,
        qkv_a,
        query_up_factor,
        key_value_factor,
        out_a,
        out_b,
        gate_a,
        gate_up_factor,
        down_a,
        down_b,
    ) = params
    (
        stream_in,
        attention_input,
        attention_middle_part,
        attention_projected,
        query,
        keys_all,
        values_all,
        attended,
        logsum,
        heads_out,
        out_mid,
        branch,
        middle,
        feedforward_input,
        gate_middle_part,
        gate_up_output,
        hidden,
        down_mid,
        ffn_out,
    ) = saved
    cos_table, sin_table = (context[4], context[5])
    norm_scale = norm_gain.astype(jnp.float32)
    qk_scale = qk_gain.astype(jnp.float32)
    adapter_rank = query_up_factor.shape[0]
    query_span_width = query_up_factor.shape[1]
    head_extent = qk_gain.shape[1]
    feedforward_width = gate_up_output.shape[1] // 2
    ffn_grad, gain_three = jax.vjp(rms_gain, ffn_out, norm_scale[3])[1](out_grad)
    ffn_low = ffn_grad.astype(jnp.bfloat16)
    down_w_grad = interior_rows(hidden, ffn_low)
    down_b_grad = interior_rows(down_mid, ffn_low)
    down_mid_grad = inner_cols(ffn_low, down_b).astype(jnp.bfloat16)
    down_a_grad = interior_rows(hidden, down_mid_grad)
    hidden_grad = inner_cols(ffn_low, down_w) + inner_cols(down_mid_grad, down_a)
    gate_up_output_gradient = jax.vjp(gated_gelu, gate_up_output)[1](hidden_grad)[0].astype(
        jnp.bfloat16
    )
    gate_up_w_grad = interior_rows(feedforward_input, gate_up_output_gradient)
    gate_b_grad = jnp.stack(
        [
            interior_rows(
                gate_middle_part[:, :adapter_rank], gate_up_output_gradient[:, :feedforward_width]
            ),
            interior_rows(
                gate_middle_part[:, adapter_rank:], gate_up_output_gradient[:, feedforward_width:]
            ),
        ]
    )
    gate_mid_grad = jnp.concatenate(
        [
            inner_cols(gate_up_output_gradient[:, :feedforward_width], gate_up_factor[0]),
            inner_cols(gate_up_output_gradient[:, feedforward_width:], gate_up_factor[1]),
        ],
        axis=1,
    ).astype(jnp.bfloat16)
    gate_a_grad = interior_rows(feedforward_input, gate_mid_grad)
    ffn_in_grad = inner_cols(gate_up_output_gradient, gate_up_matrix) + inner_cols(
        gate_mid_grad, gate_a
    )
    middle_part, gain_two = jax.vjp(rms_gain, middle, norm_scale[2])[1](ffn_in_grad)
    middle_grad = out_grad + middle_part
    branch_grad, gain_one = jax.vjp(rms_gain, branch, norm_scale[1])[1](middle_grad)
    branch_low = branch_grad.astype(jnp.bfloat16)
    out_w_grad = interior_rows(heads_out, branch_low)
    out_b_grad = interior_rows(out_mid, branch_low)
    out_mid_grad = inner_cols(branch_low, out_b).astype(jnp.bfloat16)
    out_a_grad = interior_rows(heads_out, out_mid_grad)
    heads_grad = (
        (inner_cols(branch_low, out_w) + inner_cols(out_mid_grad, out_a))
        .astype(jnp.bfloat16)
        .reshape(attended.shape)
    )
    query_grad, key_grad, value_grad = attend_back(
        query, keys_all, values_all, context, logsum, attended, heads_grad
    )

    def heads_of(raw_values, gain_values):
        return split_heads(raw_values, gain_values, cos_table, sin_table)

    raw_grad, qk_grad = jax.vjp(heads_of, attention_projected, qk_scale)[1](
        (query_grad, key_grad, value_grad)
    )
    lowrank_projected = raw_grad.astype(jnp.bfloat16)
    qkv_w_grad = interior_rows(attention_input, lowrank_projected)
    query_up_factor_gradient = interior_rows(
        attention_middle_part[:, :adapter_rank], lowrank_projected[:, :query_span_width]
    )
    kv_b_grad = jnp.stack(
        [
            interior_rows(
                attention_middle_part[:, adapter_rank : 2 * adapter_rank],
                lowrank_projected[:, query_span_width : query_span_width + head_extent],
            ),
            interior_rows(
                attention_middle_part[:, 2 * adapter_rank :],
                lowrank_projected[:, query_span_width + head_extent :],
            ),
        ]
    )
    qkv_mid_grad = jnp.concatenate(
        [
            inner_cols(lowrank_projected[:, :query_span_width], query_up_factor),
            inner_cols(
                lowrank_projected[:, query_span_width : query_span_width + head_extent],
                key_value_factor[0],
            ),
            inner_cols(lowrank_projected[:, query_span_width + head_extent :], key_value_factor[1]),
        ],
        axis=1,
    ).astype(jnp.bfloat16)
    qkv_a_grad = interior_rows(attention_input, qkv_mid_grad)
    attn_in_grad = inner_cols(lowrank_projected, attention_matrix) + inner_cols(qkv_mid_grad, qkv_a)
    stream_part, gain_zero = jax.vjp(rms_gain, stream_in, norm_scale[0])[1](attn_in_grad)
    stream_grad = middle_grad + stream_part
    gradients = (
        qkv_w_grad,
        out_w_grad,
        gate_up_w_grad,
        down_w_grad,
        jnp.stack([gain_zero, gain_one, gain_two, gain_three]),
        qk_grad,
        qkv_a_grad,
        query_up_factor_gradient,
        kv_b_grad,
        out_a_grad,
        out_b_grad,
        gate_a_grad,
        gate_b_grad,
        down_a_grad,
        down_b_grad,
    )
    return (stream_grad, gradients)


def shards(
    tokens,
    cotangent,
    lengths,
    row_packed_slot,
    shared_attention_matrix,
    shared_output_matrix,
    shared_gate_up_matrix,
    shared_down_matrix,
    norm_gain_table,
    query_key_gains,
    adapter_attention_first,
    adapter_query_second,
    adapter_key_value_second,
    adapter_output_first,
    adapter_output_second,
    adapter_gate_first,
    adapter_gate_second,
    adapter_down_first,
    adapter_down_second,
):
    count = tokens.shape[0]
    seg_all, pos_all = locate(row_packed_slot[0], lengths[0])
    offset = lax.axis_index("own") * count
    seg_query = lax.dynamic_slice_in_dim(seg_all, offset, count)
    pos_query = lax.dynamic_slice_in_dim(pos_all, offset, count)
    cos_table, sin_table = rotary(pos_query, HEAD_SIZE)
    context = (seg_query, pos_query, seg_all, pos_all, cos_table, sin_table)

    def fetch(repeat_along):
        return (
            lax.all_gather(shared_attention_matrix, "own", axis=0, tiled=True),
            lax.all_gather(shared_output_matrix, "own", axis=0, tiled=True),
            lax.all_gather(shared_gate_up_matrix, "own", axis=0, tiled=True),
            lax.all_gather(shared_down_matrix, "own", axis=0, tiled=True),
            lax.all_gather(norm_gain_table, "own", axis=1, tiled=True),
            lax.all_gather(query_key_gains, "own", axis=1, tiled=True),
            lax.all_gather(adapter_attention_first[repeat_along], "own", axis=0, tiled=True),
            lax.all_gather(adapter_query_second[repeat_along], "own", axis=0, tiled=True),
            lax.all_gather(adapter_key_value_second[repeat_along], "own", axis=1, tiled=True),
            lax.all_gather(adapter_output_first[repeat_along], "own", axis=0, tiled=True),
            lax.all_gather(adapter_output_second[repeat_along], "own", axis=0, tiled=True),
            lax.all_gather(adapter_gate_first[repeat_along], "own", axis=0, tiled=True),
            lax.all_gather(adapter_gate_second[repeat_along], "own", axis=1, tiled=True),
            lax.all_gather(adapter_down_first[repeat_along], "own", axis=0, tiled=True),
            lax.all_gather(adapter_down_second[repeat_along], "own", axis=0, tiled=True),
        )

    first_params = fetch(0)
    stream_in = tokens.astype(jnp.float32)
    stream_mid, unused = block_forward(stream_in, first_params, context)
    later_params = fetch(1)
    stream_out, saved_second = block_forward(stream_mid, later_params, context)
    mid_grad, grads_second = block_backward(
        cotangent.astype(jnp.float32), saved_second, later_params, context
    )
    again_params = fetch(0)
    redone, saved_first = block_forward(stream_in, again_params, context)
    stream_grad, grads_first = block_backward(mid_grad, saved_first, again_params, context)
    totals = tuple((grads_first[index] + grads_second[index] for index in range(6))) + tuple(
        (jnp.stack([grads_first[index], grads_second[index]]) for index in range(6, 15))
    )
    owned = (
        lax.psum_scatter(
            totals[0].astype(jnp.bfloat16), "own", scatter_dimension=0, tiled=True
        ).astype(jnp.float32),
        lax.psum_scatter(
            totals[1].astype(jnp.bfloat16), "own", scatter_dimension=0, tiled=True
        ).astype(jnp.float32),
        lax.psum_scatter(
            totals[2].astype(jnp.bfloat16), "own", scatter_dimension=0, tiled=True
        ).astype(jnp.float32),
        lax.psum_scatter(
            totals[3].astype(jnp.bfloat16), "own", scatter_dimension=0, tiled=True
        ).astype(jnp.float32),
        lax.psum_scatter(
            totals[4].astype(jnp.bfloat16), "own", scatter_dimension=1, tiled=True
        ).astype(jnp.float32),
        lax.psum_scatter(
            totals[5].astype(jnp.bfloat16), "own", scatter_dimension=1, tiled=True
        ).astype(jnp.float32),
        lax.psum_scatter(
            totals[6].astype(jnp.bfloat16), "own", scatter_dimension=1, tiled=True
        ).astype(jnp.float32),
        lax.psum_scatter(
            totals[7].astype(jnp.bfloat16), "own", scatter_dimension=1, tiled=True
        ).astype(jnp.float32),
        lax.psum_scatter(
            totals[8].astype(jnp.bfloat16), "own", scatter_dimension=2, tiled=True
        ).astype(jnp.float32),
        lax.psum_scatter(
            totals[9].astype(jnp.bfloat16), "own", scatter_dimension=1, tiled=True
        ).astype(jnp.float32),
        lax.psum_scatter(
            totals[10].astype(jnp.bfloat16), "own", scatter_dimension=1, tiled=True
        ).astype(jnp.float32),
        lax.psum_scatter(
            totals[11].astype(jnp.bfloat16), "own", scatter_dimension=1, tiled=True
        ).astype(jnp.float32),
        lax.psum_scatter(
            totals[12].astype(jnp.bfloat16), "own", scatter_dimension=2, tiled=True
        ).astype(jnp.float32),
        lax.psum_scatter(
            totals[13].astype(jnp.bfloat16), "own", scatter_dimension=1, tiled=True
        ).astype(jnp.float32),
        lax.psum_scatter(
            totals[14].astype(jnp.bfloat16), "own", scatter_dimension=1, tiled=True
        ).astype(jnp.float32),
    )
    summed = jax.tree.map(lambda part: part.astype(jnp.float32), lax.psum(for_sending(owned), "dp"))
    return (stream_out.astype(jnp.bfloat16), stream_grad.astype(jnp.bfloat16)) + tuple(summed)


def solution(mesh):
    in_specs = (
        P(("dp", "own"), None),
        P(("dp", "own"), None),
        P("dp", None),
        P("dp", None),
        P("own", None),
        P("own", None),
        P("own", None),
        P("own", None),
        P(None, "own"),
        P(None, "own"),
        P(None, "own", None),
        P(None, "own", None),
        P(None, None, "own", None),
        P(None, "own", None),
        P(None, "own", None),
        P(None, "own", None),
        P(None, None, "own", None),
        P(None, "own", None),
        P(None, "own", None),
    )
    out_specs = (
        P(("dp", "own"), None),
        P(("dp", "own"), None),
        P("own", None),
        P("own", None),
        P("own", None),
        P("own", None),
        P(None, "own"),
        P(None, "own"),
        P(None, "own", None),
        P(None, "own", None),
        P(None, None, "own", None),
        P(None, "own", None),
        P(None, "own", None),
        P(None, "own", None),
        P(None, None, "own", None),
        P(None, "own", None),
        P(None, "own", None),
    )
    return jax.shard_map(shards, mesh=mesh, in_specs=in_specs, out_specs=out_specs, check_vma=False)
```

profile of v0, /device:TPU:0, one launch (start us, length us, event | category | flops | bytes accessed | tf_op | source)
XLA Modules:
  0.0 1466.2 jit_solution(12454290629717297221)
XLA Ops:
  8.0 10.5 all-gather.18
  19.4 8.6 all-gather.19
  29.5 9.3 all-gather.2
  44.5 9.6 all-gather.1
  56.0 10.3 all-gather
  82.2 10.7 all-gather.3
  93.5 9.7 all-gather.4
  103.9 10.6 all-gather.5
  116.0 9.9 all-gather.8
  125.9 10.0 all-gather.11
  135.9 11.6 all-gather.9
  147.5 10.3 all-gather.10
  160.7 12.9 while.87
  173.7 18.1 %while.88 = (s32[]{:T(128)}, f32[256,4,256]{2,0,1:T(8,128)}, s32[256]{0:T(256)S(1)}, s32[4,512]{1,0:T(4,128)S(1)}, s32[4,512]{1,0:T(4,128)}, /*index=5*/s32[256]...) while((s32[]{:T(128)}, f32[256,4,256]{2,0,1:T(8,128)}, ...), condition=%wide.region_11.12_spmd.clone, body=%wide.region_10.11_spmd.clone.sunk | while | flops 540409856 | bytes 3427978 | solution.py:141
  203.2 22.1 %all-gather.41.cloned.1.call-done = bf16[640,4096]{1,0:T(8,128)(2,1)} async-done(((bf16[80,4096]{1,0:T(8,128)(2,1)}), bf16[640,4096]{1,0:T(8,128)(2,1)}) %all-gather.41.cloned.1.call-update) | async-done | bytes 5242896 | tf_op jit(solution)/shard_map/all_gather | solution.py:465
  225.3 5.6 convolution_add_fusion.3
  233.7 17.6 %all-gather.51.cloned.1.call-done = bf16[1,2048,256]{2,1,0:T(8,128)(2,1)} async-done(((bf16[1,256,256]{2,1,0:T(8,128)(2,1)}), bf16[1,2048,256]{2,1,0:T(8,128)(2,1)}) %all-gather.51.cloned.1.call-update) | async-done | bytes 1048592 | tf_op jit(solution)/shard_map/all_gather | solution.py:476
  253.3 30.0 %all-gather.43.cloned.1.call-done = bf16[2048,640]{1,0:T(8,128)(2,1)} async-done(((bf16[256,640]{1,0:T(8,128)(2,1)}), bf16[2048,640]{1,0:T(8,128)(2,1)}) %all-gather.43.cloned.1.call-update) | async-done | bytes 2621456 | tf_op jit(solution)/shard_map/all_gather | solution.py:466
  295.1 22.7 %all-gather.12 = bf16[1,1024,256]{2,1,0:T(8,128)(2,1)} all-gather(bf16[1,128,256]{2,1,0:T(8,128)(2,1)S(1)} %copy-done.182), channel_id=14, replica_groups=mesh['own'=8,'dp'=4] {'own'}, dimensions={1}, use_global_device_ids=true | all-gather | bytes 589824 | tf_op jit(solution)/shard_map/all_gather | solution.py:472
  317.8 9.7 all-gather.13
  327.5 10.8 all-gather.14
  338.3 9.7 all-gather.17
  351.9 12.7 while.89
  364.6 18.1 %while.90 = (s32[]{:T(128)}, f32[256,4,256]{2,0,1:T(8,128)}, s32[256]{0:T(256)S(1)}, s32[4,512]{1,0:T(4,128)S(1)}, s32[4,512]{1,0:T(4,128)}, /*index=5*/s32[256]...) while((s32[]{:T(128)}, f32[256,4,256]{2,0,1:T(8,128)}, ...), condition=%wide.region_23.24_spmd.clone, body=%wide.region_22.23_spmd.clone.sunk | while | flops 540409856 | bytes 3427978 | solution.py:141
  391.3 4.3 convolution_add_fusion.2
  423.1 40.0 %while.91 = (s32[]{:T(128)}, f32[256,4,256]{2,0,1:T(8,128)}, bf16[4,512,256]{2,1,0:T(8,128)(2,1)}, bf16[4,512,256]{2,1,0:T(8,128)(2,1)}, s32[256]{0:T(256)S(1)},...) while((s32[]{:T(128)}, f32[256,4,256]{2,0,1:T(8,128)}, ...), condition=%wide.region_32.33_spmd.clone, body=%wide.region_31.32_spmd.clone.sunk | while | flops 1347682304 | bytes 38820236 | solution.py:176
  466.8 32.5 %reduce-scatter.26.cloned.1.call-done = bf16[256,256]{1,0:T(8,128)(2,1)} async-done(((bf16[2048,256]{1,0:T(8,128)(2,1)}), bf16[256,256]{1,0:T(8,128)(2,1)}) %reduce-scatter.26.cloned.1.call-update) | async-done | bytes 131088 | tf_op jit(solution)/shard_map/reduce_scatter | solution.py:180
  503.6 34.7 %reduce-scatter.24.cloned.1.call-done = bf16[256,256]{1,0:T(8,128)(2,1)} async-done(((bf16[2048,256]{1,0:T(8,128)(2,1)}), bf16[256,256]{1,0:T(8,128)(2,1)}) %reduce-scatter.24.cloned.1.call-update) | async-done | bytes 131088 | tf_op jit(solution)/shard_map/reduce_scatter | solution.py:186
  562.5 40.2 %while.92 = (s32[]{:T(128)}, f32[256,4,256]{2,0,1:T(8,128)}, bf16[4,512,256]{2,1,0:T(8,128)(2,1)}, bf16[4,512,256]{2,1,0:T(8,128)(2,1)}, s32[256]{0:T(256)S(1)},...) while((s32[]{:T(128)}, f32[256,4,256]{2,0,1:T(8,128)}, ...), condition=%wide.region_43.44_spmd.clone, body=%wide.region_42.43_spmd.clone.sunk | while | flops 1347682304 | bytes 38820236 | solution.py:176
  618.6 20.3 %reduce-scatter.30.cloned.1.call-done = bf16[256,256]{1,0:T(8,128)(2,1)} async-done(((bf16[2048,256]{1,0:T(8,128)(2,1)}), bf16[256,256]{1,0:T(8,128)(2,1)}) %reduce-scatter.30.cloned.1.call-update) | async-done | bytes 131088 | tf_op jit(solution)/shard_map/reduce_scatter | solution.py:180
  642.7 35.3 %reduce-scatter.28.cloned.1.call-done = bf16[256,256]{1,0:T(8,128)(2,1)} async-done(((bf16[2048,256]{1,0:T(8,128)(2,1)}), bf16[256,256]{1,0:T(8,128)(2,1)}) %reduce-scatter.28.cloned.1.call-update) | async-done | bytes 131088 | tf_op jit(solution)/shard_map/reduce_scatter | solution.py:186
  711.6 3.9 add_convert_fusion
  721.9 31.2 %reduce-scatter.56.cloned.1.call-done = bf16[2,32,640]{2,1,0:T(8,128)(2,1)} async-done(((bf16[2,256,640]{2,1,0:T(8,128)(2,1)}), bf16[2,32,640]{2,1,0:T(8,128)(2,1)}) %reduce-scatter.56.cloned.1.call-update) | async-done | bytes 81936 | tf_op jit(solution)/shard_map/reduce_scatter | solution.py:537
  753.1 39.2 %reduce-scatter.46.cloned.1.call-done = bf16[2,128,256]{2,1,0:T(8,128)(2,1)} async-done(((bf16[2,1024,256]{2,1,0:T(8,128)(2,1)}), bf16[2,128,256]{2,1,0:T(8,128)(2,1)}) %reduce-scatter.46.cloned.1.call-update) | async-done | bytes 131088 | tf_op jit(solution)/shard_map/reduce_scatter | solution.py:522
  792.3 41.0 %reduce-scatter.34.cloned.1.call-done = bf16[128,640]{1,0:T(8,128)(2,1)} async-done(((bf16[1024,640]{1,0:T(8,128)(2,1)}), bf16[128,640]{1,0:T(8,128)(2,1)}) %reduce-scatter.34.cloned.1.call-update) | async-done | bytes 163856 | tf_op jit(solution)/shard_map/reduce_scatter | solution.py:498
  833.3 40.6 %reduce-scatter.50.cloned.1.call-done = bf16[2,80,512]{2,1,0:T(8,128)(2,1)} async-done(((bf16[2,640,512]{2,1,0:T(8,128)(2,1)}), bf16[2,80,512]{2,1,0:T(8,128)(2,1)}) %reduce-scatter.50.cloned.1.call-update) | async-done | bytes 163856 | tf_op jit(solution)/shard_map/reduce_scatter | solution.py:528
  873.9 37.7 %reduce-scatter.44.cloned.1.call-done = bf16[2,2,32,256]{3,2,1,0:T(8,128)(2,1)} async-done(((bf16[2,2,256,256]{3,2,1,0:T(8,128)(2,1)}), bf16[2,2,32,256]{3,2,1,0:T(8,128)(2,1)}) %reduce-scatter.44.cloned.1.call-update) | async-done | bytes 65552 | tf_op jit(solution)/shard_map/reduce_scatter | solution.py:519
  911.7 40.1 %reduce-scatter.42.cloned.1.call-done = bf16[2,32,1024]{2,1,0:T(8,128)(2,1)} async-done(((bf16[2,256,1024]{2,1,0:T(8,128)(2,1)}), bf16[2,32,1024]{2,1,0:T(8,128)(2,1)}) %reduce-scatter.42.cloned.1.call-update) | async-done | bytes 131088 | tf_op jit(solution)/shard_map/reduce_scatter | solution.py:516
  951.8 44.7 %reduce-scatter.54.cloned.1.call-done = bf16[2,256,256]{2,1,0:T(8,128)(2,1)} async-done(((bf16[2,2048,256]{2,1,0:T(8,128)(2,1)}), bf16[2,256,256]{2,1,0:T(8,128)(2,1)}) %reduce-scatter.54.cloned.1.call-update) | async-done | bytes 262160 | tf_op jit(solution)/shard_map/reduce_scatter | solution.py:534
  996.5 47.0 %reduce-scatter.38.cloned.1.call-done = bf16[256,640]{1,0:T(8,128)(2,1)} async-done(((bf16[2048,640]{1,0:T(8,128)(2,1)}), bf16[256,640]{1,0:T(8,128)(2,1)}) %reduce-scatter.38.cloned.1.call-update) | async-done | bytes 327696 | tf_op jit(solution)/shard_map/reduce_scatter | solution.py:504
  1043.5 43.6 %reduce-scatter.32.cloned.1.call-done = bf16[80,1536]{1,0:T(8,128)(2,1)} async-done(((bf16[640,1536]{1,0:T(8,128)(2,1)}), bf16[80,1536]{1,0:T(8,128)(2,1)}) %reduce-scatter.32.cloned.1.call-update) | async-done | bytes 245776 | tf_op jit(solution)/shard_map/reduce_scatter | solution.py:495
  1087.2 44.0 %reduce-scatter.40.cloned.1.call-done = bf16[2,80,768]{2,1,0:T(8,128)(2,1)} async-done(((bf16[2,640,768]{2,1,0:T(8,128)(2,1)}), bf16[2,80,768]{2,1,0:T(8,128)(2,1)}) %reduce-scatter.40.cloned.1.call-update) | async-done | bytes 245776 | tf_op jit(solution)/shard_map/reduce_scatter | solution.py:513
  1131.1 54.7 %reduce-scatter.52.cloned.1.call-done = bf16[2,2,32,2048]{3,2,1,0:T(8,128)(2,1)} async-done(((bf16[2,2,256,2048]{3,2,1,0:T(8,128)(2,1)}), bf16[2,2,32,2048]{3,2,1,0:T(8,128)(2,1)}) %reduce-scatter.52.cloned.1.call-update) | async-done | bytes 524304 | tf_op jit(solution)/shard_map/reduce_scatter | solution.py:531
  1185.8 60.3 %reduce-scatter.36.cloned.1.call-done = bf16[80,4096]{1,0:T(8,128)(2,1)} async-done(((bf16[640,4096]{1,0:T(8,128)(2,1)}), bf16[80,4096]{1,0:T(8,128)(2,1)}) %reduce-scatter.36.cloned.1.call-update) | async-done | bytes 655376 | tf_op jit(solution)/shard_map/reduce_scatter | solution.py:501
  1247.2 35.6 %reduce-scatter.60.cloned.1.call-done = bf16[32,2]{1,0:T(8,128)(2,1)} async-done(((bf16[256,2]{1,0:T(8,128)(2,1)}), bf16[32,2]{1,0:T(8,128)(2,1)}) %reduce-scatter.60.cloned.1.call-update) | async-done | bytes 144
  1283.6 35.0 %reduce-scatter.58.cloned.1.call-done = bf16[80,4]{1,0:T(8,128)(2,1)} async-done(((bf16[640,4]{1,0:T(8,128)(2,1)}), bf16[80,4]{1,0:T(8,128)(2,1)}) %reduce-scatter.58.cloned.1.call-update) | async-done | bytes 656
  1319.4 11.8 all-reduce.22
  1332.4 113.2 %all-reduce.26.cloned.1.call-done = (bf16[80,1536]{1,0:T(8,128)(2,1)}, bf16[128,640]{1,0:T(8,128)(2,1)}, bf16[80,4096]{1,0:T(8,128)(2,1)}, bf16[256,640]{1,0:T(8...) async-done(((bf16[80,1536]{1,0:T(8,128)(2,1)}, ...) | async-done | bytes 3080208 | tf_op jit(solution)/shard_map/psum | solution.py:541
  (1127 shorter events, 345.8 us)
Async XLA Ops:
  7.2 59.8 %copy-start.43 = (bf16[256,640]{1,0:T(8,128)(2,1)S(1)}, bf16[256,640]{1,0:T(8,128)(2,1)}, u32[]{:S(2)}) copy-start(bf16[256,640]{1,0:T(8,128)(2,1)} %param.31) | copy-start | bytes 983044
  7.2 62.3 %all-gather.33.cloned.1.call-start = ((), (), s32[]{:S(2)}) async-start(), calls=%async_computation.19 | async-start | bytes 2211840 | tf_op jit(solution)/shard_map/all_gather | solution.py:463
  7.9 152.7 %all-gather.35.cloned.1.call-start = ((), (), s32[]{:S(2)}) async-start(), calls=%async_computation.20 | async-start | bytes 1179648 | tf_op jit(solution)/shard_map/all_gather | solution.py:234
  73.5 86.2 %copy-start.94 = (f32[256,128]{1,0:T(8,128)}, f32[256,128]{1,0:T(8,128)S(1)}, u32[]{:S(2)}) copy-start(f32[256,128]{1,0:T(8,128)S(1)} %get-tuple-element.1087) | copy-start | bytes 393220
  73.5 86.2 %copy-start.97 = (f32[256,128]{1,0:T(8,128)}, f32[256,128]{1,0:T(8,128)S(1)}, u32[]{:S(2)}) copy-start(f32[256,128]{1,0:T(8,128)S(1)} %get-tuple-element.1088) | copy-start | bytes 393220
  74.2 99.5 %all-gather.37.cloned.1.call-start = ((), (), s32[]{:S(2)}) async-start(), calls=%async_computation.21 | async-start | bytes 1179648 | tf_op jit(solution)/shard_map/all_gather | solution.py:235
  75.0 119.1 %all-gather.39.cloned.1.call-start = ((), (), s32[]{:S(2)}) async-start(), calls=%async_computation.22 | async-start | bytes 1474560 | tf_op jit(solution)/shard_map/all_gather | solution.py:464
  75.5 122.7 %all-gather.49.cloned.1.call-start = ((), (), s32[]{:S(2)}) async-start(), calls=%async_computation.44 | async-start | bytes 2359296 | tf_op jit(solution)/shard_map/all_gather | solution.py:475
  76.4 148.9 %all-gather.41.cloned.1.call-start = ((), (), s32[]{:S(2)}) async-start(), calls=%async_computation.23 | async-start | bytes 5898240 | tf_op jit(solution)/shard_map/all_gather | solution.py:465
  77.0 48.8 %copy-start.203 = (bf16[1,2,32,256]{3,2,1,0:T(8,128)(2,1)S(1)}, bf16[1,2,32,256]{3,2,1,0:T(8,128)(2,1)}, u32[]{:S(2)}) copy-start(bf16[1,2,32,256]{3,2,1,0:T(8,128)(2,1)} %get-tuple-element.1083) | copy-start | bytes 98308
  77.0 58.8 %copy-start.173 = (bf16[1,80,768]{2,1,0:T(8,128)(2,1)S(1)}, bf16[1,80,768]{2,1,0:T(8,128)(2,1)}, u32[]{:S(2)}) copy-start(bf16[1,80,768]{2,1,0:T(8,128)(2,1)} %get-tuple-element.1071) | copy-start | bytes 368644
  77.1 174.2 %all-gather.51.cloned.1.call-start = ((), (), s32[]{:S(2)}) async-start(), calls=%async_computation.45 | async-start | bytes 1179648 | tf_op jit(solution)/shard_map/all_gather | solution.py:476
  77.9 205.5 %all-gather.43.cloned.1.call-start = ((), (), s32[]{:S(2)}) async-start(), calls=%async_computation.24 | async-start | bytes 2949120 | tf_op jit(solution)/shard_map/all_gather | solution.py:466
  78.6 273.3 %all-gather.45.cloned.1.call-start = ((), (), s32[]{:S(2)}) async-start(), calls=%async_computation.25 | async-start | bytes 1179648 | tf_op jit(solution)/shard_map/all_gather | solution.py:234
  82.2 65.3 %copy-start.183 = (bf16[1,32,1024]{2,1,0:T(8,128)(2,1)S(1)}, bf16[1,32,1024]{2,1,0:T(8,128)(2,1)}, u32[]{:S(2)}) copy-start(bf16[1,32,1024]{2,1,0:T(8,128)(2,1)} %get-tuple-element.1077) | copy-start | bytes 196612
  92.9 65.5 %copy-start.46 = (f32[256,1536]{1,0:T(8,128)S(1)}, f32[256,1536]{1,0:T(8,128)}, u32[]{:S(2)}) copy-start(f32[256,1536]{1,0:T(8,128)} %copy-done.45) | copy-start | bytes 4718596
  114.5 83.4 %copy-start.63 = (bf16[1,640,512]{2,1,0:T(8,128)(2,1)}, bf16[1,640,512]{2,1,0:T(8,128)(2,1)S(1)}, u32[]{:S(2)}) copy-start(bf16[1,640,512]{2,1,0:T(8,128)(2,1)S(1)} %all-gather.5) | copy-start | bytes 1966084
  197.2 89.0 %copy-start.27 = (f32[256,640]{1,0:T(8,128)}, f32[256,640]{1,0:T(8,128)S(1)}, u32[]{:S(2)}) copy-start(f32[256,640]{1,0:T(8,128)S(1)} %get-tuple-element.1022) | copy-start | bytes 1966084
  233.7 52.5 %copy-start.6 = (bf16[256,2048]{1,0:T(8,128)(2,1)}, bf16[256,2048]{1,0:T(8,128)(2,1)S(1)}, u32[]{:S(2)}) copy-start(bf16[256,2048]{1,0:T(8,128)(2,1)S(1)} %multiply_convert_fusion.1) | copy-start | bytes 3145732
  286.7 100.2 %copy-start.29 = (f32[256,640]{1,0:T(8,128)}, f32[256,640]{1,0:T(8,128)S(1)}, u32[]{:S(2)}) copy-start(f32[256,640]{1,0:T(8,128)S(1)} %get-tuple-element.1020) | copy-start | bytes 1966084
  293.0 71.6 %all-gather.47.cloned.1.call-start = ((), (), s32[]{:S(2)}) async-start(), calls=%async_computation.26 | async-start | bytes 1179648 | tf_op jit(solution)/shard_map/all_gather | solution.py:235
  293.7 95.1 %all-gather.53.cloned.1.call-start = ((), (), s32[]{:S(2)}) async-start(), calls=%async_computation.46 | async-start | bytes 2359296 | tf_op jit(solution)/shard_map/all_gather | solution.py:475
  294.5 106.2 %all-gather.55.cloned.1.call-start = ((), (), s32[]{:S(2)}) async-start(), calls=%async_computation.47 | async-start | bytes 1179648 | tf_op jit(solution)/shard_map/all_gather | solution.py:476
  295.0 204.3 %reduce-scatter.26.cloned.1.call-start = ((), (), s32[]{:S(2)}) async-start(), calls=%async_computation.28 | async-start | bytes 1179648 | tf_op jit(solution)/shard_map/reduce_scatter | solution.py:180
  463.1 75.2 %reduce-scatter.24.cloned.1.call-start = ((), (), s32[]{:S(2)}) async-start(), calls=%async_computation.27 | async-start | bytes 1179648 | tf_op jit(solution)/shard_map/reduce_scatter | solution.py:186
  463.7 175.2 %reduce-scatter.30.cloned.1.call-start = ((), (), s32[]{:S(2)}) async-start(), calls=%async_computation.30 | async-start | bytes 1179648 | tf_op jit(solution)/shard_map/reduce_scatter | solution.py:180
  466.8 72.6 %copy-start.116 = (bf16[1,2,256,256]{3,2,1,0:T(8,128)(2,1)S(1)}, bf16[1,2,256,256]{3,2,1,0:T(8,128)(2,1)}, u32[]{:S(2)}) copy-start(bf16[1,2,256,256]{3,2,1,0:T(8,128)(2,1)} %all-gather.11) | copy-start | bytes 786436
  602.8 75.2 %reduce-scatter.28.cloned.1.call-start = ((), (), s32[]{:S(2)}) async-start(), calls=%async_computation.29 | async-start | bytes 1179648 | tf_op jit(solution)/shard_map/reduce_scatter | solution.py:186
  603.4 118.5 %reduce-scatter.48.cloned.1.call-start = ((), (), s32[]{:S(2)}) async-start(), calls=%async_computation.39 | async-start | bytes 737280 | tf_op jit(solution)/shard_map/reduce_scatter | solution.py:525
  605.3 147.8 %reduce-scatter.56.cloned.1.call-start = ((), (), s32[]{:S(2)}) async-start(), calls=%async_computation.43 | async-start | bytes 737280 | tf_op jit(solution)/shard_map/reduce_scatter | solution.py:537
  607.0 185.3 %reduce-scatter.46.cloned.1.call-start = ((), (), s32[]{:S(2)}) async-start(), calls=%async_computation.38 | async-start | bytes 1179648 | tf_op jit(solution)/shard_map/reduce_scatter | solution.py:522
  608.8 224.5 %reduce-scatter.34.cloned.1.call-start = ((), (), s32[]{:S(2)}) async-start(), calls=%async_computation.32 | async-start | bytes 1474560 | tf_op jit(solution)/shard_map/reduce_scatter | solution.py:498
  611.1 262.8 %reduce-scatter.50.cloned.1.call-start = ((), (), s32[]{:S(2)}) async-start(), calls=%async_computation.40 | async-start | bytes 1474560 | tf_op jit(solution)/shard_map/reduce_scatter | solution.py:528
  615.1 296.5 %reduce-scatter.44.cloned.1.call-start = ((), (), s32[]{:S(2)}) async-start(), calls=%async_computation.37 | async-start | bytes 589824 | tf_op jit(solution)/shard_map/reduce_scatter | solution.py:519
  617.7 61.3 %copy-start.129 = (bf16[256,768]{1,0:T(8,128)(2,1)S(1)}, bf16[256,768]{1,0:T(8,128)(2,1)}, u32[]{:S(2)}) copy-start(bf16[256,768]{1,0:T(8,128)(2,1)} %copy-done.128) | copy-start | bytes 1179652
  681.3 270.5 %reduce-scatter.42.cloned.1.call-start = ((), (), s32[]{:S(2)}) async-start(), calls=%async_computation.36 | async-start | bytes 1179648 | tf_op jit(solution)/shard_map/reduce_scatter | solution.py:516
  685.3 311.2 %reduce-scatter.54.cloned.1.call-start = ((), (), s32[]{:S(2)}) async-start(), calls=%async_computation.42 | async-start | bytes 2359296 | tf_op jit(solution)/shard_map/reduce_scatter | solution.py:534
  688.9 354.6 %reduce-scatter.38.cloned.1.call-start = ((), (), s32[]{:S(2)}) async-start(), calls=%async_computation.34 | async-start | bytes 2949120 | tf_op jit(solution)/shard_map/reduce_scatter | solution.py:504
  692.6 394.6 %reduce-scatter.32.cloned.1.call-start = ((), (), s32[]{:S(2)}) async-start(), calls=%async_computation.31 | async-start | bytes 2211840 | tf_op jit(solution)/shard_map/reduce_scatter | solution.py:495
  696.7 434.4 %reduce-scatter.40.cloned.1.call-start = ((), (), s32[]{:S(2)}) async-start(), calls=%async_computation.35 | async-start | bytes 2211840 | tf_op jit(solution)/shard_map/reduce_scatter | solution.py:513
  702.2 483.6 %reduce-scatter.52.cloned.1.call-start = ((), (), s32[]{:S(2)}) async-start(), calls=%async_computation.41 | async-start | bytes 4718592 | tf_op jit(solution)/shard_map/reduce_scatter | solution.py:531
  708.4 537.7 %reduce-scatter.36.cloned.1.call-start = ((), (), s32[]{:S(2)}) async-start(), calls=%async_computation.33 | async-start | bytes 5898240 | tf_op jit(solution)/shard_map/reduce_scatter | solution.py:501
  715.7 567.1 %reduce-scatter.60.cloned.1.call-start = ((), (), s32[]{:S(2)}) async-start(), calls=%async_computation.49 | async-start | bytes 73728
  720.1 526.1 %copy-start.255 = (f32[256]{0:T(256)S(1)}, f32[256]{0:T(256)}, u32[]{:S(2)}) copy-start(f32[256]{0:T(256)} %copy-done.254) | copy-start | bytes 3076
  720.1 526.1 %copy-start.62 = (f32[256,640]{1,0:T(8,128)S(1)}, f32[256,640]{1,0:T(8,128)}, u32[]{:S(2)}) copy-start(f32[256,640]{1,0:T(8,128)} %copy-done.61) | copy-start | bytes 1966084
  720.1 526.1 %copy-start.150 = (f32[256,640]{1,0:T(8,128)S(1)}, f32[256,640]{1,0:T(8,128)}, u32[]{:S(2)}) copy-start(f32[256,640]{1,0:T(8,128)} %get-tuple-element.1102) | copy-start | bytes 1966084
  720.9 597.7 %reduce-scatter.58.cloned.1.call-start = ((), (), s32[]{:S(2)}) async-start(), calls=%async_computation.48 | async-start | bytes 184320
  721.9 723.7 %all-reduce.26.cloned.1.call-start = ((), (), s32[]{:S(2)}) async-start(), calls=%async_computation.50 | async-start | bytes 6160384 | tf_op jit(solution)/shard_map/psum | solution.py:541
  (310 other events, 1434.4 us)
Sparse Core Ops, SparseCore 0:
  9.9 31.1 all-gather.32
  74.3 23.7 all-gather.34
  100.6 25.1 all-gather.36
  127.5 24.6 all-gather.38
  154.5 27.8 all-gather.48
  184.2 41.1 all-gather.40
  227.8 23.4 all-gather.50
  253.2 30.0 all-gather.42
  293.1 24.8 all-gather.44
  320.3 23.7 all-gather.46
  346.6 28.1 all-gather.52
  377.1 23.5 all-gather.54
  463.3 36.0 reduce-scatter.25
  502.3 35.9 reduce-scatter.23
  602.9 35.9 reduce-scatter.29
  642.0 35.9 reduce-scatter.27
  681.0 34.5 reduce-scatter.47
  718.5 34.5 reduce-scatter.55
  756.3 36.0 reduce-scatter.45
  796.0 37.2 reduce-scatter.33
  836.6 37.2 reduce-scatter.49
  877.6 34.0 reduce-scatter.43
  915.7 36.0 reduce-scatter.41
  955.3 41.1 reduce-scatter.53
  999.8 43.6 reduce-scatter.37
  1046.8 40.3 reduce-scatter.31
  1090.8 40.2 reduce-scatter.39
  1134.5 51.2 reduce-scatter.51
  1189.6 56.5 reduce-scatter.35
  1249.6 33.1 reduce-scatter.59
  1286.7 31.8 reduce-scatter.57
  1322.1 123.4 all-reduce.25
where the time goes:
time: 1480 us; the launch traced here: 1470 us
  waiting for transfers between devices  908 us (61%)
  matrix products  196 us (13%)
  blocking collectives  186 us (13%)
  local copies, waits for them, and re-layouts  78.9 us (5%)
  other arithmetic  75.2 us (5%)
  between operations  18.5 us (1%)
    psum x1, waiting for transfers between devices, shards(): lax.psum(for_sending(owned), 'dp')  113 us
    unnamed x34, waiting for transfers between devices  75.7 us
    reduce_scatter x2, waiting for transfers between devices, attend_back(): lax.psum_scatter(value_parts.reshape(group_rows, head_extent).astype(jnp....  70 us
    reduce_scatter x1, waiting for transfers between devices, shards(): lax.psum_scatter(totals[2].astype(jnp.bfloat16), 'own', scatter_dimension...  60.3 us
    reduce_scatter x1, waiting for transfers between devices, shards(): lax.psum_scatter(totals[12].astype(jnp.bfloat16), 'own', scatter_dimensio...  54.7 us
    reduce_scatter x2, waiting for transfers between devices, attend_back(): lax.psum_scatter(key_parts.reshape(group_rows, head_extent).astype(jnp.bf...  52.8 us
    reduce_scatter x1, waiting for transfers between devices, shards(): lax.psum_scatter(totals[3].astype(jnp.bfloat16), 'own', scatter_dimension...  47 us
    reduce_scatter x1, waiting for transfers between devices, shards(): lax.psum_scatter(totals[13].astype(jnp.bfloat16), 'own', scatter_dimensio...  44.7 us
  transfers between devices with their start and end apart: 32, of which 23 were waited for; matrix products, arithmetic and copies ran while one was open for 13% of the time, Pallas kernels for 0%

commit v1 on v0

v1 whole, which is shorter than its diff:
```python
import math

import jax
import jax.numpy as jnp
from jax import lax
from jax.experimental import pallas as pl
from jax.experimental.pallas import tpu as pltpu
from jax.sharding import PartitionSpec as P

BF = jnp.bfloat16
F32 = jnp.float32
EPS = 1e-06
THETA = 1000000.0
LANES = 128
LOG2E = 1.4426950408889634
VMEM_LIMIT = 60 * 2**20
PEAK = 1e6
CORE, XBIT, YBIT = 1, 2, 4


def dot(a, b):
    return jnp.dot(a, b, preferred_element_type=F32)


def dot_nt(a, b):
    return lax.dot_general(a, b, (((1,), (1,)), ((), ())), preferred_element_type=F32)


def dot_tn(a, b):
    return lax.dot_general(a, b, (((0,), (0,)), ((), ())), preferred_element_type=F32)


def side_by_side(parts):
    return parts[0] if len(parts) == 1 else jnp.concatenate(parts, axis=1)


def stacked(parts):
    return parts[0] if len(parts) == 1 else jnp.concatenate(parts, axis=0)


class Name(str):
    def __call__(self, *more):
        return Name(self + str().join(str(m) for m in more))


class Names:
    def __getattr__(self, name):
        return Name(name)


N = Names()


class Sizes:
    pass


class Layout:
    def __init__(self, sizes, names, gains=False):
        self.at = {}
        total = 0
        for name in names:
            rows, blocks = sizes.shard[name]
            self.at[name] = (total, rows, blocks)
            total += rows * blocks
        self.gains = None
        if gains:
            self.gains = total
            total += 16
        self.total = total


class Chunk:
    def __init__(self, layout, pieces, ids):
        self.layout, self.pieces, self.ids, self.mine = layout, pieces, ids, pieces[0]


class Env:
    def __init__(self):
        self.refs = {}
        self.pending = {}

    def __getitem__(self, name):
        return self.refs[name]

    def w(self, name):
        if name in self.pending:
            sem = self.pending.pop(name)
            ref = self.refs[N.w(name)]
            pltpu.make_async_copy(ref, ref, sem).wait()
        return self.refs[N.w(name)]


def run_kernel(sizes, name, stages, ins, outs, scratch=(), weights=(), smem=(), micros=0):
    chunks = []
    for _, chunk in weights:
        if chunk not in chunks:
            chunks.append(chunk)
    smem = dict(smem)
    for number, chunk in enumerate(chunks):
        smem[N.ids(number)] = chunk.ids
    scratch = dict(scratch)
    names_in = list(ins)
    names_smem = list(smem)
    pieces = [piece for chunk in chunks for piece in chunk.pieces]
    names_out = list(outs)
    names_scratch = list(scratch)
    shapes = []
    for wname, chunk in weights:
        if wname == N.gains:
            shapes.append(((sizes.slots, 16, LANES), BF))
        else:
            _, rows, blocks = chunk.layout.at[wname]
            shapes.append(((blocks, rows * sizes.slots, LANES), BF))

    def kernel(*refs):
        env = Env()
        position = 0
        for key in names_smem + names_in:
            env.refs[key] = refs[position]
            position += 1
        piece_refs = refs[position : position + len(pieces)]
        position += len(pieces)
        for key in names_out + names_scratch:
            env.refs[key] = refs[position]
            position += 1
        of_chunk = {}
        start = 0
        for number, chunk in enumerate(chunks):
            of_chunk[number] = piece_refs[start : start + len(chunk.pieces)]
            start += len(chunk.pieces)
        for number, (wname, chunk) in enumerate(weights):
            buffer = refs[position]
            position += 1
            env.refs[N.w(wname)] = buffer
        for number, (wname, chunk) in enumerate(weights):
            sem = refs[position]
            position += 1
            buffer = env.refs[N.w(wname)]
            which = chunks.index(chunk)
            for slot in range(sizes.slots):
                piece = of_chunk[which][0 if len(chunk.pieces) == 1 else slot]
                offset = slot * chunk.layout.total if len(chunk.pieces) == 1 else 0
                if wname == N.gains:
                    source = piece.at[pl.ds(offset + chunk.layout.gains, 16), :]
                    target = buffer.at[slot]
                else:
                    first, rows, blocks = chunk.layout.at[wname]
                    first = offset + first
                    source = piece.at[pl.ds(first, blocks * rows), :].reshape(blocks, rows, LANES)
                    if sizes.slots == 1:
                        target = buffer
                    else:
                        row = pl.multiple_of(env[N.ids(which)][slot] * rows, 16)
                        target = buffer.at[:, pl.ds(row, rows), :]
                pltpu.make_async_copy(source, target, sem).start()
            env.pending[wname] = sem
        env.ids = lambda chunk: env[N.ids(chunks.index(chunk))]
        for stage in stages:
            stage(env)
        for wname, _ in weights:
            env.w(wname)

    any_space = pl.BlockSpec(memory_space=pl.ANY)
    vmem = pl.BlockSpec(memory_space=pltpu.VMEM)
    nbytes = sum(math.prod(a.shape) * a.dtype.itemsize for a in list(ins.values()) + pieces)
    nbytes += sum(math.prod(s) * jnp.dtype(d).itemsize for s, d in outs.values())
    results = pl.pallas_call(
        kernel,
        name=name,
        out_shape=[jax.ShapeDtypeStruct(*outs[key]) for key in names_out],
        in_specs=[pl.BlockSpec(memory_space=pltpu.SMEM)] * len(names_smem)
        + [vmem] * len(names_in)
        + [any_space] * len(pieces),
        out_specs=[vmem] * len(names_out),
        scratch_shapes=[pltpu.VMEM(*scratch[key]) for key in names_scratch]
        + [pltpu.VMEM(*shape) for shape in shapes]
        + [pltpu.SemaphoreType.DMA] * len(weights),
        compiler_params=pltpu.CompilerParams(vmem_limit_bytes=VMEM_LIMIT),
        cost_estimate=pl.CostEstimate(flops=int(micros * PEAK), bytes_accessed=0, transcendentals=0),
    )(*smem.values(), *ins.values(), *pieces)
    return dict(zip(names_out, results))


def columns(weight, first, count, rows=None):
    if rows is None:
        return side_by_side([weight[first + i] for i in range(count)])
    return side_by_side([weight[first + i, rows] for i in range(count)])


def root(values):
    return lax.rsqrt(jnp.mean(values * values, axis=-1, keepdims=True) + EPS)


def rms_back(values, gain, grad):
    r = root(values)
    scaled = grad * gain
    back = r * scaled - values * (r * r * r * jnp.mean(values * scaled, axis=-1, keepdims=True))
    return back, jnp.sum(values * r * grad, axis=0, keepdims=True)


def rotate(values, cos, sin):
    half = values.shape[-1] // 2
    p, q = values[:, :half], values[:, half:]
    return jnp.concatenate([p * cos - q * sin, q * cos + p * sin], axis=1)


def rotate_back(grad, cos, sin):
    half = grad.shape[-1] // 2
    a, b = grad[:, :half], grad[:, half:]
    return jnp.concatenate([a * cos + b * sin, b * cos - a * sin], axis=1)


GELU_A = math.sqrt(2.0 / math.pi)
GELU_B = 0.044715


def gelu_parts(v):
    t = jnp.tanh(GELU_A * (v + GELU_B * v * v * v))
    return 0.5 * v * (1.0 + t), t


def gelu_slope(v, t):
    return 0.5 * (1.0 + t) + 0.5 * v * (1.0 - t * t) * (GELU_A * (1.0 + 3.0 * GELU_B * v * v))


def stage_gains(sizes, chunk):
    def stage(env):
        blocks = env.w(N.gains)
        ids = env.ids(chunk)
        norm = jnp.zeros((16, sizes.D), F32)
        heads = jnp.zeros((16, sizes.HD), F32)
        width, head_width = sizes.D // sizes.slots, sizes.HD // sizes.slots

        def pick(total, each, index):
            a = lax.broadcasted_iota(jnp.int32, (LANES, total), 0)
            b = lax.broadcasted_iota(jnp.int32, (LANES, total), 1)
            return jnp.where((b == a + index * each) & (a < each), 1.0, 0.0).astype(BF)

        for m in range(sizes.slots):
            norm = norm + dot(blocks[m], pick(sizes.D, width, ids[m]))
            heads = heads + dot(blocks[m], pick(sizes.HD, head_width, ids[m]))
        env[N.norm][...] = norm
        env[N.qkg][...] = heads

    return stage


def stage_qkv(sizes, l, stream):
    def stage(env):
        x = env[stream][...]
        attn_in = (x * root(x) * env[N.norm][0:1, :]).astype(BF)
        env[N.attn_in(l)][...] = attn_in
        first = env.w(N.aqkv)
        mids = []
        for j in range(3):
            mid = dot(attn_in, columns(first, sizes.RB * j, sizes.RB)).astype(BF)
            env[N.mid(l)][j] = mid
            mids.append(mid)
        qkv, hb = env.w(N.qkv), sizes.HB
        cos, sin = env[N.cos][...], env[N.sin][...]
        gq, gk = env[N.qkg][4:5, :], env[N.qkg][5:6, :]
        bk, bv, bq = env.w(N.bk), env.w(N.bv), env.w(N.bq)
        raw = dot(attn_in, columns(qkv, hb * sizes.H, hb)) + dot(mids[1], columns(bk, 0, hb))
        env[N.raw(l)][sizes.H] = raw
        env[N.kv(l)][:, : sizes.HD] = rotate(raw * root(raw) * gk, cos, sin).astype(BF)
        raw = dot(attn_in, columns(qkv, hb * (sizes.H + 1), hb)) + dot(mids[2], columns(bv, 0, hb))
        env[N.kv(l)][:, sizes.HD :] = raw.astype(BF)
        for h in range(sizes.H):
            raw = dot(attn_in, columns(qkv, hb * h, hb)) + dot(mids[0], columns(bq, hb * h, hb))
            env[N.raw(l)][h] = raw
            env[N.q(l)][h] = rotate(raw * root(raw) * gq, cos, sin).astype(BF)

    return stage


def key_block(sizes, pieces, b, value):
    lanes = slice(sizes.HD, 2 * sizes.HD) if value else slice(0, sizes.HD)
    rows = pl.ds(pl.multiple_of(b * sizes.IB, 16), sizes.IB)
    parts = []
    for piece in pieces:
        if len(piece.shape) == 3:
            parts += [piece[g, rows, lanes] for g in range(piece.shape[0])]
        else:
            parts.append(piece[rows, lanes])
    return stacked(parts)


def query_limits(sizes, env, qb):
    rows = slice(qb * sizes.QB, (qb + 1) * sizes.QB)
    slot = jnp.concatenate([env[N.qslot][rows, :]] * sizes.H, axis=0)
    low = jnp.concatenate([env[N.qstart][rows, :]] * sizes.H, axis=0)
    last = (qb + 1) * sizes.QB // sizes.IB
    return rows, slot, low, last


def stage_attend(sizes, l):
    scale = sizes.HD ** (-0.5) * LOG2E
    M = sizes.H * sizes.QB

    def stage(env):
        pieces = [env[N.kvp(l, i)] for i in range(sizes.kv_pieces)]
        for qb in range(sizes.T // sizes.QB):
            rows, slot, low, last = query_limits(sizes, env, qb)
            query = env[N.q(l)][:, rows, :].reshape(M, sizes.HD)
            env[N.o_acc][...] = jnp.zeros((M, sizes.HD), F32)
            env[N.l_acc][...] = jnp.zeros((M, LANES), F32)

            def body(b, carry):
                keys = env[N.kslot][b]
                scores = dot_nt(query, key_block(sizes, pieces, b, False))
                allowed = (keys <= slot) & (keys >= low)
                probs = jnp.where(allowed, jnp.exp2(scores * scale), 0.0)
                part = probs[:, :LANES]
                for i in range(1, probs.shape[1] // LANES):
                    part = part + probs[:, i * LANES : (i + 1) * LANES]
                env[N.l_acc][...] += part
                env[N.o_acc][...] += dot(probs.astype(BF), key_block(sizes, pieces, b, True))
                return carry

            lax.fori_loop(env[N.first_block][qb], last, body, 0)
            total = jnp.sum(env[N.l_acc][...], axis=1, keepdims=True)
            env[N.att(l)][:, rows, :] = (env[N.o_acc][...] / total).reshape(sizes.H, sizes.QB, sizes.HD)
            env[N.lse(l)][:, rows, :] = jnp.broadcast_to(jnp.log2(total), (M, LANES)).reshape(
                sizes.H, sizes.QB, LANES
            )

    return stage


def stage_out(sizes, l, stream):
    def stage(env):
        outa, outw, outb = env.w(N.outa), env.w(N.outw), env.w(N.outb)
        mid = jnp.zeros((sizes.T, sizes.R), F32)
        branch = jnp.zeros((sizes.T, sizes.D), F32)
        for h in range(sizes.H):
            heads = env[N.att(l)][h].astype(BF)
            env[N.ho(l)][h] = heads
            rows = slice(h * sizes.HD, (h + 1) * sizes.HD)
            mid = mid + dot(heads, columns(outa, 0, sizes.RB, rows))
            branch = branch + dot(heads, columns(outw, 0, sizes.DB, rows))
        mid = mid.astype(BF)
        env[N.omid(l)][...] = mid
        branch = branch + dot(mid, columns(outb, 0, sizes.DB))
        env[N.branch(l)][...] = branch
        middle = env[stream][...] + branch * root(branch) * env[N.norm][1:2, :]
        env[N.middle(l)][...] = middle
        env[N.ffn_in(l)][...] = (middle * root(middle) * env[N.norm][2:3, :]).astype(BF)

    return stage


def stage_ffn(sizes, l):
    def stage(env):
        x = env[N.ffn_in(l)][...]
        agu = env.w(N.agu)
        mids = []
        for j in range(2):
            mid = dot(x, columns(agu, sizes.RB * j, sizes.RB)).astype(BF)
            env[N.gmid(l)][j] = mid
            mids.append(mid)
        bg, bu, gu = env.w(N.bg), env.w(N.bu), env.w(N.gu)
        dnw, dna = env.w(N.dnw), env.w(N.dna)
        blocks = sizes.F // 256
        out = jnp.zeros((sizes.T, sizes.D), F32)
        down = jnp.zeros((sizes.T, sizes.R), F32)
        for b in range(blocks):
            gate = dot(x, columns(gu, 2 * b, 2)) + dot(mids[0], columns(bg, 2 * b, 2))
            up = dot(x, columns(gu, 2 * (blocks + b), 2)) + dot(mids[1], columns(bu, 2 * b, 2))
            env[N.gu(l)][b, :, :256] = gate
            env[N.gu(l)][b, :, 256:] = up
            hidden = (gelu_parts(gate)[0] * up).astype(BF)
            env[N.hidden(l)][b] = hidden
            rows = slice(b * 256, (b + 1) * 256)
            out = out + dot(hidden, columns(dnw, 0, sizes.DB, rows))
            down = down + dot(hidden, columns(dna, 0, sizes.RB, rows))
        down = down.astype(BF)
        env[N.dmid(l)][...] = down
        out = out + dot(down, columns(env.w(N.dnb), 0, sizes.DB))
        env[N.ffn_out(l)][...] = out
        env[N.stream(l + 1)][...] = env[N.middle(l)][...] + out * root(out) * env[N.norm][3:4, :]

    return stage


def stage_ffn_back(sizes, l, grad):
    def stage(env):
        out_grad = env[grad][...]
        back, gain = rms_back(env[N.ffn_out(l)][...], env[N.norm][3:4, :], out_grad)
        env[N.dnorm(l, 3)][...] = gain
        low = back.astype(BF)
        env[N.ffn_low(l)][...] = low
        dmg = dot_nt(low, columns(env.w(N.dnb), 0, sizes.DB)).astype(BF)
        env[N.dmg(l)][...] = dmg
        dnw, dna, bg, bu, gu = env.w(N.dnw), env.w(N.dna), env.w(N.bg), env.w(N.bu), env.w(N.gu)
        blocks = sizes.F // 256
        gate_mid = jnp.zeros((sizes.T, sizes.R), F32)
        up_mid = jnp.zeros((sizes.T, sizes.R), F32)
        total = jnp.zeros((sizes.T, sizes.D), F32)
        for b in range(blocks):
            rows = slice(b * 256, (b + 1) * 256)
            hidden_grad = dot_nt(low, columns(dnw, 0, sizes.DB, rows)) + dot_nt(
                dmg, columns(dna, 0, sizes.RB, rows)
            )
            gate, up = env[N.gu(l)][b, :, :256], env[N.gu(l)][b, :, 256:]
            value, t = gelu_parts(gate)
            gate_grad = (hidden_grad * up * gelu_slope(gate, t)).astype(BF)
            up_grad = (hidden_grad * value).astype(BF)
            env[N.gug(l)][b] = gate_grad
            env[N.gug(l)][blocks + b] = up_grad
            gate_mid = gate_mid + dot_nt(gate_grad, columns(bg, 2 * b, 2))
            up_mid = up_mid + dot_nt(up_grad, columns(bu, 2 * b, 2))
            total = total + dot_nt(gate_grad, columns(gu, 2 * b, 2))
            total = total + dot_nt(up_grad, columns(gu, 2 * (blocks + b), 2))
        agu = env.w(N.agu)
        for j, mid in enumerate((gate_mid, up_mid)):
            mid = mid.astype(BF)
            env[N.gmg(l)][j] = mid
            total = total + dot_nt(mid, columns(agu, sizes.RB * j, sizes.RB))
        back, gain = rms_back(env[N.middle(l)][...], env[N.norm][2:3, :], total)
        env[N.dnorm(l, 2)][...] = gain
        env[N.mgrad(l)][...] = out_grad + back

    return stage


def stage_out_back(sizes, l):
    def stage(env):
        back, gain = rms_back(env[N.branch(l)][...], env[N.norm][1:2, :], env[N.mgrad(l)][...])
        env[N.dnorm(l, 1)][...] = gain
        low = back.astype(BF)
        env[N.blow(l)][...] = low
        omg = dot_nt(low, columns(env.w(N.outb), 0, sizes.DB)).astype(BF)
        env[N.omg(l)][...] = omg
        outw, outa = env.w(N.outw), env.w(N.outa)
        for h in range(sizes.H):
            rows = slice(h * sizes.HD, (h + 1) * sizes.HD)
            grad = dot_nt(low, columns(outw, 0, sizes.DB, rows)) + dot_nt(omg, columns(outa, 0, sizes.RB, rows))
            env[N.hgrad(l)][h] = grad.astype(BF)

    return stage


def stage_attend_back(sizes, l):
    factor = sizes.HD ** (-0.5)
    scale = factor * LOG2E
    M = sizes.H * sizes.QB
    HD = sizes.HD

    def stage(env):
        pieces = [env[N.kvp(l, i)] for i in range(sizes.kv_pieces)]
        total_blocks = sizes.T // sizes.IB
        for b in range(total_blocks):
            env[N.dkv_acc][b] = jnp.zeros((sizes.n * sizes.IB, 2 * HD), F32)
        for qb in range(sizes.T // sizes.QB):
            rows, slot, low, last = query_limits(sizes, env, qb)
            query = env[N.q(l)][:, rows, :].reshape(M, HD)
            grad = env[N.hgrad(l)][:, rows, :].reshape(M, HD)
            attended = env[N.att(l)][:, rows, :].reshape(M, HD)
            row_dot = jnp.sum(grad.astype(F32) * attended, axis=1, keepdims=True)
            lse = env[N.lse(l)][:, rows, :].reshape(M, LANES)[:, 0:1]
            env[N.o_acc][...] = jnp.zeros((M, HD), F32)

            def body(b, carry):
                keys = env[N.kslot][b]
                k = key_block(sizes, pieces, b, False)
                v = key_block(sizes, pieces, b, True)
                allowed = (keys <= slot) & (keys >= low)
                probs = jnp.where(allowed, jnp.exp2(dot_nt(query, k) * scale - lse), 0.0)
                scores_grad = (probs * (dot_nt(grad, v) - row_dot)).astype(BF)
                env[N.o_acc][...] += dot(scores_grad, k)
                env[N.dkv_acc][b, :, :HD] += dot_tn(scores_grad, query)
                env[N.dkv_acc][b, :, HD:] += dot_tn(probs.astype(BF), grad)
                return carry

            lax.fori_loop(env[N.first_block][qb], last, body, 0)
            env[N.dq(l)][:, rows, :] = (env[N.o_acc][...] * factor).reshape(sizes.H, sizes.QB, HD)
        IB = sizes.IB
        for m in range(sizes.n):
            if sizes.slots > 1:
                where = (N.dkvkeep if m < sizes.n // 2 else N.dkvsend, m % (sizes.n // 2))
            else:
                where = (N.dkvkeep, m)
            for b in range(total_blocks):
                for j, by in enumerate((factor, 1.0)):
                    lanes = slice(j * HD, (j + 1) * HD)
                    part = env[N.dkv_acc][b, m * IB : (m + 1) * IB, lanes]
                    env[where[0](l)][where[1], b * IB : (b + 1) * IB, lanes] = (part * by).astype(BF)

    return stage


def stage_q_back(sizes, l):
    def stage(env):
        cos, sin = env[N.cos][...], env[N.sin][...]
        gq = env[N.qkg][4:5, :]
        hb = sizes.HB
        qkv, bq, aqkv = env.w(N.qkv), env.w(N.bq), env.w(N.aqkv)
        gains = jnp.zeros((1, sizes.HD), F32)
        mid = jnp.zeros((sizes.T, sizes.R), F32)
        total = jnp.zeros((sizes.T, sizes.D), F32)
        for h in range(sizes.H):
            turned = rotate_back(env[N.dq(l)][h], cos, sin)
            back, gain = rms_back(env[N.raw(l)][h], gq, turned)
            gains = gains + gain
            low = back.astype(BF)
            env[N.rawq_low(l)][h] = low
            mid = mid + dot_nt(low, columns(bq, hb * h, hb))
            total = total + dot_nt(low, columns(qkv, hb * h, hb))
        mid = mid.astype(BF)
        env[N.midgq(l)][...] = mid
        total = total + dot_nt(mid, columns(aqkv, 0, sizes.RB))
        env[N.agrad(l)][...] = total
        env[N.dqg(l)][...] = gains

    return stage


def stage_kv_back(sizes, l, stream, result):
    def stage(env):
        cos, sin = env[N.cos][...], env[N.sin][...]
        hb = sizes.HB
        qkv, aqkv = env.w(N.qkv), env.w(N.aqkv)
        turned = rotate_back(env[N.dkv][:, : sizes.HD].astype(F32), cos, sin)
        back, gain = rms_back(env[N.raw(l)][sizes.H], env[N.qkg][5:6, :], turned)
        env[N.dkg(l)][...] = gain
        total = env[N.agrad(l)][...]
        for j, (low, second) in enumerate(((back.astype(BF), N.bk), (env[N.dkv][:, sizes.HD :], N.bv))):
            env[N.rawkv_low(l)][j] = low
            mid = dot_nt(low, columns(env.w(second), 0, hb)).astype(BF)
            env[N.midgkv(l)][j] = mid
            total = total + dot_nt(low, columns(qkv, hb * (sizes.H + j), hb))
            total = total + dot_nt(mid, columns(aqkv, sizes.RB * (j + 1), sizes.RB))
        back, gain = rms_back(env[stream][...], env[N.norm][0:1, :], total)
        env[N.dnorm(l, 0)][...] = gain
        env[result][...] = env[N.mgrad(l)][...] + back

    return stage


def put(sizes, env, layout, prefix, name, block, value, first_row=0):
    first, rows, _ = layout.at[name]
    count = value.shape[1] // LANES
    keep = env[N.keep(prefix)]
    if sizes.slots == 1:
        value = value.astype(BF)
        for i in range(count):
            at = first + (block + i) * rows + first_row
            keep[0, at : at + value.shape[0], :] = value[:, i * LANES : (i + 1) * LANES]
        return
    send = env[N.send(prefix)]
    core, chip = env[N.place][0], env[N.place][1]
    even_stays = core == 0
    for pair in range(value.shape[0] // (2 * rows)):
        a = value[2 * pair * rows : (2 * pair + 1) * rows]
        b = value[(2 * pair + 1) * rows : (2 * pair + 2) * rows]
        stays = jnp.where(even_stays, a, b).astype(BF)
        goes = jnp.where(even_stays, b, a).astype(BF)
        slot = jnp.bitwise_xor(first_row // (2 * rows) + pair, chip)
        for i in range(count):
            at = first + (block + i) * rows
            keep[slot, at : at + rows, :] = stays[:, i * LANES : (i + 1) * LANES]
            send[slot, at : at + rows, :] = goes[:, i * LANES : (i + 1) * LANES]


def grad_product(sizes, env, layout, prefix, name, lefts, rights, first_block=0, first_row=0):
    left = stacked([a.T if len(lefts) == 1 else a.T for a in lefts]) if len(lefts) == 1 else side_by_side(
        [a.T for a in lefts]
    )
    for block, right in rights:
        value = dot(left, stacked(right))
        put(sizes, env, layout, prefix, name, first_block + block, value, first_row)


def wide(ref, width, step=256):
    out = []
    at = 0
    while at < width:
        size = min(step, width - at)
        out.append((at // LANES, slice(at, at + size)))
        at += size
    return out


def grads_ffn_wide(sizes, env, layout, prefix, names, loops, pl_l):
    blocks = sizes.F // 256
    for j, name in enumerate((N.gug, N.guu)):
        if name in names:
            left = [env[N.ffn_in(l)][...] for l in loops]
            rights = [(2 * b, [env[N.gug(l)][j * blocks + b] for l in loops]) for b in range(blocks)]
            grad_product(sizes, env, layout, prefix, name, left, rights)
    if N.agu in names:
        rights = [(sizes.RB * j, [env[N.gmg(pl_l)][j]]) for j in range(2)]
        grad_product(sizes, env, layout, prefix, N.agu, [env[N.ffn_in(pl_l)][...]], rights)
    for j, name in enumerate((N.bg, N.bu)):
        if name in names:
            rights = [(2 * b, [env[N.gug(pl_l)][j * blocks + b]]) for b in range(blocks)]
            grad_product(sizes, env, layout, prefix, name, [env[N.gmid(pl_l)][j]], rights)


def grads_ffn_down(sizes, env, layout, prefix, names, loops, pl_l):
    blocks = sizes.F // 256
    step = 512
    for b in range(0, blocks, 2):
        row = b * 256
        if N.dnw in names:
            left = [side_by_side([env[N.hidden(l)][b], env[N.hidden(l)][b + 1]]) for l in loops]
            rights = [(i, [env[N.ffn_low(l)][:, s] for l in loops]) for i, s in wide(None, sizes.D, 640)]
            grad_product(sizes, env, layout, prefix, N.dnw, left, rights, 0, row)
        if N.dna in names:
            left = [side_by_side([env[N.hidden(pl_l)][b], env[N.hidden(pl_l)][b + 1]])]
            grad_product(sizes, env, layout, prefix, N.dna, left, [(0, [env[N.dmg(pl_l)][...]])], 0, row)
    if N.dnb in names:
        grad_product(
            sizes, env, layout, prefix, N.dnb, [env[N.dmid(pl_l)][...]], [(0, [env[N.ffn_low(pl_l)][...]])]
        )


def grads_out(sizes, env, layout, prefix, names, loops, pl_l):
    for h in range(0, sizes.H, 2):
        row = h * sizes.HD
        if N.outw in names:
            left = [side_by_side([env[N.ho(l)][h], env[N.ho(l)][h + 1]]) for l in loops]
            grad_product(
                sizes, env, layout, prefix, N.outw, left, [(0, [env[N.blow(l)][...] for l in loops])], 0, row
            )
        if N.outa in names:
            left = [side_by_side([env[N.ho(pl_l)][h], env[N.ho(pl_l)][h + 1]])]
            grad_product(sizes, env, layout, prefix, N.outa, left, [(0, [env[N.omg(pl_l)][...]])], 0, row)
    if N.outb in names:
        grad_product(
            sizes, env, layout, prefix, N.outb, [env[N.omid(pl_l)][...]], [(0, [env[N.blow(pl_l)][...]])]
        )


def grads_qkv(sizes, env, layout, prefix, names, loops, pl_l):
    hb = sizes.HB
    left = [env[N.attn_in(l)][...] for l in loops] if {N.qkvq, N.qkvkv} & set(names) else None
    if N.qkvq in names:
        rights = [(hb * h, [env[N.rawq_low(l)][h] for l in loops]) for h in range(sizes.H)]
        grad_product(sizes, env, layout, prefix, N.qkvq, left, rights)
    if N.qkvkv in names:
        rights = [(hb * j, [env[N.rawkv_low(l)][j] for l in loops]) for j in range(2)]
        grad_product(sizes, env, layout, prefix, N.qkvkv, left, rights)
    first = ([(0, N.midgq(pl_l), None)] if {N.aqkv, N.aqkvq} & set(names) else []) + (
        [(sizes.RB * j, N.midgkv(pl_l), j) for j in range(2)] if {N.aqkv, N.aqkvkv} & set(names) else []
    )
    for name in (N.aqkv, N.aqkvq, N.aqkvkv):
        if name in names:
            rights = [
                (at + (sizes.RB if name == N.aqkv and j is not None else 0), [env[ref][...] if j is None else env[ref][j]])
                for at, ref, j in first
            ]
            grad_product(sizes, env, layout, prefix, name, [env[N.attn_in(pl_l)][...]], rights)
    if N.bq in names:
        rights = [(hb * h, [env[N.rawq_low(pl_l)][h]]) for h in range(sizes.H)]
        grad_product(sizes, env, layout, prefix, N.bq, [env[N.mid(pl_l)][0]], rights)
    for j, name in enumerate((N.bk, N.bv)):
        if name in names:
            grad_product(
                sizes, env, layout, prefix, name, [env[N.mid(pl_l)][j + 1]], [(0, [env[N.rawkv_low(pl_l)][j]])]
            )


def stage_grads(sizes, parts):
    def stage(env):
        for prefix, layout, names, loops, pl_l in parts:
            for build in (grads_ffn_wide, grads_ffn_down, grads_out, grads_qkv):
                build(sizes, env, layout, prefix, names, loops, pl_l)

    return stage


def stage_gain_grads(sizes, prefix, layout):
    def stage(env):
        norm = stacked(
            [env[N.dnorm(0, i)][...] + env[N.dnorm(1, i)][...] for i in range(4)] + [jnp.zeros((12, sizes.D), F32)]
        )
        heads = stacked(
            [jnp.zeros((4, sizes.HD), F32)]
            + [env[kind(0)][...] + env[kind(1)][...] for kind in (N.dqg, N.dkg)]
            + [jnp.zeros((10, sizes.HD), F32)]
        )
        if sizes.slots == 1:
            env[N.gain_norm][...] = norm
            env[N.gain_heads][...] = heads
            return
        norm, heads = norm.astype(BF), heads.astype(BF)
        width, head_width = sizes.D // sizes.slots, sizes.HD // sizes.slots

        def pick(total, each, index):
            a = lax.broadcasted_iota(jnp.int32, (total, LANES), 0)
            b = lax.broadcasted_iota(jnp.int32, (total, LANES), 1)
            return jnp.where((a == b + index * each) & (b < each), 1.0, 0.0).astype(BF)

        at = layout.gains
        chip, core = env[N.place][1], env[N.place][0]
        for k in range(sizes.slots // 2):
            for name, flip in ((N.keep, core), (N.send, 1 - core)):
                index = 2 * jnp.bitwise_xor(k, chip) + flip
                block = dot(norm, pick(sizes.D, width, index)) + dot(heads, pick(sizes.HD, head_width, index))
                env[name(prefix)][k, at : at + 16, :] = block.astype(BF)

    return stage


def pack(sizes, layout, arrays, gains=None):
    names = list(layout.at)
    unique = []
    for name in names:
        if not any(arrays[name][0] is u for u in unique):
            unique.append(arrays[name][0])
    extra = [] if layout.gains is None else [gains]

    def kernel(*refs):
        out = refs[-1]
        for name in names:
            array, lead = arrays[name]
            source = refs[[array is u for u in unique].index(True)]
            first, rows, blocks = layout.at[name]
            for b in range(blocks):
                out[first + b * rows : first + (b + 1) * rows, :] = source[
                    lead + (slice(None), slice(b * LANES, (b + 1) * LANES))
                ]
        if layout.gains is not None:
            out[layout.gains : layout.gains + 16, :] = refs[len(unique)][...]

    return pl.pallas_call(
        kernel,
        name=N.pack,
        out_shape=jax.ShapeDtypeStruct((layout.total, LANES), BF),
        compiler_params=pltpu.CompilerParams(vmem_limit_bytes=VMEM_LIMIT),
        cost_estimate=pl.CostEstimate(flops=0, bytes_accessed=4 * layout.total * LANES, transcendentals=0),
    )(*unique, *extra)


def sort_rows(sizes, rank, *arrays):
    def kernel(rank_ref, *refs):
        count = len(refs) // 2
        place = lax.broadcasted_iota(jnp.int32, (sizes.T, sizes.T), 0)
        matrix = jnp.where(place == rank_ref[...], 1.0, 0.0).astype(BF)
        for source, target in zip(refs[:count], refs[count:]):
            target[...] = dot(matrix, source[...])

    return pl.pallas_call(
        kernel,
        name=N.sort_rows,
        out_shape=[jax.ShapeDtypeStruct(a.shape, F32) for a in arrays],
        compiler_params=pltpu.CompilerParams(vmem_limit_bytes=VMEM_LIMIT),
        cost_estimate=pl.CostEstimate(flops=0, bytes_accessed=2**21, transcendentals=0),
    )(rank, *arrays)


def unsort_rows(sizes, rank, value):
    def kernel(rank_ref, source, target):
        place = lax.broadcasted_iota(jnp.int32, (sizes.T, sizes.T), 0)
        matrix = jnp.where(place == rank_ref[...], 1.0, 0.0).astype(BF)
        target[...] = dot_tn(matrix, source[...].astype(BF)).astype(BF)

    return pl.pallas_call(
        kernel,
        name=N.unsort_rows,
        out_shape=jax.ShapeDtypeStruct(value.shape, BF),
        compiler_params=pltpu.CompilerParams(vmem_limit_bytes=VMEM_LIMIT),
        cost_estimate=pl.CostEstimate(flops=0, bytes_accessed=2**20, transcendentals=0),
    )(rank, value)


def unpack(sizes, targets, sources):
    names = list(sources)
    shapes = [jax.ShapeDtypeStruct(shape, F32) for shape, _ in targets]

    def kernel(*refs):
        ins = {name: refs[2 * i : 2 * i + 2] for i, name in enumerate(names)}
        outs = refs[2 * len(names) :]

        def rows_of(prefix, first, count):
            low, high = ins[prefix]
            half = low.shape[0]
            if first + count <= half:
                return low[first : first + count, :].astype(F32)
            if first >= half:
                return high[first - half : first + count - half, :].astype(F32)
            return jnp.concatenate(
                [low[first:half, :].astype(F32), high[: first + count - half, :].astype(F32)], axis=0
            )

        for out, (_, parts) in zip(outs, targets):
            for lead, prefix, name, column in parts:
                layout = sources[prefix][2]
                if name == N.norm:
                    out[...] = rows_of(prefix, layout.gains, 16)
                    continue
                first, rows, blocks = layout.at[name]
                for b in range(blocks):
                    out[lead + (slice(None), slice((column + b) * LANES, (column + b + 1) * LANES))] = rows_of(
                        prefix, first + b * rows, rows
                    )

    return pl.pallas_call(
        kernel,
        name=N.unpack,
        out_shape=shapes,
        compiler_params=pltpu.CompilerParams(vmem_limit_bytes=VMEM_LIMIT),
        cost_estimate=pl.CostEstimate(flops=0, bytes_accessed=2**22, transcendentals=0),
    )(*[half for name in names for half in sources[name][:2]])


def swap(sizes, value, bit):
    return lax.ppermute(value, "own", [(i, i ^ bit) for i in range(sizes.n)])


def along(value, pairs):
    return lax.ppermute(value, "dp", pairs)


def after_all(values, others):
    others = [o for o in others if not any(o is value for value in values)]
    count = len(values)

    def kernel(*refs):
        pass

    space = pl.BlockSpec(memory_space=pl.ANY)
    return pl.pallas_call(
        kernel,
        name=N.after,
        out_shape=[jax.ShapeDtypeStruct(value.shape, value.dtype) for value in values],
        in_specs=[space] * (count + len(others)),
        out_specs=[space] * count,
        input_output_aliases={i: i for i in range(count)},
        cost_estimate=pl.CostEstimate(flops=0, bytes_accessed=0, transcendentals=0),
    )(*values, *others)


def after(value, *others):
    return after_all([value], others)[0]


def gather_plain(sizes, mine, x_first, others=()):
    px, py = swap(sizes, mine, XBIT), swap(sizes, mine, YBIT)
    px = after(px, *others) if others else px
    pd = swap(sizes, px, YBIT) if x_first else swap(sizes, py, XBIT)
    here = [mine, px, py, pd]
    return here + [swap(sizes, piece, CORE) for piece in here]


def gather_direct(sizes, mine):
    here = [mine] + [swap(sizes, mine, bit) for bit in (XBIT, YBIT, XBIT | YBIT)]
    return here + [swap(sizes, piece, CORE) for piece in here]


PIECES = (0, XBIT, YBIT, XBIT | YBIT, CORE, CORE | XBIT, CORE | YBIT, CORE | XBIT | YBIT)


def gather_paired(sizes, mine, odd, others=()):
    px = swap(sizes, mine, XBIT)
    chosen = jnp.where(odd, px, mine)
    py = swap(sizes, after(chosen, *others) if others else chosen, YBIT)
    pz = along(py, [(0, 1), (1, 0), (2, 3), (3, 2)])
    here = [mine, px, py, pz]
    return here + [swap(sizes, piece, CORE) for piece in here]


def add(first, *others):
    total = first.astype(F32)
    for other in others:
        total = total + other.astype(F32)
    return total.astype(BF)


class Sum:
    def __init__(self, sizes, keep, send, mode, odd=None):
        self.sizes, self.keep, self.mode, self.odd = sizes, keep, mode, odd
        self.payload, self.done = [send], []
        self.steps = [self.core] + ([self.direct] if mode == N.direct else [self.near, self.far])
        self.steps += [self.trade, self.level, self.back]

    def step(self):
        now = self.steps.pop(0)
        now(self.payload)

    def swap(self, value, bit):
        return swap(self.sizes, value, bit)

    def core(self, sent):
        here, come = self.keep, self.swap(sent[0], CORE)
        if self.mode == N.direct:
            self.keep, *self.payload = [add(here[k], come[k]) for k in range(4)]
            return
        if self.mode == N.x:
            here, come = [a.reshape((2, 2) + a.shape[1:]) for a in (here, come)]
            pairs = [(here[:, i], come[:, i]) for i in range(2)]
        else:
            pairs = [(here[i : i + 2], come[i : i + 2]) for i in (0, 2)]
        self.keep, self.payload = add(*pairs[0]), [add(*pairs[1])]

    def direct(self, sent):
        come = [self.swap(value, bit) for value, bit in zip(sent, (XBIT, YBIT, XBIT | YBIT))]
        self.level_in(add(self.keep, *come))

    def near(self, sent):
        come = self.swap(sent[0], XBIT if self.mode == N.x else YBIT)
        self.keep, self.payload = add(self.keep[0], come[0]), [add(self.keep[1], come[1])]

    def far(self, sent):
        self.level_in(add(self.keep, self.swap(sent[0], YBIT if self.mode == N.x else XBIT)))

    def level_in(self, total):
        self.plane_total = total
        if self.odd is None:
            self.payload = [total]
            return
        rows = total.shape[0] // 2
        low, high = total[:rows], total[rows:]
        self.keep, self.payload = jnp.where(self.odd, high, low), [jnp.where(self.odd, low, high)]

    def trade(self, sent):
        self.payload = [add(self.keep, along(sent[0], [(0, 1), (1, 0), (2, 3), (3, 2)]))]

    def level(self, sent):
        self.payload = [add(sent[0], along(sent[0], [(0, 2), (2, 0), (1, 3), (3, 1)]))]

    def back(self, sent):
        come = along(sent[0], [(0, 1), (1, 0), (2, 3), (3, 2)])
        self.halves = (jnp.where(self.odd, come, sent[0]), jnp.where(self.odd, sent[0], come))
        self.payload = list(self.halves)


def make_shards(mesh):
    n, planes = mesh.shape["own"], mesh.shape["dp"]
    fast = n == 8 and planes == 4

    def shards(
        tokens,
        cotangent,
        lengths,
        row_packed_slot,
        shared_attention_matrix,
        shared_output_matrix,
        shared_gate_up_matrix,
        shared_down_matrix,
        norm_gain_table,
        query_key_gains,
        adapter_attention_first,
        adapter_query_second,
        adapter_key_value_second,
        adapter_output_first,
        adapter_output_second,
        adapter_gate_first,
        adapter_gate_second,
        adapter_down_first,
        adapter_down_second,
    ):
        s = Sizes()
        s.n, s.slots = n, (8 if fast else 1)
        s.T, s.D = tokens.shape
        s.HD = adapter_key_value_second.shape[3]
        s.H = adapter_query_second.shape[2] // s.HD
        s.R = adapter_query_second.shape[1] * n
        s.F = shared_down_matrix.shape[0] * n
        s.DB, s.RB, s.HB = s.D // LANES, s.R // LANES, s.HD // LANES
        s.IB = max(16, 256 // n)
        s.QB = s.T // 4
        s.kv_pieces = 8 if fast else 1
        QW, k = s.H * s.HD, s.slots
        s.shard = {
            N.qkv: (s.D // k, (QW + 2 * s.HD) // LANES),
            N.aqkv: (s.D // k, 3 * s.RB),
            N.gug: (s.D // k, s.F // LANES),
            N.guu: (s.D // k, s.F // LANES),
            N.qkvq: (s.D // k, QW // LANES),
            N.qkvkv: (s.D // k, 2 * s.HB),
            N.aqkvq: (s.D // k, s.RB),
            N.aqkvkv: (s.D // k, 2 * s.RB),
            N.bq: (s.R // k, QW // LANES),
            N.bk: (s.R // k, s.HB),
            N.bv: (s.R // k, s.HB),
            N.outw: (QW // k, s.DB),
            N.outa: (QW // k, s.RB),
            N.outb: (s.R // k, s.DB),
            N.gu: (s.D // k, 2 * s.F // LANES),
            N.agu: (s.D // k, 2 * s.RB),
            N.bg: (s.R // k, s.F // LANES),
            N.bu: (s.R // k, s.F // LANES),
            N.dnw: (s.F // k, s.DB),
            N.dna: (s.F // k, s.RB),
            N.dnb: (s.R // k, s.DB),
        }
        own, plane = lax.axis_index("own"), lax.axis_index("dp")

        plain_ids = jnp.stack([own ^ m for m in PIECES]).astype(jnp.int32) if fast else jnp.zeros((1,), jnp.int32)
        slots = row_packed_slot[0]
        seq = lengths[0]
        my_slots = lax.dynamic_slice_in_dim(slots, own * s.T, s.T)
        rank = (my_slots // n).reshape(1, s.T)
        rest = slots.reshape(n, s.T)[:, 0] % n
        my_rest = my_slots[0] % n
        counts = jnp.arange(seq.shape[0])
        ends = jnp.sum(jnp.where(counts[None, :] <= counts[:, None], seq[None, :], 0), axis=1)
        sorted_slots = n * jnp.arange(s.T, dtype=jnp.int32) + my_rest
        past = sorted_slots[:, None] >= ends[None, :]
        starts = jnp.sum(jnp.where(past, seq[None, :], 0), axis=1)
        position = sorted_slots - starts
        inverse = THETA ** (-jnp.arange(s.HD // 2, dtype=F32) * 2.0 / s.HD)
        angles = position.astype(F32)[:, None] * inverse[None, :]
        block_slots = s.IB * n
        first_block = starts.reshape(4, s.QB)[:, 0] // block_slots
        key_rest = rest
        if fast:
            key_rest = jnp.sum(
                jnp.where(plain_ids[:, None] == jnp.arange(n)[None, :], rest[None, :], 0), axis=1
            )
        along_rows = jnp.arange(s.T, dtype=jnp.int32).reshape(s.T // s.IB, 1, 1, s.IB) * n
        kslot = (along_rows + key_rest.reshape(1, 1, n, 1)).reshape(s.T // s.IB, 1, n * s.IB).astype(jnp.int32)
        stream0, cot = sort_rows(s, rank, tokens, cotangent)

        v = {
            N.cos: jnp.cos(angles),
            N.sin: jnp.sin(angles),
            N.qslot: sorted_slots.reshape(s.T, 1),
            N.qstart: starts.reshape(s.T, 1).astype(jnp.int32),
            N.kslot: kslot,
            N.stream0: stream0,
            N.cot: cot,
        }
        def full(array, axis):
            return array if fast else lax.all_gather(array, "own", axis=axis, tiled=True)

        w_att, w_out = full(shared_attention_matrix, 0), full(shared_output_matrix, 0)
        w_gu, w_dn = full(shared_gate_up_matrix, 0), full(shared_down_matrix, 0)
        a_att, b_q = full(adapter_attention_first, 1), full(adapter_query_second, 1)
        b_kv, a_out = full(adapter_key_value_second, 2), full(adapter_output_first, 1)
        b_out, a_gu = full(adapter_output_second, 1), full(adapter_gate_first, 1)
        b_gu, a_dn = full(adapter_gate_second, 2), full(adapter_down_first, 1)
        b_dn = full(adapter_down_second, 1)

        def arrays_of(l):
            return {
                N.qkv: (w_att, ()),
                N.aqkv: (a_att, (l,)),
                N.bq: (b_q, (l,)),
                N.bk: (b_kv, (l, 0)),
                N.bv: (b_kv, (l, 1)),
                N.outw: (w_out, ()),
                N.outa: (a_out, (l,)),
                N.outb: (b_out, (l,)),
                N.gu: (w_gu, ()),
                N.agu: (a_gu, (l,)),
                N.bg: (b_gu, (l, 0)),
                N.bu: (b_gu, (l, 1)),
                N.dnw: (w_dn, ()),
                N.dna: (a_dn, (l,)),
                N.dnb: (b_dn, (l,)),
            }

        q_names, o_names = (N.qkv, N.aqkv, N.bq, N.bk, N.bv), (N.outw, N.outa, N.outb)
        g_names, d_names = (N.gu, N.agu, N.bg, N.bu), (N.dnw, N.dna, N.dnb)
        lq_names, lr_names = (N.aqkv, N.bq, N.bk, N.bv), (N.outa, N.outb, N.agu, N.bg, N.bu, N.dna, N.dnb)
        odd = (plane & 1) == 1
        inner = (plane == 1) | (plane == 2)
        paired_ids = plain_ids
        if fast:
            over_y = jnp.where(odd, XBIT | YBIT, YBIT)
            over_z = jnp.where(odd, YBIT, XBIT | YBIT)
            order = [0, XBIT, over_y, over_z]
            paired_ids = jnp.stack([own ^ m for m in order] + [own ^ m ^ CORE for m in order]).astype(jnp.int32)
        gain_block = None
        if fast:
            gain_block = jnp.concatenate(
                [
                    jnp.pad(norm_gain_table, ((0, 0), (0, LANES - norm_gain_table.shape[1]))),
                    jnp.pad(query_key_gains, ((0, 0), (0, LANES - query_key_gains.shape[1]))),
                    jnp.zeros((10, LANES), BF),
                ],
                axis=0,
            )

        def packed(names, l, gains=False, of=()):
            layout = Layout(s, names, gains)
            arrays = {m: arrays_of(k)[m] for m, k in of} if of else arrays_of(l)
            return layout, pack(s, layout, arrays, gain_block)

        def fetch(made, scheme, start=None, turn=()):
            layout, mine = made
            if not fast:
                return Chunk(layout, [mine], plain_ids)
            if scheme == N.y:
                over = [after(mine, start.pieces[1]), after(mine, start.pieces[3])]
                px, py = swap(s, over[0], XBIT), swap(s, over[1], YBIT)
                here = [mine, px, py, swap(s, py, XBIT)]
                chunk = Chunk(layout, here + [swap(s, piece, CORE) for piece in here], plain_ids)
                chunk.gates = over
                return chunk
            if start is not None:
                mine = after(mine, *start)
            if scheme == N.whole:
                whole = Chunk(layout, [lax.all_gather(mine, "own", axis=0, tiled=True)], jnp.arange(n, dtype=jnp.int32))
                whole.mine = mine
                return whole
            if scheme == N.direct:
                return Chunk(layout, gather_direct(s, mine), plain_ids)
            if scheme == N.paired:
                return Chunk(layout, gather_paired(s, mine, odd, turn), paired_ids)
            return Chunk(layout, gather_plain(s, mine, scheme == N.x, turn), plain_ids)

        pack_g, pack_q = packed(g_names + d_names, 0), packed(q_names, 0, gains=fast)
        pack_lr = packed(lr_names, 1)
        first = [(m, 0) for m in o_names] + [(m, 1) for m in lq_names]
        pack_o = packed(o_names + lq_names, None, of=first)
        chunk_g = fetch(pack_g, N.whole)
        chunk_q = fetch(pack_q, N.x, None, (stream0, v[N.cos], pack_g[1], pack_o[1], pack_lr[1]))
        chunk_o = fetch(pack_o, N.y, chunk_q)
        chunk_lq = chunk_o
        if fast:
            v[N.stream0] = after(v[N.stream0], *chunk_o.gates)
        loop0 = {**{m: chunk_q for m in q_names}, **{m: chunk_o for m in o_names}}
        loop0 |= {m: chunk_g for m in g_names + d_names}
        of_loop = [loop0]

        def wts(names, l):
            return [(m, of_loop[l][m]) for m in names]

        T, D, HD, H, R, F = s.T, s.D, s.HD, s.H, s.R, s.F
        blocks = F // 256
        half = n // 2 if fast else n
        shapes = {
            N.norm: ((16, D), F32),
            N.qkg: ((16, HD), F32),
            N.stream1: ((T, D), F32),
            N.stream2: ((T, D), F32),
            N.o_acc: ((H * s.QB, HD), F32),
            N.l_acc: ((H * s.QB, LANES), F32),
            N.dkv_acc: ((T // s.IB, n * s.IB, 2 * HD), F32),
            N.sgrad1: ((T, D), F32),
            N.sgrad0: ((T, D), F32),
            N.gain_norm: ((16, D), F32),
            N.gain_heads: ((16, HD), F32),
        }
        for l in (0, 1):
            shapes |= {
                N.attn_in(l): ((T, D), BF),
                N.mid(l): ((3, T, R), BF),
                N.raw(l): ((H + 1, T, HD), F32),
                N.q(l): ((H, T, HD), BF),
                N.kv(l): ((T, 2 * HD), BF),
                N.att(l): ((H, T, HD), F32),
                N.lse(l): ((H, T, LANES), F32),
                N.ho(l): ((H, T, HD), BF),
                N.omid(l): ((T, R), BF),
                N.branch(l): ((T, D), F32),
                N.middle(l): ((T, D), F32),
                N.ffn_in(l): ((T, D), BF),
                N.gmid(l): ((2, T, R), BF),
                N.gu(l): ((blocks, T, 512), F32),
                N.hidden(l): ((blocks, T, 256), BF),
                N.dmid(l): ((T, R), BF),
                N.ffn_out(l): ((T, D), F32),
                N.ffn_low(l): ((T, D), BF),
                N.dmg(l): ((T, R), BF),
                N.gug(l): ((2 * blocks, T, 256), BF),
                N.gmg(l): ((2, T, R), BF),
                N.mgrad(l): ((T, D), F32),
                N.blow(l): ((T, D), BF),
                N.omg(l): ((T, R), BF),
                N.hgrad(l): ((H, T, HD), BF),
                N.dq(l): ((H, T, HD), F32),
                N.dkvkeep(l): ((half, T, 2 * HD), BF),
                N.dkvsend(l): ((half, T, 2 * HD), BF),
                N.rawq_low(l): ((H, T, HD), BF),
                N.rawkv_low(l): ((2, T, HD), BF),
                N.midgq(l): ((T, R), BF),
                N.midgkv(l): ((2, T, R), BF),
                N.agrad(l): ((T, D), F32),
                N.dqg(l): ((1, HD), F32),
                N.dkg(l): ((1, HD), F32),
            }
            for i in range(4):
                shapes[N.dnorm(l, i)] = ((1, D), F32)

        def call(name, stages, ins, outs, scratch=(), weights=(), smem=(), micros=0):
            made = run_kernel(
                s,
                name,
                stages,
                {m: v[m] for m in ins},
                {m: shapes[m] for m in outs},
                {m: shapes[m] for m in scratch},
                weights,
                {m: v[m] for m in smem},
                micros,
            )
            v.update(made)

        v[N.first_block] = first_block.astype(jnp.int32)
        v[N.place] = jnp.stack([own & 1, own >> 1]).astype(jnp.int32)

        def share_kv(l):
            if fast:
                pieces = gather_direct(s, v[N.kv(l)])
            else:
                gathered = lax.all_gather(v[N.kv(l)], "own", axis=0, tiled=False)
                pieces = [gathered]
            for i, piece in enumerate(pieces):
                v[N.kvp(l, i)] = piece

        def kv_names(l):
            return [N.kvp(l, i) for i in range(s.kv_pieces)]

        qkv_outs = [N.attn_in, N.mid, N.raw, N.q, N.kv]

        def fill(names, l):
            return [m(l) for m in names]

        if fast:
            call(
                N.qkv0,
                [stage_gains(s, chunk_q), stage_qkv(s, 0, N.stream0)],
                [N.stream0, N.cos, N.sin],
                [N.norm, N.qkg] + fill(qkv_outs, 0),
                weights=[(N.gains, chunk_q)] + wts(q_names, 0),
                micros=6.5,
            )
        else:
            norm = lax.all_gather(norm_gain_table, "own", axis=1, tiled=True).astype(F32)
            heads = lax.all_gather(query_key_gains, "own", axis=1, tiled=True).astype(F32)
            v[N.norm] = jnp.pad(norm, ((0, 12), (0, 0)))
            v[N.qkg] = jnp.pad(heads, ((4, 10), (0, 0)))
            call(
                N.qkv0,
                [stage_qkv(s, 0, N.stream0)],
                [N.stream0, N.cos, N.sin, N.norm, N.qkg],
                fill(qkv_outs, 0),
                weights=wts(q_names, 0),
                micros=6.5,
            )
        share_kv(0)
        if fast:
            mine = after(pack_lr[1], v[N.kvp(0, 3)])
            here = [mine] + [swap(s, mine, bit) for bit in (XBIT, YBIT, XBIT | YBIT)]
        of_loop.append({**loop0, **{m: chunk_lq for m in lq_names}})
        att_ins = [N.qslot, N.qstart, N.kslot]
        out_outs = [N.att, N.lse, N.ho, N.omid, N.branch, N.middle, N.ffn_in]
        ffn_outs = [N.gmid, N.gu, N.hidden, N.dmid, N.ffn_out]
        call(
            N.attend0,
            [stage_attend(s, 0), stage_out(s, 0, N.stream0)],
            [N.stream0, N.q0, N.norm] + att_ins + kv_names(0),
            fill(out_outs, 0),
            scratch=[N.o_acc, N.l_acc],
            weights=wts(o_names, 0),
            smem=[N.first_block],
            micros=11,
        )
        call(
            N.ffn0,
            [stage_ffn(s, 0), stage_qkv(s, 1, N.stream1)],
            [N.ffn_in0, N.middle0, N.norm, N.qkg, N.cos, N.sin],
            fill(ffn_outs, 0) + [N.stream1] + fill(qkv_outs, 1),
            weights=wts(g_names + d_names, 0) + wts(q_names, 1),
            micros=16,
        )
        chunk_lr = Chunk(*pack_lr[:1], [pack_lr[1]], plain_ids)
        if fast:
            *here, v[N.kv1] = after_all(here + [v[N.kv1]], [])
            chunk_lr.pieces = here + [swap(s, piece, CORE) for piece in here]
        of_loop[1] |= {m: chunk_lr for m in lr_names}
        share_kv(1)
        loop1 = [
            stage_attend(s, 1),
            stage_out(s, 1, N.stream1),
            stage_ffn(s, 1),
            stage_ffn_back(s, 1, N.cot),
            stage_out_back(s, 1),
        ]
        loop1_outs = (
            [N.stream2, N.mgrad1]
            + fill([N.ho, N.omid, N.ffn_in, N.gmid, N.hidden, N.dmid], 1)
            + fill([N.ffn_low, N.dmg, N.gug, N.gmg, N.blow, N.omg], 1)
            + [N.dnorm(1, 1), N.dnorm(1, 2), N.dnorm(1, 3)]
        )
        loop1_scratch = [N.o_acc, N.l_acc, N.branch1, N.middle1, N.gu1, N.ffn_out1]
        back_outs = [N.dq, N.dkvkeep] + ([N.dkvsend] if fast else [])
        kept = [N.att1, N.lse1, N.hgrad1]
        call(
            N.loop1,
            loop1 + ([stage_attend_back(s, 1)] if fast else []),
            [N.stream1, N.q1, N.norm, N.cot] + att_ins + kv_names(1),
            loop1_outs + (fill(back_outs, 1) if fast else kept),
            scratch=loop1_scratch + ([N.dkv_acc] + kept if fast else []),
            weights=wts(o_names + g_names + d_names, 1),
            smem=[N.first_block],
            micros=35,
        )
        if not fast:
            call(
                N.attend_back1,
                [stage_attend_back(s, 1)],
                [N.q1] + kept + att_ins + kv_names(1),
                fill(back_outs, 1),
                scratch=[N.o_acc, N.dkv_acc],
                smem=[N.first_block],
                micros=10,
            )

        plans = {
            N.la: [((N.bg, N.bu, N.agu, N.dna, N.dnb, N.outa, N.outb), 1)],
            N.g1: [((N.gug,), 0), ((N.aqkv,), 1)],
            N.g2: [((N.guu,), 0), ((N.bq, N.bk, N.bv), 1)],
            N.g3: [((N.dnw, N.agu), 0)],
            N.g4: [((N.bg, N.bu, N.dna, N.dnb), 0)],
            N.rb: [((N.outw, N.outa, N.outb, N.bq, N.qkvq, N.aqkvq), 0)],
            N.ra: [((N.qkvkv, N.aqkvkv, N.bk, N.bv), 0)],
        }
        modes = {N.la: N.direct, N.g1: N.x, N.g2: N.y, N.g3: N.x, N.g4: N.y, N.rb: N.direct, N.ra: N.direct}
        layouts = {}
        where = {}
        for m, parts in plans.items():
            layouts[m] = Layout(s, [name for names, _ in parts for name in names], gains=(m == N.ra and fast))
            shapes[N.keep(m)] = ((half if fast else 1, layouts[m].total, LANES), BF)
            shapes[N.send(m)] = shapes[N.keep(m)]
            where |= {(name, l): m for names, l in parts for name in names}

        def grads(names, ins, micros, extra=(), extra_outs=()):
            parts = []
            for m in names:
                parts += [(m, layouts[m], group, [0, 1], l) for group, l in plans[m]]
            outs = [end(m) for m in names for end in ((N.keep, N.send) if fast else (N.keep,))]
            call(
                N.grads(names[0]),
                [stage_grads(s, parts)] + list(extra),
                ins,
                outs + list(extra_outs),
                smem=[N.place] if fast else [],
                micros=micros,
            )

        sums = {}

        def open_sum(*names):
            for m in names:
                if fast:
                    sums[m] = Sum(s, v[N.keep(m)], v[N.send(m)], modes[m], odd)

        def open_kv(l):
            if fast:
                sums[N.dkv(l)] = Sum(s, v[N.dkvkeep(l)], v[N.dkvsend(l)], N.direct)
            else:
                keep = v[N.dkvkeep(l)].reshape(n * T, 2 * HD)
                v[N.dkv] = lax.psum_scatter(keep, "own", scatter_dimension=0, tiled=True)

        def close_kv(l):
            if fast:
                v[N.dkv] = sums[N.dkv(l)].payload[0]

        def phase(starts, inputs=(), need=()):
            if not fast:
                return
            starts, inputs = [sums[m] for m in starts], list(inputs)
            others = []
            for m in need:
                others += sums[m].payload if m in sums else [v[m]]
            values = after_all([p for r in starts for p in r.payload] + [v[m] for m in inputs], others)
            for r in starts:
                count = len(r.payload)
                r.payload, values = values[:count], values[count:]
            for m, value in zip(inputs, values):
                v[m] = value
            for r in starts:
                r.step()

        gain_ins = [N.dnorm(l, i) for l in (0, 1) for i in range(4)] + [N.dqg0, N.dqg1, N.dkg0, N.dkg1]
        qkv_l = [N.attn_in, N.mid, N.rawq_low, N.rawkv_low, N.midgq, N.midgkv]

        open_kv(1)
        phase([N.dkv1], [N.dq1])
        call(
            N.q_back1,
            [stage_q_back(s, 1)],
            [N.cos, N.sin, N.qkg, N.dq1, N.raw1],
            [N.rawq_low1, N.midgq1, N.agrad1, N.dqg1],
            weights=wts((N.qkv, N.bq, N.aqkv), 1),
            micros=5.8,
        )
        phase([N.dkv1], [N.gmg1], [N.agrad1])
        grads(
            [N.la],
            [N.ffn_in1, N.gmid1, N.gug1, N.gmg1, N.hidden1, N.dmid1, N.ffn_low1, N.dmg1, N.ho1, N.omid1, N.blow1, N.omg1],
            8.6,
        )
        open_sum(N.la)
        phase([N.la], [N.agrad1], [N.dkv1])
        close_kv(1)
        call(
            N.kv_back1,
            [stage_kv_back(s, 1, N.stream1, N.sgrad1)],
            [N.cos, N.sin, N.qkg, N.norm, N.dkv, N.raw1, N.agrad1, N.stream1, N.mgrad1],
            [N.dkg1, N.rawkv_low1, N.midgkv1, N.dnorm(1, 0), N.sgrad1],
            weights=wts((N.qkv, N.aqkv, N.bk, N.bv), 1),
            micros=6.2,
        )
        phase([N.la], [N.sgrad1])
        call(
            N.ffn_back0,
            [stage_ffn_back(s, 0, N.sgrad1)],
            [N.norm, N.sgrad1, N.ffn_out0, N.gu0, N.middle0],
            [N.dnorm(0, 3), N.dnorm(0, 2)] + fill([N.ffn_low, N.dmg, N.gug, N.gmg, N.mgrad], 0),
            weights=wts(d_names + (N.bg, N.bu, N.gu, N.agu), 0),
            micros=14,
        )
        grads([N.g1, N.g2], fill([N.ffn_in, N.gug], 0) + [N.ffn_in1, N.gug1] + fill(qkv_l, 1), 9.7)
        open_sum(N.g1, N.g2)
        phase([N.g1, N.g2, N.la], [N.dmg0, N.mgrad0])
        grads(
            [N.g3, N.g4],
            fill([N.ffn_in, N.gmid, N.gug, N.gmg, N.hidden, N.dmid, N.ffn_low, N.dmg], 0) + [N.hidden1, N.ffn_low1],
            8.5,
        )
        call(
            N.out_back0,
            [stage_out_back(s, 0)],
            [N.branch0, N.norm, N.mgrad0],
            [N.dnorm(0, 1), N.blow0, N.omg0, N.hgrad0],
            weights=wts(o_names, 0),
            micros=4.5,
        )
        open_sum(N.g3, N.g4)
        phase([N.g1, N.g2, N.g3, N.g4, N.la], [N.hgrad0])
        call(
            N.attend_back0,
            [stage_attend_back(s, 0)],
            [N.hgrad0, N.q0, N.att0, N.lse0] + att_ins + kv_names(0),
            fill(back_outs, 0),
            scratch=[N.o_acc, N.dkv_acc],
            smem=[N.first_block],
            micros=13,
        )
        open_kv(0)
        phase([N.dkv0, N.g1, N.g2, N.la], [N.dq0])
        call(
            N.q_back0,
            [stage_q_back(s, 0)],
            [N.cos, N.sin, N.qkg, N.dq0, N.raw0],
            [N.rawq_low0, N.midgq0, N.agrad0, N.dqg0],
            weights=wts((N.qkv, N.bq, N.aqkv), 0),
            micros=5.8,
        )
        phase([N.dkv0, N.g1, N.g2], [N.rawq_low0])
        grads(
            [N.rb],
            fill([N.ho, N.omid, N.blow, N.omg, N.mid, N.rawq_low, N.attn_in, N.midgq], 0)
            + [N.ho1, N.blow1, N.attn_in1, N.rawq_low1],
            7,
        )
        open_sum(N.rb)
        phase([N.rb, N.g3, N.g4, N.g1, N.g2], [N.agrad0], [N.dkv0])
        close_kv(0)
        call(
            N.kv_back0,
            [stage_kv_back(s, 0, N.stream0, N.sgrad0)],
            [N.cos, N.sin, N.qkg, N.norm, N.dkv, N.raw0, N.agrad0, N.stream0, N.mgrad0],
            [N.dkg0, N.rawkv_low0, N.midgkv0, N.dnorm(0, 0), N.sgrad0],
            weights=wts((N.qkv, N.aqkv, N.bk, N.bv), 0),
            micros=6.2,
        )
        grads(
            [N.ra],
            fill([N.attn_in, N.mid, N.rawkv_low, N.midgkv], 0) + [N.attn_in1, N.rawkv_low1] + gain_ins,
            3,
            [stage_gain_grads(s, N.ra, layouts[N.ra])],
            [] if fast else [N.gain_norm, N.gain_heads],
        )
        open_sum(N.ra)
        phase([N.g3, N.g4, N.rb], [N.stream2, N.sgrad0], [N.g1, N.g2])
        mixed = unsort_rows(s, rank, v[N.stream2])
        tokens_grad = unsort_rows(s, rank, v[N.sgrad0])
        v[N.mixed], v[N.tokens_grad] = mixed, tokens_grad
        phase([N.ra, N.g3, N.g4, N.rb, N.g1], [], [N.mixed, N.tokens_grad])
        phase([N.ra, N.g3, N.g4])
        phase([N.ra, N.rb, N.g3, N.g4, N.g2])
        phase([N.ra, N.rb])
        phase([N.ra])
        for m in sums:
            assert m in (N.dkv0, N.dkv1) or not sums[m].steps
        finished = {m: sums[m].payload for m in plans if fast}

        HB, RB = s.HB, s.RB
        two = (0, 1)
        targets = [
            (shared_attention_matrix.shape, [((), N.qkvq, 0, 0), ((), N.qkvkv, 0, H * HB)]),
            (shared_output_matrix.shape, [((), N.outw, 0, 0)]),
            (shared_gate_up_matrix.shape, [((), N.gug, 0, 0), ((), N.guu, 0, F // LANES)]),
            (shared_down_matrix.shape, [((), N.dnw, 0, 0)]),
            (
                adapter_attention_first.shape,
                [((0,), N.aqkvq, 0, 0), ((0,), N.aqkvkv, 0, RB), ((1,), N.aqkv, 1, 0)],
            ),
            (adapter_query_second.shape, [((l,), N.bq, l, 0) for l in two]),
            (
                adapter_key_value_second.shape,
                [((l, j), m, l, 0) for l in two for j, m in enumerate((N.bk, N.bv))],
            ),
            (adapter_output_first.shape, [((l,), N.outa, l, 0) for l in two]),
            (adapter_output_second.shape, [((l,), N.outb, l, 0) for l in two]),
            (adapter_gate_first.shape, [((l,), N.agu, l, 0) for l in two]),
            (adapter_gate_second.shape, [((l, j), m, l, 0) for l in two for j, m in enumerate((N.bg, N.bu))]),
            (adapter_down_first.shape, [((l,), N.dna, l, 0) for l in two]),
            (adapter_down_second.shape, [((l,), N.dnb, l, 0) for l in two]),
        ]
        if fast:
            plan = [(shape, [(lead, where[m, l], m, col) for lead, m, l, col in parts]) for shape, parts in targets]
            made = [None] * len(plan)
            early = [i for i, (_, parts) in enumerate(plan) if all(part[1][0] in N.lg for part in parts)]
            late = [i for i in range(len(plan)) if i not in early]
            for which, ends in ((early, []), (late, [((16, LANES), [((), N.ra, N.norm, 0)])])):
                chosen = [plan[i] for i in which] + ends
                used = sorted({part[1] for _, parts in chosen for part in parts})
                results = unpack(s, chosen, {m: (*finished[m], layouts[m]) for m in used})
                for i, value in zip(which, results):
                    made[i] = value
            grads, gains = made, results[-1]
            norm_grad = gains[:4, : norm_gain_table.shape[1]]
            heads_grad = gains[4:6, : query_key_gains.shape[1]]
        else:

            def natural(name, l):
                layout = layouts[where[name, l]]
                first, rows, count = layout.at[name]
                block = v[N.keep(where[name, l])][0, first : first + rows * count]
                return block.reshape(count, rows, LANES).transpose(1, 0, 2).reshape(rows, count * LANES)

            def reduced(value, axis):
                part = lax.psum_scatter(value.astype(BF), "own", scatter_dimension=axis, tiled=True)
                return lax.psum(part, "dp").astype(F32)

            grads = []
            for shape, parts in targets:
                of_lead = {}
                for lead, m, l, _ in parts:
                    of_lead.setdefault(lead, []).append(natural(m, l))
                value = jnp.stack([side_by_side(columns_of) for columns_of in of_lead.values()])
                value = value.reshape(shape[:-2] + value.shape[1:])
                grads.append(reduced(value, len(shape) - 2))
            norm_grad = reduced(v[N.gain_norm][:4], 1)
            heads_grad = reduced(v[N.gain_heads][4:6], 1)
        return (mixed, tokens_grad) + tuple(grads[:4]) + (norm_grad, heads_grad) + tuple(grads[4:])

    return shards


def solution(mesh):
    both, rows = P(("dp", "own"), None), P("own", None)
    second, third = P(None, "own", None), P(None, None, "own", None)
    wide_gain = P(None, "own")
    in_specs = (
        (both, both, P("dp", None), P("dp", None), rows, rows, rows, rows, wide_gain, wide_gain)
        + (second, second, third, second, second, second, third, second, second)
    )
    out_specs = (
        (both, both, rows, rows, rows, rows, wide_gain, wide_gain)
        + (second, second, third, second, second, second, third, second, second)
    )
    return jax.shard_map(make_shards(mesh), mesh=mesh, in_specs=in_specs, out_specs=out_specs, check_vma=False)
```

time: 1480 us -> 538 us (0.36)
  waiting for transfers between devices: 908 us -> 172 us
  matrix products: 196 us -> 0 us
  blocking collectives: 186 us -> 0 us
  Pallas kernels: 0 us -> 177 us
  starting transfers between devices: 1.77 us -> 77.8 us
  local copies, waits for them, and re-layouts: 78.9 us -> 15.4 us
    reduce_scatter x17 -> x0, waiting for transfers between devices: 647 us -> none  [the longest x2 70 us: attend_back(): lax.psum_scatter(value_parts.reshape(group_rows, head_extent).astype(jnp....]
    dot_general x146 -> x0, matrix products: 196 us -> none  [the longest x30 37.6 us: matrix_product(): return jnp.dot(left, right, preferred_element_type=jnp.float32)]
    pallas_call x0 -> x46, Pallas kernels: none -> 177 us  [the longest x16 154 us: run_kernel(): pl.pallas_call(kernel, name=name, out_shape=[jax.ShapeDtypeStruct(*outs[k...]
    all_gather x16 -> x0, blocking collectives: 174 us -> none  [the longest x2 33.3 us: fetch(): lax.all_gather(adapter_output_first[repeat_along], 'own', axis=0, tiled=T...]
    ppermute x0 -> x88, waiting for transfers between devices: none -> 172 us  [the longest x67 124 us: swap(): return lax.ppermute(value, 'own', [(i, i ^ bit) for i in range(sizes.n)])]
    psum x1 -> x0, waiting for transfers between devices: 113 us -> none  [shards(): lax.psum(for_sending(owned), 'dp')]
    ppermute x0 -> x88, starting transfers between devices: none -> 77.8 us  [the longest x67 52.2 us: swap(): return lax.ppermute(value, 'own', [(i, i ^ bit) for i in range(sizes.n)])]
    unnamed x34 -> x1, waiting for transfers between devices: 75.7 us -> 0.02 us
  transfers between devices with their start and end apart: 32 -> 89, of which waited for: 23 -> 27; matrix products, arithmetic and copies ran while one was open for 13% -> 11% of each run, Pallas kernels for 0% -> 26%
where the time goes in v1:
time: 538 us; the launch traced here: 531 us
  Pallas kernels  177 us (33%)
  waiting for transfers between devices  172 us (32%)
  starting transfers between devices  77.8 us (14%)
  other arithmetic  72.1 us (13%)
  between operations  16.9 us (3%)
  local copies, waits for them, and re-layouts  15.4 us (3%)
    pallas_call x16, Pallas kernels, run_kernel(): pl.pallas_call(kernel, name=name, out_shape=[jax.ShapeDtypeStruct(*outs[k...  154 us
    ppermute x67, waiting for transfers between devices, swap(): return lax.ppermute(value, 'own', [(i, i ^ bit) for i in range(sizes.n)])  124 us
    convert_element_type x36, other arithmetic, add(): return total.astype(BF)  53.6 us
    ppermute x67, starting transfers between devices, swap(): return lax.ppermute(value, 'own', [(i, i ^ bit) for i in range(sizes.n)])  52.2 us
    ppermute x21, waiting for transfers between devices, along(): return lax.ppermute(value, 'dp', pairs)  47.2 us
    ppermute x21, starting transfers between devices, along(): return lax.ppermute(value, 'dp', pairs)  25.6 us
  transfers between devices with their start and end apart: 89, of which 27 were waited for; matrix products, arithmetic and copies ran while one was open for 11% of the time, Pallas kernels for 26%

profile of v1, /device:TPU:0, one launch (start us, length us, event | category | flops | bytes accessed | tf_op | source)
XLA Modules:
  0.0 530.9 jit_solution(2505190265099844549)
XLA Ops:
  7.3 2.9 pack.6.refs_3_
  13.0 2.9 collective-permute-start
  37.3 17.2 %collective-permute-done.1.refs_1_.refs_7_.refs_13_.refs_10_.refs_14_.refs_9_ = bf16[1840,128]{1,0:T(8,128)(2,1)S(1)} collective-permute-done((bf16[1840,128]{1,0:T(8,128)(2,1)}, bf16[1840,128]{1,0:T(8,128)(2,1)S(1)}, u32[]{:S(2)}, u32[]{:S(2)}) %collective-permute-start.1) | collective-permute-done | bytes 471072 | tf_op jit(solution)/shard_map/ppermute | solution.py:810
  58.2 7.6 %qkv0.1 = (f32[16,640]{1,0:T(8,128)}, f32[16,256]{1,0:T(8,128)}, bf16[256,640]{1,0:T(8,128)(2,1)}, bf16[3,256,256]{2,1,0:T(8,128)(2,1)}, f32[5,256,256]{2,1,0:T(...) custom-call(s32[8]{0:T(128)} %stack.47.refs_0_.refs_1_.refs_2_, ...), custom_call_target="tpu_custom_call" | custom-call | flops 6500000 | tf_op jit(solution)/shard_map/qkv0/pallas_call | solution.py:168
  65.9 11.2 %collective-permute-done.15.refs_18_.refs_20_.refs_21_.refs_17_.refs_6_ = bf16[1920,128]{1,0:T(8,128)(2,1)S(1)} collective-permute-done((bf16[1920,128]{1,0:T(8,128)(2,1)}, bf16[1920,128]{1,0:T(8,128)(2,1)S(1)}, u32[]{:S(2)}, u32[]{:S(2)}) %collective-permute-start.15) | collective-permute-done | bytes 491552 | tf_op jit(solution)/shard_map/ppermute | solution.py:810
  77.1 3.9 collective-permute-start.9
  81.4 32.4 %collective-permute-done.9.refs_11_.refs_1_ = bf16[256,512]{1,0:T(8,128)(2,1)S(1)} collective-permute-done((bf16[256,512]{1,0:T(8,128)(2,1)}, bf16[256,512]{1,0:T(8,128)(2,1)S(1)}, u32[]{:S(2)}, u32[]{:S(2)}) %collective-permute-start.9) | collective-permute-done | bytes 262176 | tf_op jit(solution)/shard_map/ppermute | solution.py:810
  116.3 2.9 collective-permute-start.23
  123.7 9.7 %attend0.1 = (f32[4,256,256]{2,1,0:T(8,128)}, f32[4,256,128]{2,1,0:T(8,128)}, bf16[4,256,256]{2,1,0:T(8,128)(2,1)}, bf16[256,256]{1,0:T(8,128)(2,1)}, f32[256,64...) custom-call(s32[4]{0:T(128)} %and_select_fusion.2.refs_0_, s32[8]{0:T(128)} %stack.47.refs_0_.refs_1_.refs_2_, ...), custom_call_target="tpu_custom_call" | custom-call | flops 11000000 | tf_op jit(solution)/shard_map/attend0/pallas_call | solution.py:168
  133.9 16.0 %ffn0.1 = (bf16[2,256,256]{2,1,0:T(8,128)(2,1)}, f32[8,256,512]{2,1,0:T(8,128)}, bf16[8,256,256]{2,1,0:T(8,128)(2,1)}, bf16[256,256]{1,0:T(8,128)(2,1)}, f32[256...) custom-call(s32[8]{0:T(128)} %iota.50.refs_0_, ...), custom_call_target="tpu_custom_call" | custom-call | flops 16000000 | tf_op jit(solution)/shard_map/ffn0/pallas_call | solution.py:168
  151.4 2.8 collective-permute-start.26
  154.3 5.9 %collective-permute-done.24.refs_12_ = bf16[256,512]{1,0:T(8,128)(2,1)S(1)} collective-permute-done((bf16[256,512]{1,0:T(8,128)(2,1)}, bf16[256,512]{1,0:T(8,128)(2,1)S(1)}, u32[]{:S(2)}, u32[]{:S(2)}) %collective-permute-start.24) | collective-permute-done | bytes 262176 | tf_op jit(solution)/shard_map/ppermute | solution.py:810
  160.6 4.5 collective-permute-done.25.refs_13_
  171.6 31.7 %loop1.1 = (f32[256,640]{1,0:T(8,128)}, f32[256,640]{1,0:T(8,128)}, bf16[4,256,256]{2,1,0:T(8,128)(2,1)}, bf16[256,256]{1,0:T(8,128)(2,1)}, bf16[256,640]{1,0:T(...) custom-call(s32[4]{0:T(128)} %and_select_fusion.2.refs_0_, ...), custom_call_target="tpu_custom_call" | custom-call | flops 35000000 | tf_op jit(solution)/shard_map/loop1/pallas_call | solution.py:168
  203.7 5.8 %q_back1.1 = (bf16[4,256,256]{2,1,0:T(8,128)(2,1)}, bf16[256,256]{1,0:T(8,128)(2,1)}, f32[256,640]{1,0:T(8,128)}, f32[1,256]{1,0:T(1,128)}) custom-call(s32[8]{0:T(128)} %stack.47.refs_0_.refs_1_.refs_2_, s32[8]{0:T(128)} %stack.47.refs_0_.refs_1_.refs_2_, f32[256,128]{1,0:T(8,128)} %get-tuple-element.407.refs_2_.refs_7_.refs_1_, ...), custom_call_target="tpu_custom_call" | custom-call | flops 5800000 | tf_op jit(solution)/shard_map/q_back1/pallas_call | solution.py:168
  214.6 6.4 %gradsla.1 = (bf16[4,2432,128]{2,1,0:T(8,128)(2,1)}, bf16[4,2432,128]{2,1,0:T(8,128)(2,1)}) custom-call(s32[2]{0:T(128)} %pad_add_fusion.refs_0_, bf16[256,640]{1,0:T(8,128)(2,1)} %get-tuple-element.210.refs_1_.refs_3_, bf16[2,256,256]{2,1,0:T(8,128)(2,1)} %get-tuple-element.211.refs_2_, bf16[16,256,256]{2,1,0:T(8,128)(2,1)} %get-tuple-element.212.refs_3_.refs_4_, ...), custom_call_target="tpu_custom_call" | custom-call | flops 8600000 | tf_op jit(solution)/shard_map/gradsla/pallas_call | solution.py:168
  221.1 5.1 collective-permute-done.37
  227.1 6.4 %kv_back1.1 = (f32[1,256]{1,0:T(1,128)}, bf16[2,256,256]{2,1,0:T(8,128)(2,1)}, bf16[2,256,256]{2,1,0:T(8,128)(2,1)}, f32[1,640]{1,0:T(1,128)}, f32[256,640]{1,0:T(8,128)}) custom-call(s32[8]{0:T(128)} %stack.47.refs_0_.refs_1_.refs_2_, s32[8]{0:T(128)} %stack.47.refs_0_.refs_1_.refs_2_, f32[256,128]{1,0:T(8,128)} %get-tuple-element.407.refs_2_.refs_7_.refs_1_, ...), custom_call_target="tpu_custom_call" | custom-call | flops 6200000 | tf_op jit(solution)/shard_map/kv_back1/pallas_call | solution.py:168
  233.5 3.0 fusion.18
  240.5 13.9 %ffn_back0.1 = (f32[1,640]{1,0:T(1,128)}, f32[1,640]{1,0:T(1,128)}, bf16[256,640]{1,0:T(8,128)(2,1)}, bf16[256,256]{1,0:T(8,128)(2,1)}, bf16[16,256,256]{2,1,0:T...) custom-call(s32[8]{0:T(128)} %iota.51.refs_0_, ...), custom_call_target="tpu_custom_call" | custom-call | flops 14000000 | tf_op jit(solution)/shard_map/ffn_back0/pallas_call | solution.py:168
  254.4 9.3 %gradsg1.1 = (bf16[4,1760,128]{2,1,0:T(8,128)(2,1)}, bf16[4,1760,128]{2,1,0:T(8,128)(2,1)}, bf16[4,1664,128]{2,1,0:T(8,128)(2,1)}, bf16[4,1664,128]{2,1,0:T(8,128)(2,1)}) custom-call(s32[2]{0:T(128)} %pad_add_fusion.refs_0_, bf16[256,640]{1,0:T(8,128)(2,1)} %get-tuple-element.197.refs_3_.refs_1_, bf16[16,256,256]{2,1,0:T(8,128)(2,1)} %get-tuple-element.242.refs_2_.refs_3_, ...), custom_call_target="tpu_custom_call" | custom-call | flops 9700000 | tf_op jit(solution)/shard_map/gradsg1/pallas_call | solution.py:168
  263.8 2.8 collective-permute-done.41
  270.0 4.8 out_back0.1
  274.8 8.1 %gradsg3.1 = (bf16[4,1600,128]{2,1,0:T(8,128)(2,1)}, bf16[4,1600,128]{2,1,0:T(8,128)(2,1)}, bf16[4,1696,128]{2,1,0:T(8,128)(2,1)}, bf16[4,1696,128]{2,1,0:T(8,128)(2,1)}) custom-call(s32[2]{0:T(128)} %pad_add_fusion.refs_0_, bf16[256,640]{1,0:T(8,128)(2,1)} %get-tuple-element.197.refs_3_.refs_1_, bf16[2,256,256]{2,1,0:T(8,128)(2,1)} %get-tuple-element.200.refs_2_, ...), custom_call_target="tpu_custom_call" | custom-call | flops 8500000 | tf_op jit(solution)/shard_map/gradsg3/pallas_call | solution.py:168
  285.1 3.5 add_convert_fusion.4
  288.6 2.9 add_convert_fusion
  292.9 8.0 %collective-permute-start.49 = (bf16[1216,128]{1,0:T(8,128)(2,1)}, bf16[1216,128]{1,0:T(8,128)(2,1)}, u32[]{:S(2)}, u32[]{:S(2)}) collective-permute-start(bf16[1216,128]{1,0:T(8,128)(2,1)} %get-tuple-element.285), channel_id=1, source_target_pairs={{0,2},{2,0},{1,3},{3,1},{4,6},{6,4},{5,7},{7,5},{8,10},{10,8},{9,1... | collective-permute-start | bytes 933896 | tf_op jit(solution)/shard_map/ppermute | solution.py:814
  301.6 11.9 %attend_back0.1 = (f32[4,256,256]{2,1,0:T(8,128)}, bf16[4,256,512]{2,1,0:T(8,128)(2,1)}, bf16[4,256,512]{2,1,0:T(8,128)(2,1)}) custom-call(s32[4]{0:T(128)} %and_select_fusion.2.refs_0_, bf16[4,256,256]{2,1,0:T(8,128)(2,1)} %get-tuple-element.278.refs_1_, bf16[4,256,256]{2,1,0:T(8,128)(2,1)} %get-tuple-element.194.refs_3_.refs_2_, ...), custom_call_target="tpu_custom_call" | custom-call | flops 13000000 | tf_op jit(solution)/shard_map/attend_back0/pallas_call | solution.py:168
  317.3 4.8 collective-permute-done.47
  325.8 5.8 %q_back0.1 = (bf16[4,256,256]{2,1,0:T(8,128)(2,1)}, bf16[256,256]{1,0:T(8,128)(2,1)}, f32[256,640]{1,0:T(8,128)}, f32[1,256]{1,0:T(1,128)}) custom-call(s32[8]{0:T(128)} %stack.47.refs_0_.refs_1_.refs_2_, f32[256,128]{1,0:T(8,128)} %get-tuple-element.407.refs_2_.refs_7_.refs_1_, f32[256,128]{1,0:T(8,128)} %get-tuple-element.406.refs_3_.refs_8_.refs_2_, ...), custom_call_target="tpu_custom_call" | custom-call | flops 5800000 | tf_op jit(solution)/shard_map/q_back0/pallas_call | solution.py:168
  337.6 2.8 add_convert_fusion.7
  342.8 3.4 add_convert_fusion.2
  351.5 6.6 %gradsrb.1 = (bf16[4,2112,128]{2,1,0:T(8,128)(2,1)}, bf16[4,2112,128]{2,1,0:T(8,128)(2,1)}) custom-call(s32[2]{0:T(128)} %pad_add_fusion.refs_0_, bf16[4,256,256]{2,1,0:T(8,128)(2,1)} %get-tuple-element.273.refs_1_, bf16[256,256]{1,0:T(8,128)(2,1)} %get-tuple-element.274.refs_2_, bf16[256,640]{1,0:T(8,128)(2,1)} %get-tuple-element.275.refs_3_, ...), custom_call_target="tpu_custom_call" | custom-call | flops 7000000 | tf_op jit(solution)/shard_map/gradsrb/pallas_call | solution.py:168
  368.4 6.3 %kv_back0.1 = (f32[1,256]{1,0:T(1,128)}, bf16[2,256,256]{2,1,0:T(8,128)(2,1)}, bf16[2,256,256]{2,1,0:T(8,128)(2,1)}, f32[1,640]{1,0:T(1,128)}, f32[256,640]{1,0:T(8,128)}) custom-call(s32[8]{0:T(128)} %stack.47.refs_0_.refs_1_.refs_2_, f32[256,128]{1,0:T(8,128)} %get-tuple-element.407.refs_2_.refs_7_.refs_1_, ...), custom_call_target="tpu_custom_call" | custom-call | flops 6200000 | tf_op jit(solution)/shard_map/kv_back0/pallas_call | solution.py:168
  374.6 8.0 %collective-permute-done.63 = bf16[832,128]{1,0:T(8,128)(2,1)} collective-permute-done((bf16[832,128]{1,0:T(8,128)(2,1)}, bf16[832,128]{1,0:T(8,128)(2,1)}, u32[]{:S(2)}, u32[]{:S(2)}) %collective-permute-start.63) | collective-permute-done | bytes 213024 | tf_op jit(solution)/shard_map/ppermute | solution.py:814
  384.3 3.1 collective-permute-done.62
  391.2 2.8 fusion.22
  394.9 4.0 gradsra.1
  410.9 23.4 %collective-permute-done.65 = bf16[1696,128]{1,0:T(8,128)(2,1)S(1)} collective-permute-done((bf16[1696,128]{1,0:T(8,128)(2,1)S(1)}, bf16[1696,128]{1,0:T(8,128)(2,1)S(1)}, u32[]{:S(2)}, u32[]{:S(2)}) %collective-permute-start.65) | collective-permute-done | bytes 434208 | tf_op jit(solution)/shard_map/ppermute | solution.py:810
  445.3 4.8 collective-permute-done.72
  457.0 3.8 collective-permute-done.73
  460.8 3.5 collective-permute-done.74
  466.0 11.8 %collective-permute-done.77 = bf16[800,128]{1,0:T(8,128)(2,1)S(1)} collective-permute-done((bf16[800,128]{1,0:T(8,128)(2,1)}, bf16[800,128]{1,0:T(8,128)(2,1)S(1)}, u32[]{:S(2)}, u32[]{:S(2)}) %collective-permute-start.77) | collective-permute-done | bytes 204832 | tf_op jit(solution)/shard_map/ppermute | solution.py:814
  486.0 14.1 %collective-permute-done.86 = bf16[800,128]{1,0:T(8,128)(2,1)S(1)} collective-permute-done((bf16[800,128]{1,0:T(8,128)(2,1)}, bf16[800,128]{1,0:T(8,128)(2,1)S(1)}, u32[]{:S(2)}, u32[]{:S(2)}) %collective-permute-start.86) | collective-permute-done | bytes 204832 | tf_op jit(solution)/shard_map/ppermute | solution.py:814
  502.6 3.0 collective-permute-start.83
  506.4 2.8 collective-permute-done.83
  513.1 3.7 unpack.3
  518.4 2.9 unpack.2
  (393 shorter events, 149.2 us)
Async XLA Ops:
  7.2 126.2 %all-gather.2.cloned.1.call-start = ((), (), s32[]{:S(2)}) async-start(), calls=%async_computation | async-start | bytes 13492224 | tf_op jit(solution)/shard_map/all_gather | solution.py:1098
  13.0 18.6 %collective-permute-start = (bf16[1840,128]{1,0:T(8,128)(2,1)}, bf16[1840,128]{1,0:T(8,128)(2,1)S(1)}, u32[]{:S(2)}, u32[]{:S(2)}) collective-permute-start(bf16[1840,128]{1,0:T(8,128)(2,1)} %pack.5.refs_4_.refs_10_.refs_7_.refs_11_.refs_6_), channel_id=1, source_target_pairs={{0,8},{4,12},{8,0},{12,4},{16,24},{20,28},{24,16},{28,20},{1,9},{5... | collective-permute-start | bytes 1413128 | tf_op jit(solution)/shard_map/ppermute | solution.py:810
  15.9 21.4 %collective-permute-start.2 = (bf16[1840,128]{1,0:T(8,128)(2,1)}, bf16[1840,128]{1,0:T(8,128)(2,1)}, u32[]{:S(2)}, u32[]{:S(2)}) collective-permute-start(bf16[1840,128]{1,0:T(8,128)(2,1)} %pack.5.refs_4_.refs_10_.refs_7_.refs_11_.refs_6_), channel_id=1, source_target_pairs={{0,16},{4,20},{8,24},{12,28},{16,0},{20,4},{24,8},{28,12},{1,17},{... | collective-permute-start | bytes 1413128 | tf_op jit(solution)/shard_map/ppermute | solution.py:810
  32.4 22.2 %collective-permute-start.1 = (bf16[1840,128]{1,0:T(8,128)(2,1)}, bf16[1840,128]{1,0:T(8,128)(2,1)S(1)}, u32[]{:S(2)}, u32[]{:S(2)}) collective-permute-start(bf16[1840,128]{1,0:T(8,128)(2,1)} %after.21.refs_1_.refs_5_.refs_11_.refs_8_.refs_12_.refs_7_), channel_id=1, source_target_pairs={{0,16},{4,20},{8,24},{12,28},{16,0},{20,4},{24,8},{28,12},{1,17},{... | collective-permute-start | bytes 1413128 | tf_op jit(solution)/shard_map/ppermute | solution.py:810
  33.7 21.9 %collective-permute-start.3 = (bf16[1840,128]{1,0:T(8,128)(2,1)S(1)}, bf16[1840,128]{1,0:T(8,128)(2,1)}, u32[]{:S(2)}, u32[]{:S(2)}) collective-permute-start(bf16[1840,128]{1,0:T(8,128)(2,1)S(1)} %copy-done.2), channel_id=1, source_target_pairs={{0,4},{4,0},{8,12},{12,8},{16,20},{20,16},{24,28},{28,24},{1,5},{5... | collective-permute-start | bytes 1413128 | tf_op jit(solution)/shard_map/ppermute | solution.py:810
  33.7 23.4 %collective-permute-start.4 = (bf16[1840,128]{1,0:T(8,128)(2,1)}, bf16[1840,128]{1,0:T(8,128)(2,1)}, u32[]{:S(2)}, u32[]{:S(2)}) collective-permute-start(bf16[1840,128]{1,0:T(8,128)(2,1)} %after.21.refs_1_.refs_5_.refs_11_.refs_8_.refs_12_.refs_7_), channel_id=1, source_target_pairs={{0,4},{4,0},{8,12},{12,8},{16,20},{20,16},{24,28},{28,24},{1,5},{5... | collective-permute-start | bytes 1413128 | tf_op jit(solution)/shard_map/ppermute | solution.py:810
  34.9 22.1 %collective-permute-start.14 = (bf16[1920,128]{1,0:T(8,128)(2,1)}, bf16[1920,128]{1,0:T(8,128)(2,1)S(1)}, u32[]{:S(2)}, u32[]{:S(2)}) collective-permute-start(bf16[1920,128]{1,0:T(8,128)(2,1)} %after.22.refs_1_), channel_id=1, source_target_pairs={{0,8},{4,12},{8,0},{12,4},{16,24},{20,28},{24,16},{28,20},{1,9},{5... | collective-permute-start | bytes 1474568 | tf_op jit(solution)/shard_map/ppermute | solution.py:810
  37.3 20.9 %collective-permute-start.5 = (bf16[1840,128]{1,0:T(8,128)(2,1)}, bf16[1840,128]{1,0:T(8,128)(2,1)}, u32[]{:S(2)}, u32[]{:S(2)}) collective-permute-start(bf16[1840,128]{1,0:T(8,128)(2,1)} %collective-permute-done.2.refs_6_.refs_12_.refs_9_.refs_13_.refs_8_), channel_id=1, source_target_pairs={{0,4},{4,0},{8,12},{12,8},{16,20},{20,16},{24,28},{28,24},{1,5},{5... | collective-permute-start | bytes 1413128 | tf_op jit(solution)/shard_map/ppermute | solution.py:810
  55.5 21.5 %collective-permute-start.15 = (bf16[1920,128]{1,0:T(8,128)(2,1)}, bf16[1920,128]{1,0:T(8,128)(2,1)S(1)}, u32[]{:S(2)}, u32[]{:S(2)}) collective-permute-start(bf16[1920,128]{1,0:T(8,128)(2,1)} %after.23.refs_2_), channel_id=1, source_target_pairs={{0,16},{4,20},{8,24},{12,28},{16,0},{20,4},{24,8},{28,12},{1,17},{... | collective-permute-start | bytes 1474568 | tf_op jit(solution)/shard_map/ppermute | solution.py:810
  57.1 20.0 %collective-permute-start.17 = (bf16[1920,128]{1,0:T(8,128)(2,1)S(1)}, bf16[1920,128]{1,0:T(8,128)(2,1)S(1)}, u32[]{:S(2)}, u32[]{:S(2)}) collective-permute-start(bf16[1920,128]{1,0:T(8,128)(2,1)S(1)} %copy-done), channel_id=1, source_target_pairs={{0,4},{4,0},{8,12},{12,8},{16,20},{20,16},{24,28},{28,24},{1,5},{5... | collective-permute-start | bytes 1474568 | tf_op jit(solution)/shard_map/ppermute | solution.py:810
  57.1 24.0 %collective-permute-start.18 = (bf16[1920,128]{1,0:T(8,128)(2,1)S(1)}, bf16[1920,128]{1,0:T(8,128)(2,1)S(1)}, u32[]{:S(2)}, u32[]{:S(2)}) collective-permute-start(bf16[1920,128]{1,0:T(8,128)(2,1)S(1)} %collective-permute-done.14.refs_17_.refs_19_.refs_20_.refs_16_.refs_5_), channel_id=1, source_target_pairs={{0,4},{4,0},{8,12},{12,8},{16,20},{20,16},{24,28},{28,24},{1,5},{5... | collective-permute-start | bytes 1474568 | tf_op jit(solution)/shard_map/ppermute | solution.py:810
  65.8 15.3 %collective-permute-start.7 = (bf16[256,512]{1,0:T(8,128)(2,1)}, bf16[256,512]{1,0:T(8,128)(2,1)}, u32[]{:S(2)}, u32[]{:S(2)}) collective-permute-start(bf16[256,512]{1,0:T(8,128)(2,1)} %get-tuple-element.196.refs_8_), channel_id=1, source_target_pairs={{0,8},{4,12},{8,0},{12,4},{16,24},{20,28},{24,16},{28,20},{1,9},{5... | collective-permute-start | bytes 786440 | tf_op jit(solution)/shard_map/ppermute | solution.py:810
  77.0 39.3 %collective-permute-start.16 = (bf16[1920,128]{1,0:T(8,128)(2,1)S(1)}, bf16[1920,128]{1,0:T(8,128)(2,1)S(1)}, u32[]{:S(2)}, u32[]{:S(2)}) collective-permute-start(bf16[1920,128]{1,0:T(8,128)(2,1)S(1)} %collective-permute-done.15.refs_18_.refs_20_.refs_21_.refs_17_.refs_6_), channel_id=1, source_target_pairs={{0,8},{4,12},{8,0},{12,4},{16,24},{20,28},{24,16},{28,20},{1,9},{5... | collective-permute-start | bytes 1474568 | tf_op jit(solution)/shard_map/ppermute | solution.py:810
  77.0 42.2 %collective-permute-start.19 = (bf16[1920,128]{1,0:T(8,128)(2,1)S(1)}, bf16[1920,128]{1,0:T(8,128)(2,1)}, u32[]{:S(2)}, u32[]{:S(2)}) collective-permute-start(bf16[1920,128]{1,0:T(8,128)(2,1)S(1)} %collective-permute-done.15.refs_18_.refs_20_.refs_21_.refs_17_.refs_6_), channel_id=1, source_target_pairs={{0,4},{4,0},{8,12},{12,8},{16,20},{20,16},{24,28},{28,24},{1,5},{5... | collective-permute-start | bytes 1474568 | tf_op jit(solution)/shard_map/ppermute | solution.py:810
  77.1 36.8 %collective-permute-start.9 = (bf16[256,512]{1,0:T(8,128)(2,1)}, bf16[256,512]{1,0:T(8,128)(2,1)S(1)}, u32[]{:S(2)}, u32[]{:S(2)}) collective-permute-start(bf16[256,512]{1,0:T(8,128)(2,1)} %get-tuple-element.196.refs_8_), channel_id=1, source_target_pairs={{0,24},{4,28},{8,16},{12,20},{16,8},{20,12},{24,0},{28,4},{1,25},{... | collective-permute-start | bytes 786440 | tf_op jit(solution)/shard_map/ppermute | solution.py:810
  81.0 34.6 %collective-permute-start.8 = (bf16[256,512]{1,0:T(8,128)(2,1)}, bf16[256,512]{1,0:T(8,128)(2,1)}, u32[]{:S(2)}, u32[]{:S(2)}) collective-permute-start(bf16[256,512]{1,0:T(8,128)(2,1)} %get-tuple-element.196.refs_8_), channel_id=1, source_target_pairs={{0,16},{4,20},{8,24},{12,28},{16,0},{20,4},{24,8},{28,12},{1,17},{... | collective-permute-start | bytes 786440 | tf_op jit(solution)/shard_map/ppermute | solution.py:810
  81.1 34.8 %collective-permute-start.10 = (bf16[256,512]{1,0:T(8,128)(2,1)}, bf16[256,512]{1,0:T(8,128)(2,1)S(1)}, u32[]{:S(2)}, u32[]{:S(2)}) collective-permute-start(bf16[256,512]{1,0:T(8,128)(2,1)} %get-tuple-element.196.refs_8_), channel_id=1, source_target_pairs={{0,4},{4,0},{8,12},{12,8},{16,20},{20,16},{24,28},{28,24},{1,5},{5... | collective-permute-start | bytes 786440 | tf_op jit(solution)/shard_map/ppermute | solution.py:810
  115.7 34.3 %collective-permute-start.21 = (bf16[2432,128]{1,0:T(8,128)(2,1)}, bf16[2432,128]{1,0:T(8,128)(2,1)S(1)}, u32[]{:S(2)}, u32[]{:S(2)}) collective-permute-start(bf16[2432,128]{1,0:T(8,128)(2,1)} %after.25.refs_0_), channel_id=1, source_target_pairs={{0,8},{4,12},{8,0},{12,4},{16,24},{20,28},{24,16},{28,20},{1,9},{5... | collective-permute-start | bytes 1867784 | tf_op jit(solution)/shard_map/ppermute | solution.py:810
  115.8 34.1 %collective-permute-start.22 = (bf16[2432,128]{1,0:T(8,128)(2,1)}, bf16[2432,128]{1,0:T(8,128)(2,1)}, u32[]{:S(2)}, u32[]{:S(2)}) collective-permute-start(bf16[2432,128]{1,0:T(8,128)(2,1)} %after.25.refs_0_), channel_id=1, source_target_pairs={{0,16},{4,20},{8,24},{12,28},{16,0},{20,4},{24,8},{28,12},{1,17},{... | collective-permute-start | bytes 1867784 | tf_op jit(solution)/shard_map/ppermute | solution.py:810
  116.3 33.7 %collective-permute-start.23 = (bf16[2432,128]{1,0:T(8,128)(2,1)}, bf16[2432,128]{1,0:T(8,128)(2,1)}, u32[]{:S(2)}, u32[]{:S(2)}) collective-permute-start(bf16[2432,128]{1,0:T(8,128)(2,1)} %after.25.refs_0_), channel_id=1, source_target_pairs={{0,24},{4,28},{8,16},{12,20},{16,8},{20,12},{24,0},{28,4},{1,25},{... | collective-permute-start | bytes 1867784 | tf_op jit(solution)/shard_map/ppermute | solution.py:810
  236.5 27.3 %collective-permute-start.40 = (bf16[2432,128]{1,0:T(8,128)(2,1)}, bf16[2432,128]{1,0:T(8,128)(2,1)S(1)}, u32[]{:S(2)}, u32[]{:S(2)}) collective-permute-start(bf16[2432,128]{1,0:T(8,128)(2,1)} %get-tuple-element.255), channel_id=1, source_target_pairs={{0,8},{4,12},{8,0},{12,4},{16,24},{20,28},{24,16},{28,20},{1,9},{5... | collective-permute-start | bytes 1867784 | tf_op jit(solution)/shard_map/ppermute | solution.py:810
  236.7 29.8 %collective-permute-start.41 = (bf16[2432,128]{1,0:T(8,128)(2,1)}, bf16[2432,128]{1,0:T(8,128)(2,1)}, u32[]{:S(2)}, u32[]{:S(2)}) collective-permute-start(bf16[2432,128]{1,0:T(8,128)(2,1)} %get-tuple-element.256), channel_id=1, source_target_pairs={{0,16},{4,20},{8,24},{12,28},{16,0},{20,4},{24,8},{28,12},{1,17},{... | collective-permute-start | bytes 1867784 | tf_op jit(solution)/shard_map/ppermute | solution.py:810
  238.2 28.4 %collective-permute-start.42 = (bf16[2432,128]{1,0:T(8,128)(2,1)}, bf16[2432,128]{1,0:T(8,128)(2,1)}, u32[]{:S(2)}, u32[]{:S(2)}) collective-permute-start(bf16[2432,128]{1,0:T(8,128)(2,1)} %get-tuple-element.257), channel_id=1, source_target_pairs={{0,24},{4,28},{8,16},{12,20},{16,8},{20,12},{24,0},{28,4},{1,25},{... | collective-permute-start | bytes 1867784 | tf_op jit(solution)/shard_map/ppermute | solution.py:810
  269.4 19.2 %collective-permute-start.43 = (bf16[4,1760,128]{2,1,0:T(8,128)(2,1)}, bf16[4,1760,128]{2,1,0:T(8,128)(2,1)}, u32[]{:S(2)}, u32[]{:S(2)}) collective-permute-start(bf16[4,1760,128]{2,1,0:T(8,128)(2,1)} %get-tuple-element.263), channel_id=1, source_target_pairs={{0,4},{4,0},{8,12},{12,8},{16,20},{20,16},{24,28},{28,24},{1,5},{5... | collective-permute-start | bytes 5406728 | tf_op jit(solution)/shard_map/ppermute | solution.py:810
  291.4 24.9 %collective-permute-start.48 = (bf16[2,1664,128]{2,1,0:T(8,128)(2,1)}, bf16[2,1664,128]{2,1,0:T(8,128)(2,1)S(1)}, u32[]{:S(2)}, u32[]{:S(2)}) collective-permute-start(bf16[2,1664,128]{2,1,0:T(8,128)(2,1)} %get-tuple-element.284), channel_id=1, source_target_pairs={{0,16},{4,20},{8,24},{12,28},{16,0},{20,4},{24,8},{28,12},{1,17},{... | collective-permute-start | bytes 2555912 | tf_op jit(solution)/shard_map/ppermute | solution.py:810
  292.9 21.6 %collective-permute-start.49 = (bf16[1216,128]{1,0:T(8,128)(2,1)}, bf16[1216,128]{1,0:T(8,128)(2,1)}, u32[]{:S(2)}, u32[]{:S(2)}) collective-permute-start(bf16[1216,128]{1,0:T(8,128)(2,1)} %get-tuple-element.285), channel_id=1, source_target_pairs={{0,2},{2,0},{1,3},{3,1},{4,6},{6,4},{5,7},{7,5},{8,10},{10,8},{9,1... | collective-permute-start | bytes 933896 | tf_op jit(solution)/shard_map/ppermute | solution.py:814
  300.8 21.3 %collective-permute-start.47 = (bf16[2,1760,128]{2,1,0:T(8,128)(2,1)}, bf16[2,1760,128]{2,1,0:T(8,128)(2,1)S(1)}, u32[]{:S(2)}, u32[]{:S(2)}) collective-permute-start(bf16[2,1760,128]{2,1,0:T(8,128)(2,1)} %get-tuple-element.283), channel_id=1, source_target_pairs={{0,8},{4,12},{8,0},{12,4},{16,24},{20,28},{24,16},{28,20},{1,9},{5... | collective-permute-start | bytes 2703368 | tf_op jit(solution)/shard_map/ppermute | solution.py:810
  323.7 19.1 %collective-permute-start.53 = (bf16[4,1696,128]{2,1,0:T(8,128)(2,1)}, bf16[4,1696,128]{2,1,0:T(8,128)(2,1)}, u32[]{:S(2)}, u32[]{:S(2)}) collective-permute-start(bf16[4,1696,128]{2,1,0:T(8,128)(2,1)} %get-tuple-element.298), channel_id=1, source_target_pairs={{0,4},{4,0},{8,12},{12,8},{16,20},{20,16},{24,28},{28,24},{1,5},{5... | collective-permute-start | bytes 5210120 | tf_op jit(solution)/shard_map/ppermute | solution.py:810
  325.8 14.6 %collective-permute-start.50 = (bf16[4,256,512]{2,1,0:T(8,128)(2,1)}, bf16[4,256,512]{2,1,0:T(8,128)(2,1)}, u32[]{:S(2)}, u32[]{:S(2)}) collective-permute-start(bf16[4,256,512]{2,1,0:T(8,128)(2,1)} %get-tuple-element.287), channel_id=1, source_target_pairs={{0,4},{4,0},{8,12},{12,8},{16,20},{20,16},{24,28},{28,24},{1,5},{5... | collective-permute-start | bytes 3145736 | tf_op jit(solution)/shard_map/ppermute | solution.py:810
  342.5 15.5 %collective-permute-start.55 = (bf16[832,128]{1,0:T(8,128)(2,1)}, bf16[832,128]{1,0:T(8,128)(2,1)}, u32[]{:S(2)}, u32[]{:S(2)}) collective-permute-start(bf16[832,128]{1,0:T(8,128)(2,1)} %get-tuple-element.300), channel_id=1, source_target_pairs={{0,1},{1,0},{2,3},{3,2},{4,5},{5,4},{6,7},{7,6},{8,9},{9,8},{10,11... | collective-permute-start | bytes 638984 | tf_op jit(solution)/shard_map/ppermute | solution.py:814
  346.2 15.2 %collective-permute-start.56 = (bf16[256,512]{1,0:T(8,128)(2,1)S(1)}, bf16[256,512]{1,0:T(8,128)(2,1)S(1)}, u32[]{:S(2)}, u32[]{:S(2)}) collective-permute-start(bf16[256,512]{1,0:T(8,128)(2,1)S(1)} %copy-done.35), channel_id=1, source_target_pairs={{0,8},{4,12},{8,0},{12,4},{16,24},{20,28},{24,16},{28,20},{1,9},{5... | collective-permute-start | bytes 786440 | tf_op jit(solution)/shard_map/ppermute | solution.py:810
  363.5 27.6 %collective-permute-start.61 = (bf16[4,2112,128]{2,1,0:T(8,128)(2,1)}, bf16[4,2112,128]{2,1,0:T(8,128)(2,1)}, u32[]{:S(2)}, u32[]{:S(2)}) collective-permute-start(bf16[4,2112,128]{2,1,0:T(8,128)(2,1)} %get-tuple-element.308), channel_id=1, source_target_pairs={{0,4},{4,0},{8,12},{12,8},{16,20},{20,16},{24,28},{28,24},{1,5},{5... | collective-permute-start | bytes 6488072 | tf_op jit(solution)/shard_map/ppermute | solution.py:810
  363.6 25.5 %collective-permute-start.59 = (bf16[2,1600,128]{2,1,0:T(8,128)(2,1)}, bf16[2,1600,128]{2,1,0:T(8,128)(2,1)S(1)}, u32[]{:S(2)}, u32[]{:S(2)}) collective-permute-start(bf16[2,1600,128]{2,1,0:T(8,128)(2,1)} %get-tuple-element.305), channel_id=1, source_target_pairs={{0,8},{4,12},{8,0},{12,4},{16,24},{20,28},{24,16},{28,20},{1,9},{5... | collective-permute-start | bytes 2457608 | tf_op jit(solution)/shard_map/ppermute | solution.py:810
  364.9 17.8 %collective-permute-start.63 = (bf16[832,128]{1,0:T(8,128)(2,1)}, bf16[832,128]{1,0:T(8,128)(2,1)}, u32[]{:S(2)}, u32[]{:S(2)}) collective-permute-start(bf16[832,128]{1,0:T(8,128)(2,1)} %get-tuple-element.313), channel_id=1, source_target_pairs={{0,2},{2,0},{1,3},{3,1},{4,6},{6,4},{5,7},{7,5},{8,10},{10,8},{9,1... | collective-permute-start | bytes 638984 | tf_op jit(solution)/shard_map/ppermute | solution.py:814
  365.1 22.3 %collective-permute-start.62 = (bf16[880,128]{1,0:T(8,128)(2,1)}, bf16[880,128]{1,0:T(8,128)(2,1)}, u32[]{:S(2)}, u32[]{:S(2)}) collective-permute-start(bf16[880,128]{1,0:T(8,128)(2,1)} %get-tuple-element.312), channel_id=1, source_target_pairs={{0,2},{2,0},{1,3},{3,1},{4,6},{6,4},{5,7},{7,5},{8,10},{10,8},{9,1... | collective-permute-start | bytes 675848 | tf_op jit(solution)/shard_map/ppermute | solution.py:814
  367.8 22.4 %collective-permute-start.60 = (bf16[2,1696,128]{2,1,0:T(8,128)(2,1)}, bf16[2,1696,128]{2,1,0:T(8,128)(2,1)S(1)}, u32[]{:S(2)}, u32[]{:S(2)}) collective-permute-start(bf16[2,1696,128]{2,1,0:T(8,128)(2,1)} %get-tuple-element.306), channel_id=1, source_target_pairs={{0,16},{4,20},{8,24},{12,28},{16,0},{20,4},{24,8},{28,12},{1,17},{... | collective-permute-start | bytes 2605064 | tf_op jit(solution)/shard_map/ppermute | solution.py:810
  394.9 45.0 %collective-permute-start.80 = (bf16[1216,128]{1,0:T(8,128)(2,1)S(1)}, bf16[1216,128]{1,0:T(8,128)(2,1)}, u32[]{:S(2)}, u32[]{:S(2)}) collective-permute-start(bf16[1216,128]{1,0:T(8,128)(2,1)S(1)} %copy-done.13), channel_id=1, source_target_pairs={{0,1},{1,0},{2,3},{3,2},{4,5},{5,4},{6,7},{7,6},{8,9},{9,8},{10,11... | collective-permute-start | bytes 933896 | tf_op jit(solution)/shard_map/ppermute | solution.py:814
  398.9 36.3 %collective-permute-start.66 = (bf16[2112,128]{1,0:T(8,128)(2,1)}, bf16[2112,128]{1,0:T(8,128)(2,1)}, u32[]{:S(2)}, u32[]{:S(2)}) collective-permute-start(bf16[2112,128]{1,0:T(8,128)(2,1)} %get-tuple-element.333), channel_id=1, source_target_pairs={{0,8},{4,12},{8,0},{12,4},{16,24},{20,28},{24,16},{28,20},{1,9},{5... | collective-permute-start | bytes 1622024 | tf_op jit(solution)/shard_map/ppermute | solution.py:810
  400.4 34.8 %collective-permute-start.67 = (bf16[2112,128]{1,0:T(8,128)(2,1)S(1)}, bf16[2112,128]{1,0:T(8,128)(2,1)}, u32[]{:S(2)}, u32[]{:S(2)}) collective-permute-start(bf16[2112,128]{1,0:T(8,128)(2,1)S(1)} %copy-done.20), channel_id=1, source_target_pairs={{0,16},{4,20},{8,24},{12,28},{16,0},{20,4},{24,8},{28,12},{1,17},{... | collective-permute-start | bytes 1622024 | tf_op jit(solution)/shard_map/ppermute | solution.py:810
  401.3 33.9 %collective-permute-start.68 = (bf16[2112,128]{1,0:T(8,128)(2,1)S(1)}, bf16[2112,128]{1,0:T(8,128)(2,1)}, u32[]{:S(2)}, u32[]{:S(2)}) collective-permute-start(bf16[2112,128]{1,0:T(8,128)(2,1)S(1)} %copy-done.19), channel_id=1, source_target_pairs={{0,24},{4,28},{8,16},{12,20},{16,8},{20,12},{24,0},{28,4},{1,25},{... | collective-permute-start | bytes 1622024 | tf_op jit(solution)/shard_map/ppermute | solution.py:810
  407.5 26.8 %collective-permute-start.65 = (bf16[1696,128]{1,0:T(8,128)(2,1)S(1)}, bf16[1696,128]{1,0:T(8,128)(2,1)S(1)}, u32[]{:S(2)}, u32[]{:S(2)}) collective-permute-start(bf16[1696,128]{1,0:T(8,128)(2,1)S(1)} %copy-done.28), channel_id=1, source_target_pairs={{0,8},{4,12},{8,0},{12,4},{16,24},{20,28},{24,16},{28,20},{1,9},{5... | collective-permute-start | bytes 1302536 | tf_op jit(solution)/shard_map/ppermute | solution.py:810
  443.8 35.6 %collective-permute-start.69 = (bf16[880,128]{1,0:T(8,128)(2,1)}, bf16[880,128]{1,0:T(8,128)(2,1)S(1)}, u32[]{:S(2)}, u32[]{:S(2)}) collective-permute-start(bf16[880,128]{1,0:T(8,128)(2,1)} %get-tuple-element.336), channel_id=1, source_target_pairs={{0,1},{1,0},{2,3},{3,2},{4,5},{5,4},{6,7},{7,6},{8,9},{9,8},{10,11... | collective-permute-start | bytes 675848 | tf_op jit(solution)/shard_map/ppermute | solution.py:814
  457.0 21.6 %collective-permute-start.78 = (bf16[848,128]{1,0:T(8,128)(2,1)}, bf16[848,128]{1,0:T(8,128)(2,1)S(1)}, u32[]{:S(2)}, u32[]{:S(2)}) collective-permute-start(bf16[848,128]{1,0:T(8,128)(2,1)} %get-tuple-element.346), channel_id=1, source_target_pairs={{0,2},{2,0},{1,3},{3,1},{4,6},{6,4},{5,7},{7,5},{8,10},{10,8},{9,1... | collective-permute-start | bytes 651272 | tf_op jit(solution)/shard_map/ppermute | solution.py:814
  460.8 17.0 %collective-permute-start.77 = (bf16[800,128]{1,0:T(8,128)(2,1)}, bf16[800,128]{1,0:T(8,128)(2,1)S(1)}, u32[]{:S(2)}, u32[]{:S(2)}) collective-permute-start(bf16[800,128]{1,0:T(8,128)(2,1)} %get-tuple-element.345), channel_id=1, source_target_pairs={{0,2},{2,0},{1,3},{3,1},{4,6},{6,4},{5,7},{7,5},{8,10},{10,8},{9,1... | collective-permute-start | bytes 614408 | tf_op jit(solution)/shard_map/ppermute | solution.py:814
  480.2 32.2 %collective-permute-start.87 = (bf16[848,128]{1,0:T(8,128)(2,1)}, bf16[848,128]{1,0:T(8,128)(2,1)S(1)}, u32[]{:S(2)}, u32[]{:S(2)}) collective-permute-start(bf16[848,128]{1,0:T(8,128)(2,1)} %get-tuple-element.356), channel_id=1, source_target_pairs={{0,1},{1,0},{2,3},{3,2},{4,5},{5,4},{6,7},{7,6},{8,9},{9,8},{10,11... | collective-permute-start | bytes 651272 | tf_op jit(solution)/shard_map/ppermute | solution.py:814
  482.2 17.9 %collective-permute-start.86 = (bf16[800,128]{1,0:T(8,128)(2,1)}, bf16[800,128]{1,0:T(8,128)(2,1)S(1)}, u32[]{:S(2)}, u32[]{:S(2)}) collective-permute-start(bf16[800,128]{1,0:T(8,128)(2,1)} %get-tuple-element.355), channel_id=1, source_target_pairs={{0,1},{1,0},{2,3},{3,2},{4,5},{5,4},{6,7},{7,6},{8,9},{9,8},{10,11... | collective-permute-start | bytes 614408 | tf_op jit(solution)/shard_map/ppermute | solution.py:814
  482.2 23.4 %collective-permute-start.79 = (bf16[832,128]{1,0:T(8,128)(2,1)}, bf16[832,128]{1,0:T(8,128)(2,1)S(1)}, u32[]{:S(2)}, u32[]{:S(2)}) collective-permute-start(bf16[832,128]{1,0:T(8,128)(2,1)} %get-tuple-element.347), channel_id=1, source_target_pairs={{0,1},{1,0},{2,3},{3,2},{4,5},{5,4},{6,7},{7,6},{8,9},{9,8},{10,11... | collective-permute-start | bytes 638984 | tf_op jit(solution)/shard_map/ppermute | solution.py:814
  484.2 17.6 %collective-permute-start.82 = (bf16[1056,128]{1,0:T(8,128)(2,1)}, bf16[1056,128]{1,0:T(8,128)(2,1)S(1)}, u32[]{:S(2)}, u32[]{:S(2)}) collective-permute-start(bf16[1056,128]{1,0:T(8,128)(2,1)} %get-tuple-element.350), channel_id=1, source_target_pairs={{0,2},{2,0},{1,3},{3,1},{4,6},{6,4},{5,7},{7,5},{8,10},{10,8},{9,1... | collective-permute-start | bytes 811016 | tf_op jit(solution)/shard_map/ppermute | solution.py:814
  (105 other events, 993.6 us)
Sparse Core Ops, SparseCore 0:
  10.3 107.4 all-gather.1

commit v2 on v1

--- a/solution.py
+++ b/solution.py
@@ -79,6 +79,7 @@
     def __init__(self):
         self.refs = {}
         self.pending = {}
+        self.later = []
 
     def __getitem__(self, name):
         return self.refs[name]
@@ -88,10 +89,14 @@
             sem = self.pending.pop(name)
             ref = self.refs[N.w(name)]
             pltpu.make_async_copy(ref, ref, sem).wait()
+            if name == self.hold:
+                for copy in self.later:
+                    copy.start()
+                self.later = []
         return self.refs[N.w(name)]
 
 
-def run_kernel(sizes, name, stages, ins, outs, scratch=(), weights=(), smem=(), micros=0):
+def run_kernel(sizes, name, stages, ins, outs, scratch=(), weights=(), smem=(), micros=0, hold=None):
     chunks = []
     for _, chunk in weights:
         if chunk not in chunks:
@@ -115,6 +120,7 @@
 
     def kernel(*refs):
         env = Env()
+        env.hold, held = hold, False
         position = 0
         for key in names_smem + names_in:
             env.refs[key] = refs[position]
@@ -153,8 +159,13 @@
                     else:
                         row = pl.multiple_of(env[N.ids(which)][slot] * rows, 16)
                         target = buffer.at[:, pl.ds(row, rows), :]
-                pltpu.make_async_copy(source, target, sem).start()
+                copy = pltpu.make_async_copy(source, target, sem)
+                if held:
+                    env.later.append(copy)
+                else:
+                    copy.start()
             env.pending[wname] = sem
+            held = held or wname == hold
         env.ids = lambda chunk: env[N.ids(chunks.index(chunk))]
         for stage in stages:
             stage(env)
@@ -290,7 +301,7 @@
     rows = slice(qb * sizes.QB, (qb + 1) * sizes.QB)
     slot = jnp.concatenate([env[N.qslot][rows, :]] * sizes.H, axis=0)
     low = jnp.concatenate([env[N.qstart][rows, :]] * sizes.H, axis=0)
-    last = (qb + 1) * sizes.QB // sizes.IB
+    last = -(-(qb + 1) * sizes.QB // sizes.IB)
     return rows, slot, low, last
 
 
@@ -360,18 +371,18 @@
             env[N.gmid(l)][j] = mid
             mids.append(mid)
         bg, bu, gu = env.w(N.bg), env.w(N.bu), env.w(N.gu)
-        dnw, dna = env.w(N.dnw), env.w(N.dna)
         blocks = sizes.F // 256
         out = jnp.zeros((sizes.T, sizes.D), F32)
         down = jnp.zeros((sizes.T, sizes.R), F32)
         for b in range(blocks):
             gate = dot(x, columns(gu, 2 * b, 2)) + dot(mids[0], columns(bg, 2 * b, 2))
             up = dot(x, columns(gu, 2 * (blocks + b), 2)) + dot(mids[1], columns(bu, 2 * b, 2))
-            env[N.gu(l)][b, :, :256] = gate
-            env[N.gu(l)][b, :, 256:] = up
+            env[N.gu(l)][b, :, :256] = gate.astype(env[N.gu(l)].dtype)
+            env[N.gu(l)][b, :, 256:] = up.astype(env[N.gu(l)].dtype)
             hidden = (gelu_parts(gate)[0] * up).astype(BF)
             env[N.hidden(l)][b] = hidden
             rows = slice(b * 256, (b + 1) * 256)
+            dnw, dna = env.w(N.dnw), env.w(N.dna)
             out = out + dot(hidden, columns(dnw, 0, sizes.DB, rows))
             down = down + dot(hidden, columns(dna, 0, sizes.RB, rows))
         down = down.astype(BF)
@@ -392,7 +403,7 @@
         env[N.ffn_low(l)][...] = low
         dmg = dot_nt(low, columns(env.w(N.dnb), 0, sizes.DB)).astype(BF)
         env[N.dmg(l)][...] = dmg
-        dnw, dna, bg, bu, gu = env.w(N.dnw), env.w(N.dna), env.w(N.bg), env.w(N.bu), env.w(N.gu)
+        dnw, dna = env.w(N.dnw), env.w(N.dna)
         blocks = sizes.F // 256
         gate_mid = jnp.zeros((sizes.T, sizes.R), F32)
         up_mid = jnp.zeros((sizes.T, sizes.R), F32)
@@ -402,12 +413,13 @@
             hidden_grad = dot_nt(low, columns(dnw, 0, sizes.DB, rows)) + dot_nt(
                 dmg, columns(dna, 0, sizes.RB, rows)
             )
-            gate, up = env[N.gu(l)][b, :, :256], env[N.gu(l)][b, :, 256:]
+            gate, up = env[N.gu(l)][b, :, :256].astype(F32), env[N.gu(l)][b, :, 256:].astype(F32)
             value, t = gelu_parts(gate)
             gate_grad = (hidden_grad * up * gelu_slope(gate, t)).astype(BF)
             up_grad = (hidden_grad * value).astype(BF)
             env[N.gug(l)][b] = gate_grad
             env[N.gug(l)][blocks + b] = up_grad
+            bg, bu, gu = env.w(N.bg), env.w(N.bu), env.w(N.gu)
             gate_mid = gate_mid + dot_nt(gate_grad, columns(bg, 2 * b, 2))
             up_mid = up_mid + dot_nt(up_grad, columns(bu, 2 * b, 2))
             total = total + dot_nt(gate_grad, columns(gu, 2 * b, 2))
@@ -789,7 +801,8 @@
             for lead, prefix, name, column in parts:
                 layout = sources[prefix][2]
                 if name == N.norm:
-                    out[...] = rows_of(prefix, layout.gains, 16)
+                    first, count = lead
+                    out[...] = rows_of(prefix, layout.gains, 16)[first : first + count, : out.shape[1]]
                     continue
                 first, rows, blocks = layout.at[name]
                 for b in range(blocks):
@@ -960,7 +973,7 @@
         s.R = adapter_query_second.shape[1] * n
         s.F = shared_down_matrix.shape[0] * n
         s.DB, s.RB, s.HB = s.D // LANES, s.R // LANES, s.HD // LANES
-        s.IB = max(16, 256 // n)
+        s.IB = max(16, 1024 // n)
         s.QB = s.T // 4
         s.kv_pieces = 8 if fast else 1
         QW, k = s.H * s.HD, s.slots
@@ -1152,7 +1165,7 @@
                 N.middle(l): ((T, D), F32),
                 N.ffn_in(l): ((T, D), BF),
                 N.gmid(l): ((2, T, R), BF),
-                N.gu(l): ((blocks, T, 512), F32),
+                N.gu(l): ((blocks, T, 512), BF if l == 0 else F32),
                 N.hidden(l): ((blocks, T, 256), BF),
                 N.dmid(l): ((T, R), BF),
                 N.ffn_out(l): ((T, D), F32),
@@ -1178,7 +1191,7 @@
             for i in range(4):
                 shapes[N.dnorm(l, i)] = ((1, D), F32)
 
-        def call(name, stages, ins, outs, scratch=(), weights=(), smem=(), micros=0):
+        def call(name, stages, ins, outs, scratch=(), weights=(), smem=(), micros=0, hold=None):
             made = run_kernel(
                 s,
                 name,
@@ -1189,6 +1202,7 @@
                 weights,
                 {m: v[m] for m in smem},
                 micros,
+                hold,
             )
             v.update(made)
 
@@ -1257,7 +1271,8 @@
             [stage_ffn(s, 0), stage_qkv(s, 1, N.stream1)],
             [N.ffn_in0, N.middle0, N.norm, N.qkg, N.cos, N.sin],
             fill(ffn_outs, 0) + [N.stream1] + fill(qkv_outs, 1),
-            weights=wts(g_names + d_names, 0) + wts(q_names, 1),
+            weights=wts((N.agu, N.gu, N.bg, N.bu) + d_names, 0) + wts((N.aqkv, N.qkv, N.bk, N.bv, N.bq), 1),
+            hold=N.bu,
             micros=16,
         )
         chunk_lr = Chunk(*pack_lr[:1], [pack_lr[1]], plain_ids)
@@ -1373,7 +1388,14 @@
         qkv_l = [N.attn_in, N.mid, N.rawq_low, N.rawkv_low, N.midgq, N.midgkv]
 
         open_kv(1)
-        phase([N.dkv1], [N.dq1])
+        phase([N.dkv1], [N.gmg1])
+        grads(
+            [N.la],
+            [N.ffn_in1, N.gmid1, N.gug1, N.gmg1, N.hidden1, N.dmid1, N.ffn_low1, N.dmg1, N.ho1, N.omid1, N.blow1, N.omg1],
+            8.6,
+        )
+        open_sum(N.la)
+        phase([N.dkv1, N.la], [N.dq1])
         call(
             N.q_back1,
             [stage_q_back(s, 1)],
@@ -1382,13 +1404,6 @@
             weights=wts((N.qkv, N.bq, N.aqkv), 1),
             micros=5.8,
         )
-        phase([N.dkv1], [N.gmg1], [N.agrad1])
-        grads(
-            [N.la],
-            [N.ffn_in1, N.gmid1, N.gug1, N.gmg1, N.hidden1, N.dmid1, N.ffn_low1, N.dmg1, N.ho1, N.omid1, N.blow1, N.omg1],
-            8.6,
-        )
-        open_sum(N.la)
         phase([N.la], [N.agrad1], [N.dkv1])
         close_kv(1)
         call(
@@ -1399,23 +1414,18 @@
             weights=wts((N.qkv, N.aqkv, N.bk, N.bv), 1),
             micros=6.2,
         )
-        phase([N.la], [N.sgrad1])
         call(
             N.ffn_back0,
             [stage_ffn_back(s, 0, N.sgrad1)],
             [N.norm, N.sgrad1, N.ffn_out0, N.gu0, N.middle0],
             [N.dnorm(0, 3), N.dnorm(0, 2)] + fill([N.ffn_low, N.dmg, N.gug, N.gmg, N.mgrad], 0),
-            weights=wts(d_names + (N.bg, N.bu, N.gu, N.agu), 0),
+            weights=wts((N.dnb, N.dnw, N.dna, N.bg, N.bu, N.gu, N.agu), 0),
+            hold=N.dnw,
             micros=14,
         )
         grads([N.g1, N.g2], fill([N.ffn_in, N.gug], 0) + [N.ffn_in1, N.gug1] + fill(qkv_l, 1), 9.7)
         open_sum(N.g1, N.g2)
-        phase([N.g1, N.g2, N.la], [N.dmg0, N.mgrad0])
-        grads(
-            [N.g3, N.g4],
-            fill([N.ffn_in, N.gmid, N.gug, N.gmg, N.hidden, N.dmid, N.ffn_low, N.dmg], 0) + [N.hidden1, N.ffn_low1],
-            8.5,
-        )
+        phase([N.g1, N.g2], [N.mgrad0], [N.la])
         call(
             N.out_back0,
             [stage_out_back(s, 0)],
@@ -1424,8 +1434,15 @@
             weights=wts(o_names, 0),
             micros=4.5,
         )
+        phase([N.g1, N.g2, N.la], [N.dmg0, N.hgrad0], [N.blow0])
+        grads(
+            [N.g3, N.g4],
+            fill([N.ffn_in, N.gmid, N.gug, N.gmg, N.hidden, N.dmid, N.ffn_low, N.dmg], 0) + [N.hidden1, N.ffn_low1],
+            8.5,
+        )
         open_sum(N.g3, N.g4)
-        phase([N.g1, N.g2, N.g3, N.g4, N.la], [N.hgrad0])
+        if fast:
+            v[N.hgrad0] = after(v[N.hgrad0], v[N.keep(N.g3)])
         call(
             N.attend_back0,
             [stage_attend_back(s, 0)],
@@ -1445,7 +1462,7 @@
             weights=wts((N.qkv, N.bq, N.aqkv), 0),
             micros=5.8,
         )
-        phase([N.dkv0, N.g1, N.g2], [N.rawq_low0])
+        phase([N.dkv0, N.g3, N.g4], [N.rawq_low0], [N.g1, N.g2])
         grads(
             [N.rb],
             fill([N.ho, N.omid, N.blow, N.omg, N.mid, N.rawq_low, N.attn_in, N.midgq], 0)
@@ -1453,8 +1470,10 @@
             7,
         )
         open_sum(N.rb)
-        phase([N.rb, N.g3, N.g4, N.g1, N.g2], [N.agrad0], [N.dkv0])
+        phase([N.g3, N.g4, N.rb, N.g1, N.g2], [N.agrad0, N.stream2], [N.dkv0])
         close_kv(0)
+        mixed = unsort_rows(s, rank, v[N.stream2])
+        v[N.mixed] = mixed
         call(
             N.kv_back0,
             [stage_kv_back(s, 0, N.stream0, N.sgrad0)],
@@ -1471,15 +1490,14 @@
             [] if fast else [N.gain_norm, N.gain_heads],
         )
         open_sum(N.ra)
-        phase([N.g3, N.g4, N.rb], [N.stream2, N.sgrad0], [N.g1, N.g2])
-        mixed = unsort_rows(s, rank, v[N.stream2])
         tokens_grad = unsort_rows(s, rank, v[N.sgrad0])
-        v[N.mixed], v[N.tokens_grad] = mixed, tokens_grad
-        phase([N.ra, N.g3, N.g4, N.rb, N.g1], [], [N.mixed, N.tokens_grad])
-        phase([N.ra, N.g3, N.g4])
+        v[N.tokens_grad] = tokens_grad
+        phase([N.g3, N.g4, N.ra, N.la], [], [N.mixed, N.tokens_grad, N.g1, N.g2])
+        phase([N.rb, N.g1, N.g2], [], [N.g3, N.g4, N.ra])
+        phase([N.ra, N.g3, N.g4], [], [N.rb, N.g1, N.g2])
+        phase([N.ra, N.rb, N.g3, N.g4, N.g1])
         phase([N.ra, N.rb, N.g3, N.g4, N.g2])
         phase([N.ra, N.rb])
-        phase([N.ra])
         for m in sums:
             assert m in (N.dkv0, N.dkv1) or not sums[m].steps
         finished = {m: sums[m].payload for m in plans if fast}
@@ -1512,15 +1530,17 @@
             made = [None] * len(plan)
             early = [i for i, (_, parts) in enumerate(plan) if all(part[1][0] in N.lg for part in parts)]
             late = [i for i in range(len(plan)) if i not in early]
-            for which, ends in ((early, []), (late, [((16, LANES), [((), N.ra, N.norm, 0)])])):
-                chosen = [plan[i] for i in which] + ends
+            ends = [
+                (norm_gain_table.shape, [((0, 4), N.ra, N.norm, 0)]),
+                (query_key_gains.shape, [((4, 2), N.ra, N.norm, 0)]),
+            ]
+            for which, last in ((early, []), (late, ends)):
+                chosen = [plan[i] for i in which] + last
                 used = sorted({part[1] for _, parts in chosen for part in parts})
                 results = unpack(s, chosen, {m: (*finished[m], layouts[m]) for m in used})
                 for i, value in zip(which, results):
                     made[i] = value
-            grads, gains = made, results[-1]
-            norm_grad = gains[:4, : norm_gain_table.shape[1]]
-            heads_grad = gains[4:6, : query_key_gains.shape[1]]
+            grads, (norm_grad, heads_grad) = made, results[-2:]
         else:
 
             def natural(name, l):

time: 538 us -> 515 us (0.957)
  waiting for transfers between devices: 172 us -> 159 us
  Pallas kernels: 177 us -> 171 us
    ppermute x67, waiting for transfers between devices: 124 us -> 105 us  [swap(): return lax.ppermute(value, 'own', [(i, i ^ bit) for i in range(sizes.n)])]
    ppermute x21, waiting for transfers between devices: 47.2 us -> 53.6 us  [along(): return lax.ppermute(value, 'dp', pairs)]
    pallas_call x16, Pallas kernels: 154 us -> 149 us  [run_kernel(): pl.pallas_call(kernel, name=name, out_shape=[jax.ShapeDtypeStruct(*outs[k...]
  transfers between devices with their start and end apart: 89 -> 89, of which waited for: 27 -> 35; matrix products, arithmetic and copies ran while one was open for 11% -> 12% of each run, Pallas kernels for 26% -> 27%
where the time goes in v2:
time: 515 us; the launch traced here: 507 us
  Pallas kernels  171 us (33%)
  waiting for transfers between devices  159 us (31%)
  starting transfers between devices  74.3 us (14%)
  other arithmetic  73.8 us (14%)
  between operations  16.9 us (3%)
  local copies, waits for them, and re-layouts  12.2 us (2%)
    pallas_call x16, Pallas kernels, run_kernel(): pl.pallas_call(kernel, name=name, out_shape=[jax.ShapeDtypeStruct(*outs[k...  149 us
    ppermute x67, waiting for transfers between devices, swap(): return lax.ppermute(value, 'own', [(i, i ^ bit) for i in range(sizes.n)])  105 us
    convert_element_type x36, other arithmetic, add(): return total.astype(BF)  56.2 us
    ppermute x21, waiting for transfers between devices, along(): return lax.ppermute(value, 'dp', pairs)  53.6 us
    ppermute x67, starting transfers between devices, swap(): return lax.ppermute(value, 'own', [(i, i ^ bit) for i in range(sizes.n)])  50.1 us
    ppermute x21, starting transfers between devices, along(): return lax.ppermute(value, 'dp', pairs)  24.1 us
  transfers between devices with their start and end apart: 89, of which 35 were waited for; matrix products, arithmetic and copies ran while one was open for 12% of the time, Pallas kernels for 27%

profile of v2, /device:TPU:0, one launch (start us, length us, event | category | flops | bytes accessed | tf_op | source)
XLA Modules:
  0.0 507.2 jit_solution(17885341982309484534)
XLA Ops:
  7.3 2.9 pack.6.refs_3_
  13.0 2.9 collective-permute-start
  27.5 4.1 collective-permute-done.refs_0_
  39.2 13.0 %collective-permute-done.1.refs_1_.refs_7_.refs_21_.refs_10_.refs_14_.refs_9_.refs_13_ = bf16[1840,128]{1,0:T(8,128)(2,1)S(1)} collective-permute-done((bf16[1840,128]{1,0:T(8,128)(2,1)}, bf16[1840,128]{1,0:T(8,128)(2,1)S(1)}, u32[]{:S(2)}, u32[]{:S(2)}) %collective-permute-start.1) | collective-permute-done | bytes 471072 | tf_op jit(solution)/shard_map/ppermute | solution.py:823
  53.3 15.4 %collective-permute-done.2.refs_6_.refs_20_.refs_9_.refs_13_.refs_8_.refs_12_ = bf16[1840,128]{1,0:T(8,128)(2,1)S(1)} collective-permute-done((bf16[1840,128]{1,0:T(8,128)(2,1)S(1)}, bf16[1840,128]{1,0:T(8,128)(2,1)S(1)}, u32[]{:S(2)}, u32[]{:S(2)}) %collective-permute-start.2) | collective-permute-done | bytes 471072 | tf_op jit(solution)/shard_map/ppermute | solution.py:823
  72.9 6.4 %qkv0.1 = (f32[16,640]{1,0:T(8,128)}, f32[16,256]{1,0:T(8,128)}, bf16[256,640]{1,0:T(8,128)(2,1)}, bf16[3,256,256]{2,1,0:T(8,128)(2,1)}, f32[5,256,256]{2,1,0:T(...) custom-call(s32[8]{0:T(128)} %stack.47.refs_0_.refs_1_.refs_2_, ...), custom_call_target="tpu_custom_call" | custom-call | flops 6500000 | tf_op jit(solution)/shard_map/qkv0/pallas_call | solution.py:179
  81.2 7.2 %collective-permute-done.15.refs_18_.refs_12_.refs_21_.refs_17_.refs_6_ = bf16[1920,128]{1,0:T(8,128)(2,1)S(1)} collective-permute-done((bf16[1920,128]{1,0:T(8,128)(2,1)}, bf16[1920,128]{1,0:T(8,128)(2,1)S(1)}, u32[]{:S(2)}, u32[]{:S(2)}) %collective-permute-start.15) | collective-permute-done | bytes 491552 | tf_op jit(solution)/shard_map/ppermute | solution.py:823
  90.7 3.2 collective-permute-done.7.refs_9_
  93.9 6.4 %collective-permute-done.9.refs_11_.refs_1_ = bf16[256,512]{1,0:T(8,128)(2,1)S(1)} collective-permute-done((bf16[256,512]{1,0:T(8,128)(2,1)}, bf16[256,512]{1,0:T(8,128)(2,1)S(1)}, u32[]{:S(2)}, u32[]{:S(2)}) %collective-permute-start.9) | collective-permute-done | bytes 262176 | tf_op jit(solution)/shard_map/ppermute | solution.py:823
  101.0 9.5 %collective-permute-done.8.refs_10_ = bf16[256,512]{1,0:T(8,128)(2,1)} collective-permute-done((bf16[256,512]{1,0:T(8,128)(2,1)}, bf16[256,512]{1,0:T(8,128)(2,1)}, u32[]{:S(2)}, u32[]{:S(2)}) %collective-permute-start.8) | collective-permute-done | bytes 262176 | tf_op jit(solution)/shard_map/ppermute | solution.py:823
  118.7 8.0 %attend0.1 = (f32[4,256,256]{2,1,0:T(8,128)}, f32[4,256,128]{2,1,0:T(8,128)}, bf16[4,256,256]{2,1,0:T(8,128)(2,1)}, bf16[256,256]{1,0:T(8,128)(2,1)}, f32[256,64...) custom-call(s32[4]{0:T(128)} %and_select_fusion.2.refs_0_, s32[8]{0:T(128)} %stack.47.refs_0_.refs_1_.refs_2_, ...), custom_call_target="tpu_custom_call" | custom-call | flops 11000000 | tf_op jit(solution)/shard_map/attend0/pallas_call | solution.py:179
  127.3 16.1 %ffn0.1 = (bf16[2,256,256]{2,1,0:T(8,128)(2,1)}, bf16[8,256,512]{2,1,0:T(8,128)(2,1)}, bf16[8,256,256]{2,1,0:T(8,128)(2,1)}, bf16[256,256]{1,0:T(8,128)(2,1)}, f...) custom-call(s32[8]{0:T(128)} %iota.50.refs_0_, ...), custom_call_target="tpu_custom_call" | custom-call | flops 16000000 | tf_op jit(solution)/shard_map/ffn0/pallas_call | solution.py:179
  144.3 2.8 collective-permute-start.26
  147.0 5.9 %collective-permute-done.24.refs_12_ = bf16[256,512]{1,0:T(8,128)(2,1)S(1)} collective-permute-done((bf16[256,512]{1,0:T(8,128)(2,1)}, bf16[256,512]{1,0:T(8,128)(2,1)S(1)}, u32[]{:S(2)}, u32[]{:S(2)}) %collective-permute-start.24) | collective-permute-done | bytes 262176 | tf_op jit(solution)/shard_map/ppermute | solution.py:823
  153.5 4.4 collective-permute-done.26.refs_14_
  163.8 29.6 %loop1.1 = (f32[256,640]{1,0:T(8,128)}, f32[256,640]{1,0:T(8,128)}, bf16[4,256,256]{2,1,0:T(8,128)(2,1)}, bf16[256,256]{1,0:T(8,128)(2,1)}, bf16[256,640]{1,0:T(...) custom-call(s32[4]{0:T(128)} %and_select_fusion.2.refs_0_, ...), custom_call_target="tpu_custom_call" | custom-call | flops 35000000 | tf_op jit(solution)/shard_map/loop1/pallas_call | solution.py:179
  194.2 6.5 %gradsla.1 = (bf16[4,2432,128]{2,1,0:T(8,128)(2,1)}, bf16[4,2432,128]{2,1,0:T(8,128)(2,1)}) custom-call(s32[2]{0:T(128)} %pad_add_fusion.refs_0_, bf16[256,640]{1,0:T(8,128)(2,1)} %get-tuple-element.214.refs_1_.refs_3_, bf16[2,256,256]{2,1,0:T(8,128)(2,1)} %get-tuple-element.215.refs_2_, bf16[16,256,256]{2,1,0:T(8,128)(2,1)} %get-tuple-element.216.refs_3_.refs_4_, ...), custom_call_target="tpu_custom_call" | custom-call | flops 8600000 | tf_op jit(solution)/shard_map/gradsla/pallas_call | solution.py:179
  205.9 5.9 %q_back1.1 = (bf16[4,256,256]{2,1,0:T(8,128)(2,1)}, bf16[256,256]{1,0:T(8,128)(2,1)}, f32[256,640]{1,0:T(8,128)}, f32[1,256]{1,0:T(1,128)}) custom-call(s32[8]{0:T(128)} %stack.47.refs_0_.refs_1_.refs_2_, s32[8]{0:T(128)} %stack.47.refs_0_.refs_1_.refs_2_, f32[256,128]{1,0:T(8,128)} %get-tuple-element.407.refs_2_.refs_7_.refs_1_, ...), custom_call_target="tpu_custom_call" | custom-call | flops 5800000 | tf_op jit(solution)/shard_map/q_back1/pallas_call | solution.py:179
  211.8 6.7 %collective-permute-done.37 = bf16[256,512]{1,0:T(8,128)(2,1)S(1)} collective-permute-done((bf16[256,512]{1,0:T(8,128)(2,1)}, bf16[256,512]{1,0:T(8,128)(2,1)S(1)}, u32[]{:S(2)}, u32[]{:S(2)}) %collective-permute-start.37) | collective-permute-done | bytes 262176 | tf_op jit(solution)/shard_map/ppermute | solution.py:823
  220.5 3.0 fusion.18
  226.9 6.2 %kv_back1.1 = (f32[1,256]{1,0:T(1,128)}, bf16[2,256,256]{2,1,0:T(8,128)(2,1)}, bf16[2,256,256]{2,1,0:T(8,128)(2,1)}, f32[1,640]{1,0:T(1,128)}, f32[256,640]{1,0:T(8,128)}) custom-call(s32[8]{0:T(128)} %stack.47.refs_0_.refs_1_.refs_2_, s32[8]{0:T(128)} %stack.47.refs_0_.refs_1_.refs_2_, f32[256,128]{1,0:T(8,128)} %get-tuple-element.407.refs_2_.refs_7_.refs_1_, ...), custom_call_target="tpu_custom_call" | custom-call | flops 6200000 | tf_op jit(solution)/shard_map/kv_back1/pallas_call | solution.py:179
  233.7 14.2 %ffn_back0.1 = (f32[1,640]{1,0:T(1,128)}, f32[1,640]{1,0:T(1,128)}, bf16[256,640]{1,0:T(8,128)(2,1)}, bf16[256,256]{1,0:T(8,128)(2,1)}, bf16[16,256,256]{2,1,0:T...) custom-call(s32[8]{0:T(128)} %iota.51.refs_0_, ...), custom_call_target="tpu_custom_call" | custom-call | flops 14000000 | tf_op jit(solution)/shard_map/ffn_back0/pallas_call | solution.py:179
  247.9 9.7 %gradsg1.1 = (bf16[4,1760,128]{2,1,0:T(8,128)(2,1)}, bf16[4,1760,128]{2,1,0:T(8,128)(2,1)}, bf16[4,1664,128]{2,1,0:T(8,128)(2,1)}, bf16[4,1664,128]{2,1,0:T(8,128)(2,1)}) custom-call(s32[2]{0:T(128)} %pad_add_fusion.refs_0_, bf16[256,640]{1,0:T(8,128)(2,1)} %get-tuple-element.197.refs_3_.refs_1_, bf16[16,256,256]{2,1,0:T(8,128)(2,1)} %get-tuple-element.241.refs_2_.refs_3_, ...), custom_call_target="tpu_custom_call" | custom-call | flops 9700000 | tf_op jit(solution)/shard_map/gradsg1/pallas_call | solution.py:179
  261.8 4.8 out_back0.1
  267.3 3.5 add_convert_fusion.4
  272.0 2.9 add_convert_fusion
  278.2 8.2 %gradsg3.1 = (bf16[4,1600,128]{2,1,0:T(8,128)(2,1)}, bf16[4,1600,128]{2,1,0:T(8,128)(2,1)}, bf16[4,1696,128]{2,1,0:T(8,128)(2,1)}, bf16[4,1696,128]{2,1,0:T(8,128)(2,1)}) custom-call(s32[2]{0:T(128)} %pad_add_fusion.refs_0_, bf16[256,640]{1,0:T(8,128)(2,1)} %get-tuple-element.197.refs_3_.refs_1_, bf16[2,256,256]{2,1,0:T(8,128)(2,1)} %get-tuple-element.200.refs_2_, ...), custom_call_target="tpu_custom_call" | custom-call | flops 8500000 | tf_op jit(solution)/shard_map/gradsg3/pallas_call | solution.py:179
  286.4 10.3 %attend_back0.1 = (f32[4,256,256]{2,1,0:T(8,128)}, bf16[4,256,512]{2,1,0:T(8,128)(2,1)}, bf16[4,256,512]{2,1,0:T(8,128)(2,1)}) custom-call(s32[4]{0:T(128)} %and_select_fusion.2.refs_0_, bf16[4,256,256]{2,1,0:T(8,128)(2,1)} %after.32.refs_1_, bf16[4,256,256]{2,1,0:T(8,128)(2,1)} %get-tuple-element.194.refs_3_.refs_2_, ...), custom_call_target="tpu_custom_call" | custom-call | flops 13000000 | tf_op jit(solution)/shard_map/attend_back0/pallas_call | solution.py:179
  303.7 5.7 %q_back0.1 = (bf16[4,256,256]{2,1,0:T(8,128)(2,1)}, bf16[256,256]{1,0:T(8,128)(2,1)}, f32[256,640]{1,0:T(8,128)}, f32[1,256]{1,0:T(1,128)}) custom-call(s32[8]{0:T(128)} %stack.47.refs_0_.refs_1_.refs_2_, f32[256,128]{1,0:T(8,128)} %get-tuple-element.407.refs_2_.refs_7_.refs_1_, f32[256,128]{1,0:T(8,128)} %get-tuple-element.406.refs_3_.refs_8_.refs_2_, ...), custom_call_target="tpu_custom_call" | custom-call | flops 5800000 | tf_op jit(solution)/shard_map/q_back0/pallas_call | solution.py:179
  309.4 3.3 collective-permute-done.50
  321.9 6.7 %gradsrb.1 = (bf16[4,2112,128]{2,1,0:T(8,128)(2,1)}, bf16[4,2112,128]{2,1,0:T(8,128)(2,1)}) custom-call(s32[2]{0:T(128)} %pad_add_fusion.refs_0_, bf16[4,256,256]{2,1,0:T(8,128)(2,1)} %get-tuple-element.289.refs_1_, bf16[256,256]{1,0:T(8,128)(2,1)} %get-tuple-element.290.refs_2_, bf16[256,640]{1,0:T(8,128)(2,1)} %get-tuple-element.266.refs_5_.refs_3_, ...), custom_call_target="tpu_custom_call" | custom-call | flops 7000000 | tf_op jit(solution)/shard_map/gradsrb/pallas_call | solution.py:179
  328.6 4.0 collective-permute-start.58
  335.1 3.1 add_convert_fusion.6
  338.2 2.9 add_convert_fusion.2
  347.2 6.2 %kv_back0.1 = (f32[1,256]{1,0:T(1,128)}, bf16[2,256,256]{2,1,0:T(8,128)(2,1)}, bf16[2,256,256]{2,1,0:T(8,128)(2,1)}, f32[1,640]{1,0:T(1,128)}, f32[256,640]{1,0:T(8,128)}) custom-call(s32[8]{0:T(128)} %stack.47.refs_0_.refs_1_.refs_2_, f32[256,128]{1,0:T(8,128)} %get-tuple-element.407.refs_2_.refs_7_.refs_1_, ...), custom_call_target="tpu_custom_call" | custom-call | flops 6200000 | tf_op jit(solution)/shard_map/kv_back0/pallas_call | solution.py:179
  357.7 3.9 gradsra.1
  365.1 2.9 collective-permute-done.57
  372.2 9.0 %collective-permute-done.62 = bf16[1600,128]{1,0:T(8,128)(2,1)S(1)} collective-permute-done((bf16[1600,128]{1,0:T(8,128)(2,1)}, bf16[1600,128]{1,0:T(8,128)(2,1)S(1)}, u32[]{:S(2)}, u32[]{:S(2)}) %collective-permute-start.62) | collective-permute-done | bytes 409632 | tf_op jit(solution)/shard_map/ppermute | solution.py:823
  386.2 2.8 fusion.23
  389.0 2.6 collective-permute-start.69
  395.4 10.8 %collective-permute-done.69 = bf16[832,128]{1,0:T(8,128)(2,1)S(1)} collective-permute-done((bf16[832,128]{1,0:T(8,128)(2,1)}, bf16[832,128]{1,0:T(8,128)(2,1)S(1)}, u32[]{:S(2)}, u32[]{:S(2)}) %collective-permute-start.69) | collective-permute-done | bytes 213024 | tf_op jit(solution)/shard_map/ppermute | solution.py:827
  412.0 3.5 collective-permute-done.66
  430.3 7.0 %collective-permute-done.73 = bf16[800,128]{1,0:T(8,128)(2,1)S(1)} collective-permute-done((bf16[800,128]{1,0:T(8,128)(2,1)}, bf16[800,128]{1,0:T(8,128)(2,1)S(1)}, u32[]{:S(2)}, u32[]{:S(2)}) %collective-permute-start.73) | collective-permute-done | bytes 204832 | tf_op jit(solution)/shard_map/ppermute | solution.py:827
  446.7 11.6 %collective-permute-done.78 = bf16[800,128]{1,0:T(8,128)(2,1)S(1)} collective-permute-done((bf16[800,128]{1,0:T(8,128)(2,1)}, bf16[800,128]{1,0:T(8,128)(2,1)S(1)}, u32[]{:S(2)}, u32[]{:S(2)}) %collective-permute-start.78) | collective-permute-done | bytes 204832 | tf_op jit(solution)/shard_map/ppermute | solution.py:827
  468.6 13.3 %collective-permute-done.86 = bf16[800,128]{1,0:T(8,128)(2,1)S(1)} collective-permute-done((bf16[800,128]{1,0:T(8,128)(2,1)}, bf16[800,128]{1,0:T(8,128)(2,1)S(1)}, u32[]{:S(2)}, u32[]{:S(2)}) %collective-permute-start.86) | collective-permute-done | bytes 204832 | tf_op jit(solution)/shard_map/ppermute | solution.py:827
  489.2 3.7 unpack.3
  492.9 2.7 collective-permute-done.84
  497.2 2.9 unpack.2
  (373 shorter events, 162.1 us)
Async XLA Ops:
  7.2 119.6 %all-gather.2.cloned.1.call-start = ((), (), s32[]{:S(2)}) async-start(), calls=%async_computation | async-start | bytes 13492224 | tf_op jit(solution)/shard_map/all_gather | solution.py:1111
  13.0 18.6 %collective-permute-start = (bf16[1840,128]{1,0:T(8,128)(2,1)}, bf16[1840,128]{1,0:T(8,128)(2,1)S(1)}, u32[]{:S(2)}, u32[]{:S(2)}) collective-permute-start(bf16[1840,128]{1,0:T(8,128)(2,1)} %pack.5.refs_4_.refs_18_.refs_7_.refs_11_.refs_6_.refs_10_), channel_id=1, source_target_pairs={{0,8},{4,12},{8,0},{12,4},{16,24},{20,28},{24,16},{28,20},{1,9},{5... | collective-permute-start | bytes 1413128 | tf_op jit(solution)/shard_map/ppermute | solution.py:823
  32.4 19.8 %collective-permute-start.1 = (bf16[1840,128]{1,0:T(8,128)(2,1)}, bf16[1840,128]{1,0:T(8,128)(2,1)S(1)}, u32[]{:S(2)}, u32[]{:S(2)}) collective-permute-start(bf16[1840,128]{1,0:T(8,128)(2,1)} %after.21.refs_1_.refs_5_.refs_19_.refs_8_.refs_12_.refs_7_.refs_11_), channel_id=1, source_target_pairs={{0,16},{4,20},{8,24},{12,28},{16,0},{20,4},{24,8},{28,12},{1,17},{... | collective-permute-start | bytes 1413128 | tf_op jit(solution)/shard_map/ppermute | solution.py:823
  33.7 35.0 %collective-permute-start.2 = (bf16[1840,128]{1,0:T(8,128)(2,1)S(1)}, bf16[1840,128]{1,0:T(8,128)(2,1)S(1)}, u32[]{:S(2)}, u32[]{:S(2)}) collective-permute-start(bf16[1840,128]{1,0:T(8,128)(2,1)S(1)} %copy-done.2), channel_id=1, source_target_pairs={{0,16},{4,20},{8,24},{12,28},{16,0},{20,4},{24,8},{28,12},{1,17},{... | collective-permute-start | bytes 1413128 | tf_op jit(solution)/shard_map/ppermute | solution.py:823
  34.7 34.0 %collective-permute-start.3 = (bf16[1840,128]{1,0:T(8,128)(2,1)S(1)}, bf16[1840,128]{1,0:T(8,128)(2,1)}, u32[]{:S(2)}, u32[]{:S(2)}) collective-permute-start(bf16[1840,128]{1,0:T(8,128)(2,1)S(1)} %copy-done.2), channel_id=1, source_target_pairs={{0,4},{4,0},{8,12},{12,8},{16,20},{20,16},{24,28},{28,24},{1,5},{5... | collective-permute-start | bytes 1413128 | tf_op jit(solution)/shard_map/ppermute | solution.py:823
  34.7 34.5 %collective-permute-start.4 = (bf16[1840,128]{1,0:T(8,128)(2,1)}, bf16[1840,128]{1,0:T(8,128)(2,1)}, u32[]{:S(2)}, u32[]{:S(2)}) collective-permute-start(bf16[1840,128]{1,0:T(8,128)(2,1)} %after.21.refs_1_.refs_5_.refs_19_.refs_8_.refs_12_.refs_7_.refs_11_), channel_id=1, source_target_pairs={{0,4},{4,0},{8,12},{12,8},{16,20},{20,16},{24,28},{28,24},{1,5},{5... | collective-permute-start | bytes 1413128 | tf_op jit(solution)/shard_map/ppermute | solution.py:823
  36.0 33.3 %collective-permute-start.14 = (bf16[1920,128]{1,0:T(8,128)(2,1)}, bf16[1920,128]{1,0:T(8,128)(2,1)S(1)}, u32[]{:S(2)}, u32[]{:S(2)}) collective-permute-start(bf16[1920,128]{1,0:T(8,128)(2,1)} %after.22.refs_1_), channel_id=1, source_target_pairs={{0,8},{4,12},{8,0},{12,4},{16,24},{20,28},{24,16},{28,20},{1,9},{5... | collective-permute-start | bytes 1474568 | tf_op jit(solution)/shard_map/ppermute | solution.py:823
  53.0 35.3 %collective-permute-start.15 = (bf16[1920,128]{1,0:T(8,128)(2,1)}, bf16[1920,128]{1,0:T(8,128)(2,1)S(1)}, u32[]{:S(2)}, u32[]{:S(2)}) collective-permute-start(bf16[1920,128]{1,0:T(8,128)(2,1)} %after.23.refs_2_), channel_id=1, source_target_pairs={{0,16},{4,20},{8,24},{12,28},{16,0},{20,4},{24,8},{28,12},{1,17},{... | collective-permute-start | bytes 1474568 | tf_op jit(solution)/shard_map/ppermute | solution.py:823
  68.7 21.1 %collective-permute-start.17 = (bf16[1920,128]{1,0:T(8,128)(2,1)S(1)}, bf16[1920,128]{1,0:T(8,128)(2,1)S(1)}, u32[]{:S(2)}, u32[]{:S(2)}) collective-permute-start(bf16[1920,128]{1,0:T(8,128)(2,1)S(1)} %copy-done), channel_id=1, source_target_pairs={{0,4},{4,0},{8,12},{12,8},{16,20},{20,16},{24,28},{28,24},{1,5},{5... | collective-permute-start | bytes 1474568 | tf_op jit(solution)/shard_map/ppermute | solution.py:823
  69.3 20.8 %collective-permute-start.18 = (bf16[1920,128]{1,0:T(8,128)(2,1)S(1)}, bf16[1920,128]{1,0:T(8,128)(2,1)S(1)}, u32[]{:S(2)}, u32[]{:S(2)}) collective-permute-start(bf16[1920,128]{1,0:T(8,128)(2,1)S(1)} %collective-permute-done.14.refs_17_.refs_11_.refs_20_.refs_16_.refs_5_), channel_id=1, source_target_pairs={{0,4},{4,0},{8,12},{12,8},{16,20},{20,16},{24,28},{28,24},{1,5},{5... | collective-permute-start | bytes 1474568 | tf_op jit(solution)/shard_map/ppermute | solution.py:823
  80.8 19.5 %collective-permute-start.9 = (bf16[256,512]{1,0:T(8,128)(2,1)}, bf16[256,512]{1,0:T(8,128)(2,1)S(1)}, u32[]{:S(2)}, u32[]{:S(2)}) collective-permute-start(bf16[256,512]{1,0:T(8,128)(2,1)} %get-tuple-element.196.refs_8_), channel_id=1, source_target_pairs={{0,24},{4,28},{8,16},{12,20},{16,8},{20,12},{24,0},{28,4},{1,25},{... | collective-permute-start | bytes 786440 | tf_op jit(solution)/shard_map/ppermute | solution.py:823
  88.3 23.2 %collective-permute-start.16 = (bf16[1920,128]{1,0:T(8,128)(2,1)S(1)}, bf16[1920,128]{1,0:T(8,128)(2,1)S(1)}, u32[]{:S(2)}, u32[]{:S(2)}) collective-permute-start(bf16[1920,128]{1,0:T(8,128)(2,1)S(1)} %collective-permute-done.15.refs_18_.refs_12_.refs_21_.refs_17_.refs_6_), channel_id=1, source_target_pairs={{0,8},{4,12},{8,0},{12,4},{16,24},{20,28},{24,16},{28,20},{1,9},{5... | collective-permute-start | bytes 1474568 | tf_op jit(solution)/shard_map/ppermute | solution.py:823
  89.8 24.2 %collective-permute-start.19 = (bf16[1920,128]{1,0:T(8,128)(2,1)S(1)}, bf16[1920,128]{1,0:T(8,128)(2,1)S(1)}, u32[]{:S(2)}, u32[]{:S(2)}) collective-permute-start(bf16[1920,128]{1,0:T(8,128)(2,1)S(1)} %collective-permute-done.15.refs_18_.refs_12_.refs_21_.refs_17_.refs_6_), channel_id=1, source_target_pairs={{0,4},{4,0},{8,12},{12,8},{16,20},{20,16},{24,28},{28,24},{1,5},{5... | collective-permute-start | bytes 1474568 | tf_op jit(solution)/shard_map/ppermute | solution.py:823
  90.1 20.4 %collective-permute-start.8 = (bf16[256,512]{1,0:T(8,128)(2,1)}, bf16[256,512]{1,0:T(8,128)(2,1)}, u32[]{:S(2)}, u32[]{:S(2)}) collective-permute-start(bf16[256,512]{1,0:T(8,128)(2,1)} %get-tuple-element.196.refs_8_), channel_id=1, source_target_pairs={{0,16},{4,20},{8,24},{12,28},{16,0},{20,4},{24,8},{28,12},{1,17},{... | collective-permute-start | bytes 786440 | tf_op jit(solution)/shard_map/ppermute | solution.py:823
  93.9 17.4 %collective-permute-start.10 = (bf16[256,512]{1,0:T(8,128)(2,1)}, bf16[256,512]{1,0:T(8,128)(2,1)S(1)}, u32[]{:S(2)}, u32[]{:S(2)}) collective-permute-start(bf16[256,512]{1,0:T(8,128)(2,1)} %get-tuple-element.196.refs_8_), channel_id=1, source_target_pairs={{0,4},{4,0},{8,12},{12,8},{16,20},{20,16},{24,28},{28,24},{1,5},{5... | collective-permute-start | bytes 786440 | tf_op jit(solution)/shard_map/ppermute | solution.py:823
  110.5 33.0 %collective-permute-start.21 = (bf16[2432,128]{1,0:T(8,128)(2,1)}, bf16[2432,128]{1,0:T(8,128)(2,1)}, u32[]{:S(2)}, u32[]{:S(2)}) collective-permute-start(bf16[2432,128]{1,0:T(8,128)(2,1)} %after.25.refs_0_), channel_id=1, source_target_pairs={{0,8},{4,12},{8,0},{12,4},{16,24},{20,28},{24,16},{28,20},{1,9},{5... | collective-permute-start | bytes 1867784 | tf_op jit(solution)/shard_map/ppermute | solution.py:823
  111.3 32.2 %collective-permute-start.22 = (bf16[2432,128]{1,0:T(8,128)(2,1)}, bf16[2432,128]{1,0:T(8,128)(2,1)}, u32[]{:S(2)}, u32[]{:S(2)}) collective-permute-start(bf16[2432,128]{1,0:T(8,128)(2,1)} %after.25.refs_0_), channel_id=1, source_target_pairs={{0,16},{4,20},{8,24},{12,28},{16,0},{20,4},{24,8},{28,12},{1,17},{... | collective-permute-start | bytes 1867784 | tf_op jit(solution)/shard_map/ppermute | solution.py:823
  111.6 31.9 %collective-permute-start.23 = (bf16[2432,128]{1,0:T(8,128)(2,1)}, bf16[2432,128]{1,0:T(8,128)(2,1)}, u32[]{:S(2)}, u32[]{:S(2)}) collective-permute-start(bf16[2432,128]{1,0:T(8,128)(2,1)} %after.25.refs_0_), channel_id=1, source_target_pairs={{0,24},{4,28},{8,16},{12,20},{16,8},{20,12},{24,0},{28,4},{1,25},{... | collective-permute-start | bytes 1867784 | tf_op jit(solution)/shard_map/ppermute | solution.py:823
  202.0 18.5 %collective-permute-start.39 = (bf16[4,2432,128]{2,1,0:T(8,128)(2,1)}, bf16[4,2432,128]{2,1,0:T(8,128)(2,1)}, u32[]{:S(2)}, u32[]{:S(2)}) collective-permute-start(bf16[4,2432,128]{2,1,0:T(8,128)(2,1)} %get-tuple-element.233), channel_id=1, source_target_pairs={{0,4},{4,0},{8,12},{12,8},{16,20},{20,16},{24,28},{28,24},{1,5},{5... | collective-permute-start | bytes 7471112 | tf_op jit(solution)/shard_map/ppermute | solution.py:823
  223.4 34.2 %collective-permute-start.40 = (bf16[2432,128]{1,0:T(8,128)(2,1)}, bf16[2432,128]{1,0:T(8,128)(2,1)S(1)}, u32[]{:S(2)}, u32[]{:S(2)}) collective-permute-start(bf16[2432,128]{1,0:T(8,128)(2,1)} %get-tuple-element.256), channel_id=1, source_target_pairs={{0,8},{4,12},{8,0},{12,4},{16,24},{20,28},{24,16},{28,20},{1,9},{5... | collective-permute-start | bytes 1867784 | tf_op jit(solution)/shard_map/ppermute | solution.py:823
  223.9 33.8 %collective-permute-start.41 = (bf16[2432,128]{1,0:T(8,128)(2,1)}, bf16[2432,128]{1,0:T(8,128)(2,1)}, u32[]{:S(2)}, u32[]{:S(2)}) collective-permute-start(bf16[2432,128]{1,0:T(8,128)(2,1)} %get-tuple-element.257), channel_id=1, source_target_pairs={{0,16},{4,20},{8,24},{12,28},{16,0},{20,4},{24,8},{28,12},{1,17},{... | collective-permute-start | bytes 1867784 | tf_op jit(solution)/shard_map/ppermute | solution.py:823
  225.2 33.3 %collective-permute-start.42 = (bf16[2432,128]{1,0:T(8,128)(2,1)}, bf16[2432,128]{1,0:T(8,128)(2,1)}, u32[]{:S(2)}, u32[]{:S(2)}) collective-permute-start(bf16[2432,128]{1,0:T(8,128)(2,1)} %get-tuple-element.258), channel_id=1, source_target_pairs={{0,24},{4,28},{8,16},{12,20},{16,8},{20,12},{24,0},{28,4},{1,25},{... | collective-permute-start | bytes 1867784 | tf_op jit(solution)/shard_map/ppermute | solution.py:823
  274.9 22.7 %collective-permute-start.46 = (bf16[2,1664,128]{2,1,0:T(8,128)(2,1)}, bf16[2,1664,128]{2,1,0:T(8,128)(2,1)}, u32[]{:S(2)}, u32[]{:S(2)}) collective-permute-start(bf16[2,1664,128]{2,1,0:T(8,128)(2,1)} %get-tuple-element.275), channel_id=1, source_target_pairs={{0,16},{4,20},{8,24},{12,28},{16,0},{20,4},{24,8},{28,12},{1,17},{... | collective-permute-start | bytes 2555912 | tf_op jit(solution)/shard_map/ppermute | solution.py:823
  275.7 21.1 %collective-permute-start.47 = (bf16[1216,128]{1,0:T(8,128)(2,1)}, bf16[1216,128]{1,0:T(8,128)(2,1)S(1)}, u32[]{:S(2)}, u32[]{:S(2)}) collective-permute-start(bf16[1216,128]{1,0:T(8,128)(2,1)} %get-tuple-element.276), channel_id=1, source_target_pairs={{0,1},{1,0},{2,3},{3,2},{4,5},{5,4},{6,7},{7,6},{8,9},{9,8},{10,11... | collective-permute-start | bytes 933896 | tf_op jit(solution)/shard_map/ppermute | solution.py:827
  277.1 22.3 %collective-permute-start.45 = (bf16[2,1760,128]{2,1,0:T(8,128)(2,1)}, bf16[2,1760,128]{2,1,0:T(8,128)(2,1)}, u32[]{:S(2)}, u32[]{:S(2)}) collective-permute-start(bf16[2,1760,128]{2,1,0:T(8,128)(2,1)} %get-tuple-element.274), channel_id=1, source_target_pairs={{0,8},{4,12},{8,0},{12,4},{16,24},{20,28},{24,16},{28,20},{1,9},{5... | collective-permute-start | bytes 2703368 | tf_op jit(solution)/shard_map/ppermute | solution.py:823
  317.9 17.2 %collective-permute-start.51 = (bf16[4,1600,128]{2,1,0:T(8,128)(2,1)}, bf16[4,1600,128]{2,1,0:T(8,128)(2,1)}, u32[]{:S(2)}, u32[]{:S(2)}) collective-permute-start(bf16[4,1600,128]{2,1,0:T(8,128)(2,1)} %get-tuple-element.286), channel_id=1, source_target_pairs={{0,4},{4,0},{8,12},{12,8},{16,20},{20,16},{24,28},{28,24},{1,5},{5... | collective-permute-start | bytes 4915208 | tf_op jit(solution)/shard_map/ppermute | solution.py:823
  317.9 20.3 %collective-permute-start.52 = (bf16[4,1696,128]{2,1,0:T(8,128)(2,1)}, bf16[4,1696,128]{2,1,0:T(8,128)(2,1)}, u32[]{:S(2)}, u32[]{:S(2)}) collective-permute-start(bf16[4,1696,128]{2,1,0:T(8,128)(2,1)} %get-tuple-element.288), channel_id=1, source_target_pairs={{0,4},{4,0},{8,12},{12,8},{16,20},{20,16},{24,28},{28,24},{1,5},{5... | collective-permute-start | bytes 5210120 | tf_op jit(solution)/shard_map/ppermute | solution.py:823
  328.6 16.6 %collective-permute-start.58 = (bf16[1216,128]{1,0:T(8,128)(2,1)S(1)}, bf16[1216,128]{1,0:T(8,128)(2,1)S(1)}, u32[]{:S(2)}, u32[]{:S(2)}) collective-permute-start(bf16[1216,128]{1,0:T(8,128)(2,1)S(1)} %copy-done.17), channel_id=1, source_target_pairs={{0,2},{2,0},{1,3},{3,1},{4,6},{6,4},{5,7},{7,5},{8,10},{10,8},{9,1... | collective-permute-start | bytes 933896 | tf_op jit(solution)/shard_map/ppermute | solution.py:827
  341.1 20.5 %collective-permute-start.60 = (bf16[832,128]{1,0:T(8,128)(2,1)}, bf16[832,128]{1,0:T(8,128)(2,1)S(1)}, u32[]{:S(2)}, u32[]{:S(2)}) collective-permute-start(bf16[832,128]{1,0:T(8,128)(2,1)} %get-tuple-element.325), channel_id=1, source_target_pairs={{0,1},{1,0},{2,3},{3,2},{4,5},{5,4},{6,7},{7,6},{8,9},{9,8},{10,11... | collective-permute-start | bytes 638984 | tf_op jit(solution)/shard_map/ppermute | solution.py:827
  341.6 21.6 %collective-permute-start.56 = (bf16[2,1600,128]{2,1,0:T(8,128)(2,1)}, bf16[2,1600,128]{2,1,0:T(8,128)(2,1)}, u32[]{:S(2)}, u32[]{:S(2)}) collective-permute-start(bf16[2,1600,128]{2,1,0:T(8,128)(2,1)} %get-tuple-element.320), channel_id=1, source_target_pairs={{0,8},{4,12},{8,0},{12,4},{16,24},{20,28},{24,16},{28,20},{1,9},{5... | collective-permute-start | bytes 2457608 | tf_op jit(solution)/shard_map/ppermute | solution.py:823
  346.0 40.3 %collective-permute-start.64 = (bf16[4,2112,128]{2,1,0:T(8,128)(2,1)}, bf16[4,2112,128]{2,1,0:T(8,128)(2,1)}, u32[]{:S(2)}, u32[]{:S(2)}) collective-permute-start(bf16[4,2112,128]{2,1,0:T(8,128)(2,1)} %get-tuple-element.330), channel_id=1, source_target_pairs={{0,4},{4,0},{8,12},{12,8},{16,20},{20,16},{24,28},{28,24},{1,5},{5... | collective-permute-start | bytes 6488072 | tf_op jit(solution)/shard_map/ppermute | solution.py:823
  346.0 16.4 %collective-permute-start.59 = (bf16[880,128]{1,0:T(8,128)(2,1)}, bf16[880,128]{1,0:T(8,128)(2,1)S(1)}, u32[]{:S(2)}, u32[]{:S(2)}) collective-permute-start(bf16[880,128]{1,0:T(8,128)(2,1)} %get-tuple-element.324), channel_id=1, source_target_pairs={{0,1},{1,0},{2,3},{3,2},{4,5},{5,4},{6,7},{7,6},{8,9},{9,8},{10,11... | collective-permute-start | bytes 675848 | tf_op jit(solution)/shard_map/ppermute | solution.py:827
  346.0 22.0 %collective-permute-start.57 = (bf16[2,1696,128]{2,1,0:T(8,128)(2,1)}, bf16[2,1696,128]{2,1,0:T(8,128)(2,1)}, u32[]{:S(2)}, u32[]{:S(2)}) collective-permute-start(bf16[2,1696,128]{2,1,0:T(8,128)(2,1)} %get-tuple-element.321), channel_id=1, source_target_pairs={{0,16},{4,20},{8,24},{12,28},{16,0},{20,4},{24,8},{28,12},{1,17},{... | collective-permute-start | bytes 2605064 | tf_op jit(solution)/shard_map/ppermute | solution.py:823
  389.0 17.2 %collective-permute-start.69 = (bf16[832,128]{1,0:T(8,128)(2,1)}, bf16[832,128]{1,0:T(8,128)(2,1)S(1)}, u32[]{:S(2)}, u32[]{:S(2)}) collective-permute-start(bf16[832,128]{1,0:T(8,128)(2,1)} %get-tuple-element.335), channel_id=1, source_target_pairs={{0,2},{2,0},{1,3},{3,1},{4,6},{6,4},{5,7},{7,5},{8,10},{10,8},{9,1... | collective-permute-start | bytes 638984 | tf_op jit(solution)/shard_map/ppermute | solution.py:827
  391.6 20.4 %collective-permute-start.65 = (bf16[2112,128]{1,0:T(8,128)(2,1)}, bf16[2112,128]{1,0:T(8,128)(2,1)S(1)}, u32[]{:S(2)}, u32[]{:S(2)}) collective-permute-start(bf16[2112,128]{1,0:T(8,128)(2,1)} %get-tuple-element.331), channel_id=1, source_target_pairs={{0,8},{4,12},{8,0},{12,4},{16,24},{20,28},{24,16},{28,20},{1,9},{5... | collective-permute-start | bytes 1622024 | tf_op jit(solution)/shard_map/ppermute | solution.py:823
  392.6 22.9 %collective-permute-start.66 = (bf16[2112,128]{1,0:T(8,128)(2,1)}, bf16[2112,128]{1,0:T(8,128)(2,1)S(1)}, u32[]{:S(2)}, u32[]{:S(2)}) collective-permute-start(bf16[2112,128]{1,0:T(8,128)(2,1)} %get-tuple-element.332), channel_id=1, source_target_pairs={{0,16},{4,20},{8,24},{12,28},{16,0},{20,4},{24,8},{28,12},{1,17},{... | collective-permute-start | bytes 1622024 | tf_op jit(solution)/shard_map/ppermute | solution.py:823
  394.0 22.6 %collective-permute-start.67 = (bf16[2112,128]{1,0:T(8,128)(2,1)}, bf16[2112,128]{1,0:T(8,128)(2,1)S(1)}, u32[]{:S(2)}, u32[]{:S(2)}) collective-permute-start(bf16[2112,128]{1,0:T(8,128)(2,1)} %get-tuple-element.333), channel_id=1, source_target_pairs={{0,24},{4,28},{8,16},{12,20},{16,8},{20,12},{24,0},{28,4},{1,25},{... | collective-permute-start | bytes 1622024 | tf_op jit(solution)/shard_map/ppermute | solution.py:823
  395.1 15.2 %collective-permute-start.68 = (bf16[880,128]{1,0:T(8,128)(2,1)}, bf16[880,128]{1,0:T(8,128)(2,1)S(1)}, u32[]{:S(2)}, u32[]{:S(2)}) collective-permute-start(bf16[880,128]{1,0:T(8,128)(2,1)} %get-tuple-element.334), channel_id=1, source_target_pairs={{0,2},{2,0},{1,3},{3,1},{4,6},{6,4},{5,7},{7,5},{8,10},{10,8},{9,1... | collective-permute-start | bytes 675848 | tf_op jit(solution)/shard_map/ppermute | solution.py:827
  422.5 17.6 %collective-permute-start.81 = (bf16[1216,128]{1,0:T(8,128)(2,1)S(1)}, bf16[1216,128]{1,0:T(8,128)(2,1)S(1)}, u32[]{:S(2)}, u32[]{:S(2)}) collective-permute-start(bf16[1216,128]{1,0:T(8,128)(2,1)S(1)} %copy-done.16), channel_id=1, source_target_pairs={{0,1},{1,0},{2,3},{3,2},{4,5},{5,4},{6,7},{7,6},{8,9},{9,8},{10,11... | collective-permute-start | bytes 933896 | tf_op jit(solution)/shard_map/ppermute | solution.py:827
  423.5 14.6 %collective-permute-start.74 = (bf16[848,128]{1,0:T(8,128)(2,1)}, bf16[848,128]{1,0:T(8,128)(2,1)S(1)}, u32[]{:S(2)}, u32[]{:S(2)}) collective-permute-start(bf16[848,128]{1,0:T(8,128)(2,1)} %get-tuple-element.340), channel_id=1, source_target_pairs={{0,1},{1,0},{2,3},{3,2},{4,5},{5,4},{6,7},{7,6},{8,9},{9,8},{10,11... | collective-permute-start | bytes 651272 | tf_op jit(solution)/shard_map/ppermute | solution.py:827
  441.0 18.0 %collective-permute-start.79 = (bf16[848,128]{1,0:T(8,128)(2,1)}, bf16[848,128]{1,0:T(8,128)(2,1)S(1)}, u32[]{:S(2)}, u32[]{:S(2)}) collective-permute-start(bf16[848,128]{1,0:T(8,128)(2,1)} %get-tuple-element.345), channel_id=1, source_target_pairs={{0,2},{2,0},{1,3},{3,1},{4,6},{6,4},{5,7},{7,5},{8,10},{10,8},{9,1... | collective-permute-start | bytes 651272 | tf_op jit(solution)/shard_map/ppermute | solution.py:827
  441.5 16.7 %collective-permute-start.78 = (bf16[800,128]{1,0:T(8,128)(2,1)}, bf16[800,128]{1,0:T(8,128)(2,1)S(1)}, u32[]{:S(2)}, u32[]{:S(2)}) collective-permute-start(bf16[800,128]{1,0:T(8,128)(2,1)} %get-tuple-element.344), channel_id=1, source_target_pairs={{0,2},{2,0},{1,3},{3,1},{4,6},{6,4},{5,7},{7,5},{8,10},{10,8},{9,1... | collective-permute-start | bytes 614408 | tf_op jit(solution)/shard_map/ppermute | solution.py:827
  444.0 16.1 %collective-permute-start.77 = (bf16[1056,128]{1,0:T(8,128)(2,1)}, bf16[1056,128]{1,0:T(8,128)(2,1)S(1)}, u32[]{:S(2)}, u32[]{:S(2)}) collective-permute-start(bf16[1056,128]{1,0:T(8,128)(2,1)} %get-tuple-element.343), channel_id=1, source_target_pairs={{0,1},{1,0},{2,3},{3,2},{4,5},{5,4},{6,7},{7,6},{8,9},{9,8},{10,11... | collective-permute-start | bytes 811016 | tf_op jit(solution)/shard_map/ppermute | solution.py:827
  444.7 17.7 %collective-permute-start.75 = (bf16[880,128]{1,0:T(8,128)(2,1)}, bf16[880,128]{1,0:T(8,128)(2,1)S(1)}, u32[]{:S(2)}, u32[]{:S(2)}) collective-permute-start(bf16[880,128]{1,0:T(8,128)(2,1)} %get-tuple-element.341), channel_id=1, source_target_pairs={{0,1},{1,0},{2,3},{3,2},{4,5},{5,4},{6,7},{7,6},{8,9},{9,8},{10,11... | collective-permute-start | bytes 675848 | tf_op jit(solution)/shard_map/ppermute | solution.py:827
  463.2 25.2 %collective-permute-start.87 = (bf16[848,128]{1,0:T(8,128)(2,1)}, bf16[848,128]{1,0:T(8,128)(2,1)S(1)}, u32[]{:S(2)}, u32[]{:S(2)}) collective-permute-start(bf16[848,128]{1,0:T(8,128)(2,1)} %get-tuple-element.355), channel_id=1, source_target_pairs={{0,1},{1,0},{2,3},{3,2},{4,5},{5,4},{6,7},{7,6},{8,9},{9,8},{10,11... | collective-permute-start | bytes 651272 | tf_op jit(solution)/shard_map/ppermute | solution.py:827
  463.4 18.6 %collective-permute-start.86 = (bf16[800,128]{1,0:T(8,128)(2,1)}, bf16[800,128]{1,0:T(8,128)(2,1)S(1)}, u32[]{:S(2)}, u32[]{:S(2)}) collective-permute-start(bf16[800,128]{1,0:T(8,128)(2,1)} %get-tuple-element.354), channel_id=1, source_target_pairs={{0,1},{1,0},{2,3},{3,2},{4,5},{5,4},{6,7},{7,6},{8,9},{9,8},{10,11... | collective-permute-start | bytes 614408 | tf_op jit(solution)/shard_map/ppermute | solution.py:827
  465.3 19.6 %collective-permute-start.80 = (bf16[832,128]{1,0:T(8,128)(2,1)}, bf16[832,128]{1,0:T(8,128)(2,1)S(1)}, u32[]{:S(2)}, u32[]{:S(2)}) collective-permute-start(bf16[832,128]{1,0:T(8,128)(2,1)} %get-tuple-element.346), channel_id=1, source_target_pairs={{0,1},{1,0},{2,3},{3,2},{4,5},{5,4},{6,7},{7,6},{8,9},{9,8},{10,11... | collective-permute-start | bytes 638984 | tf_op jit(solution)/shard_map/ppermute | solution.py:827
  465.4 20.2 %collective-permute-start.83 = (bf16[1056,128]{1,0:T(8,128)(2,1)}, bf16[1056,128]{1,0:T(8,128)(2,1)S(1)}, u32[]{:S(2)}, u32[]{:S(2)}) collective-permute-start(bf16[1056,128]{1,0:T(8,128)(2,1)} %get-tuple-element.349), channel_id=1, source_target_pairs={{0,2},{2,0},{1,3},{3,1},{4,6},{6,4},{5,7},{7,5},{8,10},{10,8},{9,1... | collective-permute-start | bytes 811016 | tf_op jit(solution)/shard_map/ppermute | solution.py:827
  (97 other events, 785.7 us)
Sparse Core Ops, SparseCore 0:
  10.3 107.7 all-gather.1

commit v3 on v2

--- a/solution.py
+++ b/solution.py
@@ -96,7 +96,8 @@
         return self.refs[N.w(name)]
 
 
-def run_kernel(sizes, name, stages, ins, outs, scratch=(), weights=(), smem=(), micros=0, hold=None):
+def run_kernel(sizes, name, stages, ins, outs, scratch=(), weights=(), smem=(), micros=0, hold=None, early=()):
+    early = dict(early)
     chunks = []
     for _, chunk in weights:
         if chunk not in chunks:
@@ -130,6 +131,10 @@
         for key in names_out + names_scratch:
             env.refs[key] = refs[position]
             position += 1
+        whole = {}
+        for key in early:
+            whole[key] = env.refs[key]
+            env.refs[key] = refs[len(refs) - 2 * len(early) + list(early).index(key)]
         of_chunk = {}
         start = 0
         for number, chunk in enumerate(chunks):
@@ -167,10 +172,18 @@
             env.pending[wname] = sem
             held = held or wname == hold
         env.ids = lambda chunk: env[N.ids(chunks.index(chunk))]
-        for stage in stages:
+        going = []
+        early_sems = dict(zip(early, refs[len(refs) - len(early) :]))
+        for number, stage in enumerate(stages):
             stage(env)
+            for key, last in early.items():
+                if last == number:
+                    going.append(pltpu.make_async_copy(env[key], whole[key], early_sems[key]))
+                    going[-1].start()
         for wname, _ in weights:
             env.w(wname)
+        for copy in going:
+            copy.wait()
 
     any_space = pl.BlockSpec(memory_space=pl.ANY)
     vmem = pl.BlockSpec(memory_space=pltpu.VMEM)
@@ -183,10 +196,12 @@
         in_specs=[pl.BlockSpec(memory_space=pltpu.SMEM)] * len(names_smem)
         + [vmem] * len(names_in)
         + [any_space] * len(pieces),
-        out_specs=[vmem] * len(names_out),
+        out_specs=[any_space if key in early else vmem for key in names_out],
         scratch_shapes=[pltpu.VMEM(*scratch[key]) for key in names_scratch]
         + [pltpu.VMEM(*shape) for shape in shapes]
-        + [pltpu.SemaphoreType.DMA] * len(weights),
+        + [pltpu.SemaphoreType.DMA] * len(weights)
+        + [pltpu.VMEM(*outs[key]) for key in early]
+        + [pltpu.SemaphoreType.DMA] * len(early),
         compiler_params=pltpu.CompilerParams(vmem_limit_bytes=VMEM_LIMIT),
         cost_estimate=pl.CostEstimate(flops=int(micros * PEAK), bytes_accessed=0, transcendentals=0),
     )(*smem.values(), *ins.values(), *pieces)
@@ -1191,7 +1206,7 @@
             for i in range(4):
                 shapes[N.dnorm(l, i)] = ((1, D), F32)
 
-        def call(name, stages, ins, outs, scratch=(), weights=(), smem=(), micros=0, hold=None):
+        def call(name, stages, ins, outs, scratch=(), weights=(), smem=(), micros=0, hold=None, early=()):
             made = run_kernel(
                 s,
                 name,
@@ -1203,6 +1218,7 @@
                 {m: v[m] for m in smem},
                 micros,
                 hold,
+                early,
             )
             v.update(made)
 
@@ -1257,27 +1273,22 @@
         out_outs = [N.att, N.lse, N.ho, N.omid, N.branch, N.middle, N.ffn_in]
         ffn_outs = [N.gmid, N.gu, N.hidden, N.dmid, N.ffn_out]
         call(
-            N.attend0,
-            [stage_attend(s, 0), stage_out(s, 0, N.stream0)],
-            [N.stream0, N.q0, N.norm] + att_ins + kv_names(0),
-            fill(out_outs, 0),
+            N.loop0,
+            [stage_attend(s, 0), stage_out(s, 0, N.stream0), stage_ffn(s, 0), stage_qkv(s, 1, N.stream1)],
+            [N.stream0, N.q0, N.norm, N.qkg, N.cos, N.sin] + att_ins + kv_names(0),
+            fill(out_outs + ffn_outs, 0) + [N.stream1] + fill(qkv_outs, 1),
             scratch=[N.o_acc, N.l_acc],
-            weights=wts(o_names, 0),
+            weights=wts(o_names + (N.agu, N.gu, N.bg, N.bu) + d_names, 0)
+            + wts((N.aqkv, N.qkv, N.bk, N.bv, N.bq), 1),
             smem=[N.first_block],
-            micros=11,
-        )
-        call(
-            N.ffn0,
-            [stage_ffn(s, 0), stage_qkv(s, 1, N.stream1)],
-            [N.ffn_in0, N.middle0, N.norm, N.qkg, N.cos, N.sin],
-            fill(ffn_outs, 0) + [N.stream1] + fill(qkv_outs, 1),
-            weights=wts((N.agu, N.gu, N.bg, N.bu) + d_names, 0) + wts((N.aqkv, N.qkv, N.bk, N.bv, N.bq), 1),
-            hold=N.bu,
-            micros=16,
+            micros=20,
+            early={N.att0: 0, N.lse0: 0, N.ho0: 1, N.branch0: 1, N.middle0: 1, N.gu0: 2, N.hidden0: 2, N.ffn_out0: 2}
+            if fast
+            else (),
         )
         chunk_lr = Chunk(*pack_lr[:1], [pack_lr[1]], plain_ids)
         if fast:
-            *here, v[N.kv1] = after_all(here + [v[N.kv1]], [])
+            here = list(after_all(here, [v[N.stream1]]))
             chunk_lr.pieces = here + [swap(s, piece, CORE) for piece in here]
         of_loop[1] |= {m: chunk_lr for m in lr_names}
         share_kv(1)
@@ -1306,6 +1317,7 @@
             weights=wts(o_names + g_names + d_names, 1),
             smem=[N.first_block],
             micros=35,
+            early={N.ho1: 1, N.hidden1: 2, N.stream2: 2, N.gug1: 3, N.mgrad1: 3} if fast else (),
         )
         if not fast:
             call(
@@ -1408,20 +1420,14 @@
         close_kv(1)
         call(
             N.kv_back1,
-            [stage_kv_back(s, 1, N.stream1, N.sgrad1)],
-            [N.cos, N.sin, N.qkg, N.norm, N.dkv, N.raw1, N.agrad1, N.stream1, N.mgrad1],
-            [N.dkg1, N.rawkv_low1, N.midgkv1, N.dnorm(1, 0), N.sgrad1],
-            weights=wts((N.qkv, N.aqkv, N.bk, N.bv), 1),
-            micros=6.2,
-        )
-        call(
-            N.ffn_back0,
-            [stage_ffn_back(s, 0, N.sgrad1)],
-            [N.norm, N.sgrad1, N.ffn_out0, N.gu0, N.middle0],
-            [N.dnorm(0, 3), N.dnorm(0, 2)] + fill([N.ffn_low, N.dmg, N.gug, N.gmg, N.mgrad], 0),
-            weights=wts((N.dnb, N.dnw, N.dna, N.bg, N.bu, N.gu, N.agu), 0),
-            hold=N.dnw,
-            micros=14,
+            [stage_kv_back(s, 1, N.stream1, N.sgrad1), stage_ffn_back(s, 0, N.sgrad1)],
+            [N.cos, N.sin, N.qkg, N.norm, N.dkv, N.raw1, N.agrad1, N.stream1, N.mgrad1]
+            + [N.ffn_out0, N.gu0, N.middle0],
+            [N.dkg1, N.rawkv_low1, N.midgkv1, N.dnorm(1, 0), N.dnorm(0, 3), N.dnorm(0, 2)]
+            + fill([N.ffn_low, N.dmg, N.gug, N.gmg, N.mgrad], 0),
+            scratch=[N.sgrad1],
+            weights=wts((N.qkv, N.aqkv, N.bk, N.bv), 1) + wts((N.dnb, N.dnw, N.dna, N.bg, N.bu, N.gu, N.agu), 0),
+            micros=17,
         )
         grads([N.g1, N.g2], fill([N.ffn_in, N.gug], 0) + [N.ffn_in1, N.gug1] + fill(qkv_l, 1), 9.7)
         open_sum(N.g1, N.g2)

time: 515 us -> 505 us (0.981)
  Pallas kernels: 171 us -> 162 us
    pallas_call x16 -> x14, Pallas kernels: 149 us -> 139 us  [run_kernel(): pl.pallas_call(kernel, name=name, out_shape=[jax.ShapeDtypeStruct(*outs[k...]
    unnamed x116 -> x120, local copies, waits for them, and re-layouts: 8.37 us -> 10.5 us
  transfers between devices with their start and end apart: 89 -> 89, of which waited for: 35 -> 32; matrix products, arithmetic and copies ran while one was open for 12% -> 12% of each run, Pallas kernels for 27% -> 26%
where the time goes in v3:
time: 505 us; the launch traced here: 497 us
  Pallas kernels  162 us (32%)
  waiting for transfers between devices  156 us (31%)
  starting transfers between devices  74.7 us (15%)
  other arithmetic  74.1 us (15%)
  between operations  16.8 us (3%)
  local copies, waits for them, and re-layouts  14.6 us (3%)
    pallas_call x14, Pallas kernels, run_kernel(): pl.pallas_call(kernel, name=name, out_shape=[jax.ShapeDtypeStruct(*outs[k...  139 us
    ppermute x67, waiting for transfers between devices, swap(): return lax.ppermute(value, 'own', [(i, i ^ bit) for i in range(sizes.n)])  104 us
    convert_element_type x36, other arithmetic, add(): return total.astype(BF)  56.4 us
    ppermute x67, starting transfers between devices, swap(): return lax.ppermute(value, 'own', [(i, i ^ bit) for i in range(sizes.n)])  52.2 us
    ppermute x21, waiting for transfers between devices, along(): return lax.ppermute(value, 'dp', pairs)  51.4 us
    ppermute x21, starting transfers between devices, along(): return lax.ppermute(value, 'dp', pairs)  22.5 us
    unnamed x120, local copies, waits for them, and re-layouts  10.5 us
  transfers between devices with their start and end apart: 89, of which 32 were waited for; matrix products, arithmetic and copies ran while one was open for 12% of the time, Pallas kernels for 26%

profile of v3, /device:TPU:0, one launch (start us, length us, event | category | flops | bytes accessed | tf_op | source)
XLA Modules:
  0.0 497.5 jit_solution(15159994628780524190)
XLA Ops:
  7.3 2.9 pack.6.refs_3_
  13.0 2.9 collective-permute-start
  23.8 2.5 sort_rows.1
  27.5 4.1 collective-permute-done.refs_0_
  38.9 13.3 %collective-permute-done.1.refs_1_.refs_7_.refs_33_.refs_10_.refs_18_.refs_9_.refs_13_ = bf16[1840,128]{1,0:T(8,128)(2,1)S(1)} collective-permute-done((bf16[1840,128]{1,0:T(8,128)(2,1)}, bf16[1840,128]{1,0:T(8,128)(2,1)S(1)}, u32[]{:S(2)}, u32[]{:S(2)}) %collective-permute-start.1) | collective-permute-done | bytes 471072 | tf_op jit(solution)/shard_map/ppermute | solution.py:838
  53.3 15.3 %collective-permute-done.2.refs_6_.refs_32_.refs_9_.refs_17_.refs_8_.refs_12_ = bf16[1840,128]{1,0:T(8,128)(2,1)S(1)} collective-permute-done((bf16[1840,128]{1,0:T(8,128)(2,1)S(1)}, bf16[1840,128]{1,0:T(8,128)(2,1)S(1)}, u32[]{:S(2)}, u32[]{:S(2)}) %collective-permute-start.2) | collective-permute-done | bytes 471072 | tf_op jit(solution)/shard_map/ppermute | solution.py:838
  73.4 6.4 %qkv0.1 = (f32[16,640]{1,0:T(8,128)}, f32[16,256]{1,0:T(8,128)}, bf16[256,640]{1,0:T(8,128)(2,1)}, bf16[3,256,256]{2,1,0:T(8,128)(2,1)}, f32[5,256,256]{2,1,0:T(...) custom-call(s32[8]{0:T(128)} %stack.47.refs_0_.refs_1_.refs_3_.refs_2_, ...), custom_call_target="tpu_custom_call" | custom-call | flops 6500000 | tf_op jit(solution)/shard_map/qkv0/pallas_call | solution.py:192
  81.3 11.2 %collective-permute-done.15.refs_23_.refs_21_.refs_17_.refs_25_.refs_6_ = bf16[1920,128]{1,0:T(8,128)(2,1)} collective-permute-done((bf16[1920,128]{1,0:T(8,128)(2,1)}, bf16[1920,128]{1,0:T(8,128)(2,1)}, u32[]{:S(2)}, u32[]{:S(2)}) %collective-permute-start.15) | collective-permute-done | bytes 491552 | tf_op jit(solution)/shard_map/ppermute | solution.py:838
  92.5 2.6 collective-permute-start.16
  97.0 13.0 %collective-permute-done.7.refs_14_.refs_9_ = bf16[256,512]{1,0:T(8,128)(2,1)S(1)} collective-permute-done((bf16[256,512]{1,0:T(8,128)(2,1)}, bf16[256,512]{1,0:T(8,128)(2,1)S(1)}, u32[]{:S(2)}, u32[]{:S(2)}) %collective-permute-start.7) | collective-permute-done | bytes 262176 | tf_op jit(solution)/shard_map/ppermute | solution.py:838
  119.0 18.8 %loop0.1 = (f32[4,256,256]{2,1,0:T(8,128)}, f32[4,256,128]{2,1,0:T(8,128)}, bf16[4,256,256]{2,1,0:T(8,128)(2,1)}, bf16[256,256]{1,0:T(8,128)(2,1)}, f32[256,640]...) custom-call(s32[4]{0:T(128)} %and_select_fusion.2.refs_0_, ...), custom_call_target="tpu_custom_call" | custom-call | flops 20000000 | tf_op jit(solution)/shard_map/loop0/pallas_call | solution.py:192
  141.4 5.9 %collective-permute-done.21.refs_12_ = bf16[256,512]{1,0:T(8,128)(2,1)} collective-permute-done((bf16[256,512]{1,0:T(8,128)(2,1)}, bf16[256,512]{1,0:T(8,128)(2,1)}, u32[]{:S(2)}, u32[]{:S(2)}) %collective-permute-start.21) | collective-permute-done | bytes 262176 | tf_op jit(solution)/shard_map/ppermute | solution.py:838
  148.7 4.5 collective-permute-done.22.refs_13_
  155.6 2.7 collective-permute-done.26.refs_17_
  161.6 28.3 %loop1.1 = (f32[256,640]{1,0:T(8,128)}, f32[256,640]{1,0:T(8,128)}, bf16[4,256,256]{2,1,0:T(8,128)(2,1)}, bf16[256,256]{1,0:T(8,128)(2,1)}, bf16[256,640]{1,0:T(...) custom-call(s32[4]{0:T(128)} %and_select_fusion.2.refs_0_, ...), custom_call_target="tpu_custom_call" | custom-call | flops 35000000 | tf_op jit(solution)/shard_map/loop1/pallas_call | solution.py:192
  191.0 6.5 %gradsla.1 = (bf16[4,2432,128]{2,1,0:T(8,128)(2,1)}, bf16[4,2432,128]{2,1,0:T(8,128)(2,1)}) custom-call(s32[2]{0:T(128)} %pad_add_fusion.refs_0_, bf16[256,640]{1,0:T(8,128)(2,1)} %get-tuple-element.210.refs_1_.refs_3_, bf16[2,256,256]{2,1,0:T(8,128)(2,1)} %get-tuple-element.211.refs_2_, bf16[16,256,256]{2,1,0:T(8,128)(2,1)} %get-tuple-element.212.refs_3_.refs_4_, ...), custom_call_target="tpu_custom_call" | custom-call | flops 8600000 | tf_op jit(solution)/shard_map/gradsla/pallas_call | solution.py:192
  199.9 2.6 collective-permute-start.38
  202.5 5.9 %q_back1.1 = (bf16[4,256,256]{2,1,0:T(8,128)(2,1)}, bf16[256,256]{1,0:T(8,128)(2,1)}, f32[256,640]{1,0:T(8,128)}, f32[1,256]{1,0:T(1,128)}) custom-call(s32[8]{0:T(128)} %stack.47.refs_0_.refs_1_.refs_3_.refs_2_, s32[8]{0:T(128)} %stack.47.refs_0_.refs_1_.refs_3_.refs_2_, f32[256,128]{1,0:T(8,128)} %get-tuple-element.403.refs_2_.refs_8_.refs_3_.refs_1_, ...), custom_call_target="tpu_custom_call" | custom-call | flops 5800000 | tf_op jit(solution)/shard_map/q_back1/pallas_call | solution.py:192
  208.4 5.6 %collective-permute-done.37 = bf16[256,512]{1,0:T(8,128)(2,1)S(1)} collective-permute-done((bf16[256,512]{1,0:T(8,128)(2,1)}, bf16[256,512]{1,0:T(8,128)(2,1)S(1)}, u32[]{:S(2)}, u32[]{:S(2)}) %collective-permute-start.37) | collective-permute-done | bytes 262176 | tf_op jit(solution)/shard_map/ppermute | solution.py:838
  215.9 3.1 fusion.18
  223.0 17.3 %kv_back1.1 = (f32[1,256]{1,0:T(1,128)}, bf16[2,256,256]{2,1,0:T(8,128)(2,1)}, bf16[2,256,256]{2,1,0:T(8,128)(2,1)}, f32[1,640]{1,0:T(1,128)}, f32[1,640]{1,0:T(...) custom-call(s32[8]{0:T(128)} %stack.47.refs_0_.refs_1_.refs_3_.refs_, ...), custom_call_target="tpu_custom_call" | custom-call | flops 17000000 | tf_op jit(solution)/shard_map/kv_back1/pallas_call | solution.py:192
  240.3 9.7 %gradsg1.1 = (bf16[4,1760,128]{2,1,0:T(8,128)(2,1)}, bf16[4,1760,128]{2,1,0:T(8,128)(2,1)}, bf16[4,1664,128]{2,1,0:T(8,128)(2,1)}, bf16[4,1664,128]{2,1,0:T(8,128)(2,1)}) custom-call(s32[2]{0:T(128)} %pad_add_fusion.refs_0_, bf16[256,640]{1,0:T(8,128)(2,1)} %get-tuple-element.196.refs_1_, bf16[16,256,256]{2,1,0:T(8,128)(2,1)} %get-tuple-element.237.refs_2_.refs_3_, ...), custom_call_target="tpu_custom_call" | custom-call | flops 9700000 | tf_op jit(solution)/shard_map/gradsg1/pallas_call | solution.py:192
  254.1 4.8 out_back0.1
  259.6 3.5 add_convert_fusion.4
  264.4 2.9 add_convert_fusion
  269.4 8.2 %gradsg3.1 = (bf16[4,1600,128]{2,1,0:T(8,128)(2,1)}, bf16[4,1600,128]{2,1,0:T(8,128)(2,1)}, bf16[4,1696,128]{2,1,0:T(8,128)(2,1)}, bf16[4,1696,128]{2,1,0:T(8,128)(2,1)}) custom-call(s32[2]{0:T(128)} %pad_add_fusion.refs_0_, bf16[256,640]{1,0:T(8,128)(2,1)} %get-tuple-element.196.refs_1_, bf16[2,256,256]{2,1,0:T(8,128)(2,1)} %get-tuple-element.197.refs_2_, ...), custom_call_target="tpu_custom_call" | custom-call | flops 8500000 | tf_op jit(solution)/shard_map/gradsg3/pallas_call | solution.py:192
  277.6 10.3 %attend_back0.1 = (f32[4,256,256]{2,1,0:T(8,128)}, bf16[4,256,512]{2,1,0:T(8,128)(2,1)}, bf16[4,256,512]{2,1,0:T(8,128)(2,1)}) custom-call(s32[4]{0:T(128)} %and_select_fusion.2.refs_0_, bf16[4,256,256]{2,1,0:T(8,128)(2,1)} %after.32.refs_1_, bf16[4,256,256]{2,1,0:T(8,128)(2,1)} %get-tuple-element.192.refs_5_.refs_2_, ...), custom_call_target="tpu_custom_call" | custom-call | flops 13000000 | tf_op jit(solution)/shard_map/attend_back0/pallas_call | solution.py:192
  294.9 5.7 %q_back0.1 = (bf16[4,256,256]{2,1,0:T(8,128)(2,1)}, bf16[256,256]{1,0:T(8,128)(2,1)}, f32[256,640]{1,0:T(8,128)}, f32[1,256]{1,0:T(1,128)}) custom-call(s32[8]{0:T(128)} %stack.47.refs_0_.refs_1_.refs_3_.refs_2_, f32[256,128]{1,0:T(8,128)} %get-tuple-element.403.refs_2_.refs_8_.refs_3_.refs_1_, ...), custom_call_target="tpu_custom_call" | custom-call | flops 5800000 | tf_op jit(solution)/shard_map/q_back0/pallas_call | solution.py:192
  300.6 3.3 collective-permute-done.50
  313.1 6.7 %gradsrb.1 = (bf16[4,2112,128]{2,1,0:T(8,128)(2,1)}, bf16[4,2112,128]{2,1,0:T(8,128)(2,1)}) custom-call(s32[2]{0:T(128)} %pad_add_fusion.refs_0_, bf16[4,256,256]{2,1,0:T(8,128)(2,1)} %get-tuple-element.285.refs_1_, bf16[256,256]{1,0:T(8,128)(2,1)} %get-tuple-element.286.refs_2_, bf16[256,640]{1,0:T(8,128)(2,1)} %get-tuple-element.262.refs_5_.refs_3_, ...), custom_call_target="tpu_custom_call" | custom-call | flops 7000000 | tf_op jit(solution)/shard_map/gradsrb/pallas_call | solution.py:192
  326.5 3.1 add_convert_fusion.6
  329.6 2.9 add_convert_fusion.2
  338.2 6.2 %kv_back0.1 = (f32[1,256]{1,0:T(1,128)}, bf16[2,256,256]{2,1,0:T(8,128)(2,1)}, bf16[2,256,256]{2,1,0:T(8,128)(2,1)}, f32[1,640]{1,0:T(1,128)}, f32[256,640]{1,0:T(8,128)}) custom-call(s32[8]{0:T(128)} %stack.47.refs_0_.refs_1_.refs_3_.refs_2_, f32[256,128]{1,0:T(8,128)} %get-tuple-element.403.refs_2_.refs_8_.refs_3_.refs_1_, ...), custom_call_target="tpu_custom_call" | custom-call | flops 6200000 | tf_op jit(solution)/shard_map/kv_back0/pallas_call | solution.py:192
  348.7 3.9 gradsra.1
  356.0 2.8 collective-permute-done.57
  363.0 9.0 %collective-permute-done.62 = bf16[1600,128]{1,0:T(8,128)(2,1)S(1)} collective-permute-done((bf16[1600,128]{1,0:T(8,128)(2,1)}, bf16[1600,128]{1,0:T(8,128)(2,1)S(1)}, u32[]{:S(2)}, u32[]{:S(2)}) %collective-permute-start.62) | collective-permute-done | bytes 409632 | tf_op jit(solution)/shard_map/ppermute | solution.py:838
  377.1 2.8 fusion.23
  379.9 2.5 collective-permute-start.69
  386.3 10.8 %collective-permute-done.69 = bf16[832,128]{1,0:T(8,128)(2,1)S(1)} collective-permute-done((bf16[832,128]{1,0:T(8,128)(2,1)}, bf16[832,128]{1,0:T(8,128)(2,1)S(1)}, u32[]{:S(2)}, u32[]{:S(2)}) %collective-permute-start.69) | collective-permute-done | bytes 213024 | tf_op jit(solution)/shard_map/ppermute | solution.py:842
  398.7 2.5 collective-permute-done.68
  402.9 4.6 collective-permute-done.66
  420.9 7.4 %collective-permute-done.73 = bf16[800,128]{1,0:T(8,128)(2,1)S(1)} collective-permute-done((bf16[800,128]{1,0:T(8,128)(2,1)}, bf16[800,128]{1,0:T(8,128)(2,1)S(1)}, u32[]{:S(2)}, u32[]{:S(2)}) %collective-permute-start.73) | collective-permute-done | bytes 204832 | tf_op jit(solution)/shard_map/ppermute | solution.py:842
  436.6 2.5 collective-permute-done.76
  439.8 8.4 %collective-permute-done.78 = bf16[800,128]{1,0:T(8,128)(2,1)S(1)} collective-permute-done((bf16[800,128]{1,0:T(8,128)(2,1)}, bf16[800,128]{1,0:T(8,128)(2,1)S(1)}, u32[]{:S(2)}, u32[]{:S(2)}) %collective-permute-start.78) | collective-permute-done | bytes 204832 | tf_op jit(solution)/shard_map/ppermute | solution.py:842
  459.5 12.6 %collective-permute-done.86 = bf16[800,128]{1,0:T(8,128)(2,1)S(1)} collective-permute-done((bf16[800,128]{1,0:T(8,128)(2,1)}, bf16[800,128]{1,0:T(8,128)(2,1)S(1)}, u32[]{:S(2)}, u32[]{:S(2)}) %collective-permute-start.86) | collective-permute-done | bytes 204832 | tf_op jit(solution)/shard_map/ppermute | solution.py:842
  479.5 3.7 unpack.3
  483.1 2.7 collective-permute-done.84
  487.5 2.9 unpack.2
  (375 shorter events, 159.1 us)
Async XLA Ops:
  7.2 111.3 %all-gather.2.cloned.1.call-start = ((), (), s32[]{:S(2)}) async-start(), calls=%async_computation | async-start | bytes 13492224 | tf_op jit(solution)/shard_map/all_gather | solution.py:1126
  13.0 18.6 %collective-permute-start = (bf16[1840,128]{1,0:T(8,128)(2,1)}, bf16[1840,128]{1,0:T(8,128)(2,1)S(1)}, u32[]{:S(2)}, u32[]{:S(2)}) collective-permute-start(bf16[1840,128]{1,0:T(8,128)(2,1)} %pack.5.refs_4_.refs_30_.refs_7_.refs_15_.refs_6_.refs_10_), channel_id=1, source_target_pairs={{0,8},{4,12},{8,0},{12,4},{16,24},{20,28},{24,16},{28,20},{1,9},{5... | collective-permute-start | bytes 1413128 | tf_op jit(solution)/shard_map/ppermute | solution.py:838
  32.4 19.8 %collective-permute-start.1 = (bf16[1840,128]{1,0:T(8,128)(2,1)}, bf16[1840,128]{1,0:T(8,128)(2,1)S(1)}, u32[]{:S(2)}, u32[]{:S(2)}) collective-permute-start(bf16[1840,128]{1,0:T(8,128)(2,1)} %after.21.refs_1_.refs_5_.refs_31_.refs_8_.refs_16_.refs_7_.refs_11_), channel_id=1, source_target_pairs={{0,16},{4,20},{8,24},{12,28},{16,0},{20,4},{24,8},{28,12},{1,17},{... | collective-permute-start | bytes 1413128 | tf_op jit(solution)/shard_map/ppermute | solution.py:838
  33.7 34.8 %collective-permute-start.2 = (bf16[1840,128]{1,0:T(8,128)(2,1)S(1)}, bf16[1840,128]{1,0:T(8,128)(2,1)S(1)}, u32[]{:S(2)}, u32[]{:S(2)}) collective-permute-start(bf16[1840,128]{1,0:T(8,128)(2,1)S(1)} %copy-done.3), channel_id=1, source_target_pairs={{0,16},{4,20},{8,24},{12,28},{16,0},{20,4},{24,8},{28,12},{1,17},{... | collective-permute-start | bytes 1413128 | tf_op jit(solution)/shard_map/ppermute | solution.py:838
  34.8 33.8 %collective-permute-start.3 = (bf16[1840,128]{1,0:T(8,128)(2,1)S(1)}, bf16[1840,128]{1,0:T(8,128)(2,1)S(1)}, u32[]{:S(2)}, u32[]{:S(2)}) collective-permute-start(bf16[1840,128]{1,0:T(8,128)(2,1)S(1)} %copy-done.3), channel_id=1, source_target_pairs={{0,4},{4,0},{8,12},{12,8},{16,20},{20,16},{24,28},{28,24},{1,5},{5... | collective-permute-start | bytes 1413128 | tf_op jit(solution)/shard_map/ppermute | solution.py:838
  35.5 33.6 %collective-permute-start.14 = (bf16[1920,128]{1,0:T(8,128)(2,1)}, bf16[1920,128]{1,0:T(8,128)(2,1)}, u32[]{:S(2)}, u32[]{:S(2)}) collective-permute-start(bf16[1920,128]{1,0:T(8,128)(2,1)} %after.22.refs_1_), channel_id=1, source_target_pairs={{0,8},{4,12},{8,0},{12,4},{16,24},{20,28},{24,16},{28,20},{1,9},{5... | collective-permute-start | bytes 1474568 | tf_op jit(solution)/shard_map/ppermute | solution.py:838
  37.9 31.1 %collective-permute-start.4 = (bf16[1840,128]{1,0:T(8,128)(2,1)S(1)}, bf16[1840,128]{1,0:T(8,128)(2,1)S(1)}, u32[]{:S(2)}, u32[]{:S(2)}) collective-permute-start(bf16[1840,128]{1,0:T(8,128)(2,1)S(1)} %copy-done.2), channel_id=1, source_target_pairs={{0,4},{4,0},{8,12},{12,8},{16,20},{20,16},{24,28},{28,24},{1,5},{5... | collective-permute-start | bytes 1413128 | tf_op jit(solution)/shard_map/ppermute | solution.py:838
  53.0 39.5 %collective-permute-start.15 = (bf16[1920,128]{1,0:T(8,128)(2,1)}, bf16[1920,128]{1,0:T(8,128)(2,1)}, u32[]{:S(2)}, u32[]{:S(2)}) collective-permute-start(bf16[1920,128]{1,0:T(8,128)(2,1)} %after.23.refs_2_), channel_id=1, source_target_pairs={{0,16},{4,20},{8,24},{12,28},{16,0},{20,4},{24,8},{28,12},{1,17},{... | collective-permute-start | bytes 1474568 | tf_op jit(solution)/shard_map/ppermute | solution.py:838
  69.1 26.3 %collective-permute-start.17 = (bf16[1920,128]{1,0:T(8,128)(2,1)S(1)}, bf16[1920,128]{1,0:T(8,128)(2,1)}, u32[]{:S(2)}, u32[]{:S(2)}) collective-permute-start(bf16[1920,128]{1,0:T(8,128)(2,1)S(1)} %copy-done), channel_id=1, source_target_pairs={{0,4},{4,0},{8,12},{12,8},{16,20},{20,16},{24,28},{28,24},{1,5},{5... | collective-permute-start | bytes 1474568 | tf_op jit(solution)/shard_map/ppermute | solution.py:838
  69.2 26.3 %collective-permute-start.18 = (bf16[1920,128]{1,0:T(8,128)(2,1)}, bf16[1920,128]{1,0:T(8,128)(2,1)}, u32[]{:S(2)}, u32[]{:S(2)}) collective-permute-start(bf16[1920,128]{1,0:T(8,128)(2,1)} %collective-permute-done.14.refs_22_.refs_20_.refs_16_.refs_24_.refs_5_), channel_id=1, source_target_pairs={{0,4},{4,0},{8,12},{12,8},{16,20},{20,16},{24,28},{28,24},{1,5},{5... | collective-permute-start | bytes 1474568 | tf_op jit(solution)/shard_map/ppermute | solution.py:838
  79.8 16.4 %collective-permute-start.9 = (bf16[256,512]{1,0:T(8,128)(2,1)}, bf16[256,512]{1,0:T(8,128)(2,1)S(1)}, u32[]{:S(2)}, u32[]{:S(2)}) collective-permute-start(bf16[256,512]{1,0:T(8,128)(2,1)} %get-tuple-element.195.refs_13_.refs_8_), channel_id=1, source_target_pairs={{0,24},{4,28},{8,16},{12,20},{16,8},{20,12},{24,0},{28,4},{1,25},{... | collective-permute-start | bytes 786440 | tf_op jit(solution)/shard_map/ppermute | solution.py:838
  92.5 19.4 %collective-permute-start.16 = (bf16[1920,128]{1,0:T(8,128)(2,1)}, bf16[1920,128]{1,0:T(8,128)(2,1)S(1)}, u32[]{:S(2)}, u32[]{:S(2)}) collective-permute-start(bf16[1920,128]{1,0:T(8,128)(2,1)} %collective-permute-done.15.refs_23_.refs_21_.refs_17_.refs_25_.refs_6_), channel_id=1, source_target_pairs={{0,8},{4,12},{8,0},{12,4},{16,24},{20,28},{24,16},{28,20},{1,9},{5... | collective-permute-start | bytes 1474568 | tf_op jit(solution)/shard_map/ppermute | solution.py:838
  95.1 17.4 %collective-permute-start.19 = (bf16[1920,128]{1,0:T(8,128)(2,1)}, bf16[1920,128]{1,0:T(8,128)(2,1)S(1)}, u32[]{:S(2)}, u32[]{:S(2)}) collective-permute-start(bf16[1920,128]{1,0:T(8,128)(2,1)} %collective-permute-done.15.refs_23_.refs_21_.refs_17_.refs_25_.refs_6_), channel_id=1, source_target_pairs={{0,4},{4,0},{8,12},{12,8},{16,20},{20,16},{24,28},{28,24},{1,5},{5... | collective-permute-start | bytes 1474568 | tf_op jit(solution)/shard_map/ppermute | solution.py:838
  95.3 14.7 %collective-permute-start.7 = (bf16[256,512]{1,0:T(8,128)(2,1)}, bf16[256,512]{1,0:T(8,128)(2,1)S(1)}, u32[]{:S(2)}, u32[]{:S(2)}) collective-permute-start(bf16[256,512]{1,0:T(8,128)(2,1)} %get-tuple-element.195.refs_13_.refs_8_), channel_id=1, source_target_pairs={{0,8},{4,12},{8,0},{12,4},{16,24},{20,28},{24,16},{28,20},{1,9},{5... | collective-permute-start | bytes 786440 | tf_op jit(solution)/shard_map/ppermute | solution.py:838
  95.4 14.9 %collective-permute-start.8 = (bf16[256,512]{1,0:T(8,128)(2,1)}, bf16[256,512]{1,0:T(8,128)(2,1)S(1)}, u32[]{:S(2)}, u32[]{:S(2)}) collective-permute-start(bf16[256,512]{1,0:T(8,128)(2,1)} %get-tuple-element.195.refs_13_.refs_8_), channel_id=1, source_target_pairs={{0,16},{4,20},{8,24},{12,28},{16,0},{20,4},{24,8},{28,12},{1,17},{... | collective-permute-start | bytes 786440 | tf_op jit(solution)/shard_map/ppermute | solution.py:838
  96.3 15.6 %collective-permute-start.10 = (bf16[256,512]{1,0:T(8,128)(2,1)}, bf16[256,512]{1,0:T(8,128)(2,1)S(1)}, u32[]{:S(2)}, u32[]{:S(2)}) collective-permute-start(bf16[256,512]{1,0:T(8,128)(2,1)} %get-tuple-element.195.refs_13_.refs_8_), channel_id=1, source_target_pairs={{0,4},{4,0},{8,12},{12,8},{16,20},{20,16},{24,28},{28,24},{1,5},{5... | collective-permute-start | bytes 786440 | tf_op jit(solution)/shard_map/ppermute | solution.py:838
  110.0 29.4 %collective-permute-start.28 = (bf16[2432,128]{1,0:T(8,128)(2,1)}, bf16[2432,128]{1,0:T(8,128)(2,1)S(1)}, u32[]{:S(2)}, u32[]{:S(2)}) collective-permute-start(bf16[2432,128]{1,0:T(8,128)(2,1)} %after.25.refs_0_), channel_id=1, source_target_pairs={{0,8},{4,12},{8,0},{12,4},{16,24},{20,28},{24,16},{28,20},{1,9},{5... | collective-permute-start | bytes 1867784 | tf_op jit(solution)/shard_map/ppermute | solution.py:838
  110.4 31.1 %collective-permute-start.29 = (bf16[2432,128]{1,0:T(8,128)(2,1)}, bf16[2432,128]{1,0:T(8,128)(2,1)S(1)}, u32[]{:S(2)}, u32[]{:S(2)}) collective-permute-start(bf16[2432,128]{1,0:T(8,128)(2,1)} %after.25.refs_0_), channel_id=1, source_target_pairs={{0,16},{4,20},{8,24},{12,28},{16,0},{20,4},{24,8},{28,12},{1,17},{... | collective-permute-start | bytes 1867784 | tf_op jit(solution)/shard_map/ppermute | solution.py:838
  115.4 32.0 %collective-permute-start.30 = (bf16[2432,128]{1,0:T(8,128)(2,1)}, bf16[2432,128]{1,0:T(8,128)(2,1)S(1)}, u32[]{:S(2)}, u32[]{:S(2)}) collective-permute-start(bf16[2432,128]{1,0:T(8,128)(2,1)} %after.25.refs_0_), channel_id=1, source_target_pairs={{0,24},{4,28},{8,16},{12,20},{16,8},{20,12},{24,0},{28,4},{1,25},{... | collective-permute-start | bytes 1867784 | tf_op jit(solution)/shard_map/ppermute | solution.py:838
  198.8 17.1 %collective-permute-start.39 = (bf16[4,2432,128]{2,1,0:T(8,128)(2,1)}, bf16[4,2432,128]{2,1,0:T(8,128)(2,1)}, u32[]{:S(2)}, u32[]{:S(2)}) collective-permute-start(bf16[4,2432,128]{2,1,0:T(8,128)(2,1)} %get-tuple-element.229), channel_id=1, source_target_pairs={{0,4},{4,0},{8,12},{12,8},{16,20},{20,16},{24,28},{28,24},{1,5},{5... | collective-permute-start | bytes 7471112 | tf_op jit(solution)/shard_map/ppermute | solution.py:838
  218.9 31.1 %collective-permute-start.40 = (bf16[2432,128]{1,0:T(8,128)(2,1)}, bf16[2432,128]{1,0:T(8,128)(2,1)S(1)}, u32[]{:S(2)}, u32[]{:S(2)}) collective-permute-start(bf16[2432,128]{1,0:T(8,128)(2,1)} %get-tuple-element.252), channel_id=1, source_target_pairs={{0,8},{4,12},{8,0},{12,4},{16,24},{20,28},{24,16},{28,20},{1,9},{5... | collective-permute-start | bytes 1867784 | tf_op jit(solution)/shard_map/ppermute | solution.py:838
  220.0 30.0 %collective-permute-start.41 = (bf16[2432,128]{1,0:T(8,128)(2,1)}, bf16[2432,128]{1,0:T(8,128)(2,1)}, u32[]{:S(2)}, u32[]{:S(2)}) collective-permute-start(bf16[2432,128]{1,0:T(8,128)(2,1)} %get-tuple-element.253), channel_id=1, source_target_pairs={{0,16},{4,20},{8,24},{12,28},{16,0},{20,4},{24,8},{28,12},{1,17},{... | collective-permute-start | bytes 1867784 | tf_op jit(solution)/shard_map/ppermute | solution.py:838
  220.7 30.2 %collective-permute-start.42 = (bf16[2432,128]{1,0:T(8,128)(2,1)}, bf16[2432,128]{1,0:T(8,128)(2,1)}, u32[]{:S(2)}, u32[]{:S(2)}) collective-permute-start(bf16[2432,128]{1,0:T(8,128)(2,1)} %get-tuple-element.254), channel_id=1, source_target_pairs={{0,24},{4,28},{8,16},{12,20},{16,8},{20,12},{24,0},{28,4},{1,25},{... | collective-permute-start | bytes 1867784 | tf_op jit(solution)/shard_map/ppermute | solution.py:838
  267.2 21.5 %collective-permute-start.46 = (bf16[2,1664,128]{2,1,0:T(8,128)(2,1)}, bf16[2,1664,128]{2,1,0:T(8,128)(2,1)}, u32[]{:S(2)}, u32[]{:S(2)}) collective-permute-start(bf16[2,1664,128]{2,1,0:T(8,128)(2,1)} %get-tuple-element.271), channel_id=1, source_target_pairs={{0,16},{4,20},{8,24},{12,28},{16,0},{20,4},{24,8},{28,12},{1,17},{... | collective-permute-start | bytes 2555912 | tf_op jit(solution)/shard_map/ppermute | solution.py:838
  268.1 19.8 %collective-permute-start.47 = (bf16[1216,128]{1,0:T(8,128)(2,1)}, bf16[1216,128]{1,0:T(8,128)(2,1)S(1)}, u32[]{:S(2)}, u32[]{:S(2)}) collective-permute-start(bf16[1216,128]{1,0:T(8,128)(2,1)} %get-tuple-element.272), channel_id=1, source_target_pairs={{0,1},{1,0},{2,3},{3,2},{4,5},{5,4},{6,7},{7,6},{8,9},{9,8},{10,11... | collective-permute-start | bytes 933896 | tf_op jit(solution)/shard_map/ppermute | solution.py:842
  268.5 22.1 %collective-permute-start.45 = (bf16[2,1760,128]{2,1,0:T(8,128)(2,1)}, bf16[2,1760,128]{2,1,0:T(8,128)(2,1)}, u32[]{:S(2)}, u32[]{:S(2)}) collective-permute-start(bf16[2,1760,128]{2,1,0:T(8,128)(2,1)} %get-tuple-element.270), channel_id=1, source_target_pairs={{0,8},{4,12},{8,0},{12,4},{16,24},{20,28},{24,16},{28,20},{1,9},{5... | collective-permute-start | bytes 2703368 | tf_op jit(solution)/shard_map/ppermute | solution.py:838
  309.1 17.4 %collective-permute-start.51 = (bf16[4,1600,128]{2,1,0:T(8,128)(2,1)}, bf16[4,1600,128]{2,1,0:T(8,128)(2,1)}, u32[]{:S(2)}, u32[]{:S(2)}) collective-permute-start(bf16[4,1600,128]{2,1,0:T(8,128)(2,1)} %get-tuple-element.282), channel_id=1, source_target_pairs={{0,4},{4,0},{8,12},{12,8},{16,20},{20,16},{24,28},{28,24},{1,5},{5... | collective-permute-start | bytes 4915208 | tf_op jit(solution)/shard_map/ppermute | solution.py:838
  309.1 20.6 %collective-permute-start.52 = (bf16[4,1696,128]{2,1,0:T(8,128)(2,1)}, bf16[4,1696,128]{2,1,0:T(8,128)(2,1)}, u32[]{:S(2)}, u32[]{:S(2)}) collective-permute-start(bf16[4,1696,128]{2,1,0:T(8,128)(2,1)} %get-tuple-element.284), channel_id=1, source_target_pairs={{0,4},{4,0},{8,12},{12,8},{16,20},{20,16},{24,28},{28,24},{1,5},{5... | collective-permute-start | bytes 5210120 | tf_op jit(solution)/shard_map/ppermute | solution.py:838
  319.8 16.2 %collective-permute-start.58 = (bf16[1216,128]{1,0:T(8,128)(2,1)S(1)}, bf16[1216,128]{1,0:T(8,128)(2,1)S(1)}, u32[]{:S(2)}, u32[]{:S(2)}) collective-permute-start(bf16[1216,128]{1,0:T(8,128)(2,1)S(1)} %copy-done.18), channel_id=1, source_target_pairs={{0,2},{2,0},{1,3},{3,1},{4,6},{6,4},{5,7},{7,5},{8,10},{10,8},{9,1... | collective-permute-start | bytes 933896 | tf_op jit(solution)/shard_map/ppermute | solution.py:842
  332.5 20.1 %collective-permute-start.60 = (bf16[832,128]{1,0:T(8,128)(2,1)}, bf16[832,128]{1,0:T(8,128)(2,1)S(1)}, u32[]{:S(2)}, u32[]{:S(2)}) collective-permute-start(bf16[832,128]{1,0:T(8,128)(2,1)} %get-tuple-element.321), channel_id=1, source_target_pairs={{0,1},{1,0},{2,3},{3,2},{4,5},{5,4},{6,7},{7,6},{8,9},{9,8},{10,11... | collective-permute-start | bytes 638984 | tf_op jit(solution)/shard_map/ppermute | solution.py:842
  333.0 21.2 %collective-permute-start.56 = (bf16[2,1600,128]{2,1,0:T(8,128)(2,1)}, bf16[2,1600,128]{2,1,0:T(8,128)(2,1)}, u32[]{:S(2)}, u32[]{:S(2)}) collective-permute-start(bf16[2,1600,128]{2,1,0:T(8,128)(2,1)} %get-tuple-element.316), channel_id=1, source_target_pairs={{0,8},{4,12},{8,0},{12,4},{16,24},{20,28},{24,16},{28,20},{1,9},{5... | collective-permute-start | bytes 2457608 | tf_op jit(solution)/shard_map/ppermute | solution.py:838
  336.8 40.3 %collective-permute-start.64 = (bf16[4,2112,128]{2,1,0:T(8,128)(2,1)}, bf16[4,2112,128]{2,1,0:T(8,128)(2,1)}, u32[]{:S(2)}, u32[]{:S(2)}) collective-permute-start(bf16[4,2112,128]{2,1,0:T(8,128)(2,1)} %get-tuple-element.326), channel_id=1, source_target_pairs={{0,4},{4,0},{8,12},{12,8},{16,20},{20,16},{24,28},{28,24},{1,5},{5... | collective-permute-start | bytes 6488072 | tf_op jit(solution)/shard_map/ppermute | solution.py:838
  336.8 16.6 %collective-permute-start.59 = (bf16[880,128]{1,0:T(8,128)(2,1)}, bf16[880,128]{1,0:T(8,128)(2,1)S(1)}, u32[]{:S(2)}, u32[]{:S(2)}) collective-permute-start(bf16[880,128]{1,0:T(8,128)(2,1)} %get-tuple-element.320), channel_id=1, source_target_pairs={{0,1},{1,0},{2,3},{3,2},{4,5},{5,4},{6,7},{7,6},{8,9},{9,8},{10,11... | collective-permute-start | bytes 675848 | tf_op jit(solution)/shard_map/ppermute | solution.py:842
  336.8 22.0 %collective-permute-start.57 = (bf16[2,1696,128]{2,1,0:T(8,128)(2,1)}, bf16[2,1696,128]{2,1,0:T(8,128)(2,1)}, u32[]{:S(2)}, u32[]{:S(2)}) collective-permute-start(bf16[2,1696,128]{2,1,0:T(8,128)(2,1)} %get-tuple-element.317), channel_id=1, source_target_pairs={{0,16},{4,20},{8,24},{12,28},{16,0},{20,4},{24,8},{28,12},{1,17},{... | collective-permute-start | bytes 2605064 | tf_op jit(solution)/shard_map/ppermute | solution.py:838
  379.9 17.2 %collective-permute-start.69 = (bf16[832,128]{1,0:T(8,128)(2,1)}, bf16[832,128]{1,0:T(8,128)(2,1)S(1)}, u32[]{:S(2)}, u32[]{:S(2)}) collective-permute-start(bf16[832,128]{1,0:T(8,128)(2,1)} %get-tuple-element.331), channel_id=1, source_target_pairs={{0,2},{2,0},{1,3},{3,1},{4,6},{6,4},{5,7},{7,5},{8,10},{10,8},{9,1... | collective-permute-start | bytes 638984 | tf_op jit(solution)/shard_map/ppermute | solution.py:842
  382.3 20.5 %collective-permute-start.65 = (bf16[2112,128]{1,0:T(8,128)(2,1)}, bf16[2112,128]{1,0:T(8,128)(2,1)S(1)}, u32[]{:S(2)}, u32[]{:S(2)}) collective-permute-start(bf16[2112,128]{1,0:T(8,128)(2,1)} %get-tuple-element.327), channel_id=1, source_target_pairs={{0,8},{4,12},{8,0},{12,4},{16,24},{20,28},{24,16},{28,20},{1,9},{5... | collective-permute-start | bytes 1622024 | tf_op jit(solution)/shard_map/ppermute | solution.py:838
  383.5 23.9 %collective-permute-start.66 = (bf16[2112,128]{1,0:T(8,128)(2,1)}, bf16[2112,128]{1,0:T(8,128)(2,1)S(1)}, u32[]{:S(2)}, u32[]{:S(2)}) collective-permute-start(bf16[2112,128]{1,0:T(8,128)(2,1)} %get-tuple-element.328), channel_id=1, source_target_pairs={{0,16},{4,20},{8,24},{12,28},{16,0},{20,4},{24,8},{28,12},{1,17},{... | collective-permute-start | bytes 1622024 | tf_op jit(solution)/shard_map/ppermute | solution.py:838
  384.1 23.4 %collective-permute-start.67 = (bf16[2112,128]{1,0:T(8,128)(2,1)}, bf16[2112,128]{1,0:T(8,128)(2,1)S(1)}, u32[]{:S(2)}, u32[]{:S(2)}) collective-permute-start(bf16[2112,128]{1,0:T(8,128)(2,1)} %get-tuple-element.329), channel_id=1, source_target_pairs={{0,24},{4,28},{8,16},{12,20},{16,8},{20,12},{24,0},{28,4},{1,25},{... | collective-permute-start | bytes 1622024 | tf_op jit(solution)/shard_map/ppermute | solution.py:838
  385.8 15.3 %collective-permute-start.68 = (bf16[880,128]{1,0:T(8,128)(2,1)}, bf16[880,128]{1,0:T(8,128)(2,1)S(1)}, u32[]{:S(2)}, u32[]{:S(2)}) collective-permute-start(bf16[880,128]{1,0:T(8,128)(2,1)} %get-tuple-element.330), channel_id=1, source_target_pairs={{0,2},{2,0},{1,3},{3,1},{4,6},{6,4},{5,7},{7,5},{8,10},{10,8},{9,1... | collective-permute-start | bytes 675848 | tf_op jit(solution)/shard_map/ppermute | solution.py:842
  413.4 17.3 %collective-permute-start.81 = (bf16[1216,128]{1,0:T(8,128)(2,1)S(1)}, bf16[1216,128]{1,0:T(8,128)(2,1)S(1)}, u32[]{:S(2)}, u32[]{:S(2)}) collective-permute-start(bf16[1216,128]{1,0:T(8,128)(2,1)S(1)} %copy-done.17), channel_id=1, source_target_pairs={{0,1},{1,0},{2,3},{3,2},{4,5},{5,4},{6,7},{7,6},{8,9},{9,8},{10,11... | collective-permute-start | bytes 933896 | tf_op jit(solution)/shard_map/ppermute | solution.py:842
  431.7 17.3 %collective-permute-start.79 = (bf16[848,128]{1,0:T(8,128)(2,1)}, bf16[848,128]{1,0:T(8,128)(2,1)S(1)}, u32[]{:S(2)}, u32[]{:S(2)}) collective-permute-start(bf16[848,128]{1,0:T(8,128)(2,1)} %get-tuple-element.341), channel_id=1, source_target_pairs={{0,2},{2,0},{1,3},{3,1},{4,6},{6,4},{5,7},{7,5},{8,10},{10,8},{9,1... | collective-permute-start | bytes 651272 | tf_op jit(solution)/shard_map/ppermute | solution.py:842
  432.5 15.7 %collective-permute-start.78 = (bf16[800,128]{1,0:T(8,128)(2,1)}, bf16[800,128]{1,0:T(8,128)(2,1)S(1)}, u32[]{:S(2)}, u32[]{:S(2)}) collective-permute-start(bf16[800,128]{1,0:T(8,128)(2,1)} %get-tuple-element.340), channel_id=1, source_target_pairs={{0,2},{2,0},{1,3},{3,1},{4,6},{6,4},{5,7},{7,5},{8,10},{10,8},{9,1... | collective-permute-start | bytes 614408 | tf_op jit(solution)/shard_map/ppermute | solution.py:842
  434.6 15.3 %collective-permute-start.77 = (bf16[1056,128]{1,0:T(8,128)(2,1)}, bf16[1056,128]{1,0:T(8,128)(2,1)S(1)}, u32[]{:S(2)}, u32[]{:S(2)}) collective-permute-start(bf16[1056,128]{1,0:T(8,128)(2,1)} %get-tuple-element.339), channel_id=1, source_target_pairs={{0,1},{1,0},{2,3},{3,2},{4,5},{5,4},{6,7},{7,6},{8,9},{9,8},{10,11... | collective-permute-start | bytes 811016 | tf_op jit(solution)/shard_map/ppermute | solution.py:842
  435.7 16.6 %collective-permute-start.75 = (bf16[880,128]{1,0:T(8,128)(2,1)}, bf16[880,128]{1,0:T(8,128)(2,1)S(1)}, u32[]{:S(2)}, u32[]{:S(2)}) collective-permute-start(bf16[880,128]{1,0:T(8,128)(2,1)} %get-tuple-element.337), channel_id=1, source_target_pairs={{0,1},{1,0},{2,3},{3,2},{4,5},{5,4},{6,7},{7,6},{8,9},{9,8},{10,11... | collective-permute-start | bytes 675848 | tf_op jit(solution)/shard_map/ppermute | solution.py:842
  453.1 25.5 %collective-permute-start.87 = (bf16[848,128]{1,0:T(8,128)(2,1)}, bf16[848,128]{1,0:T(8,128)(2,1)S(1)}, u32[]{:S(2)}, u32[]{:S(2)}) collective-permute-start(bf16[848,128]{1,0:T(8,128)(2,1)} %get-tuple-element.351), channel_id=1, source_target_pairs={{0,1},{1,0},{2,3},{3,2},{4,5},{5,4},{6,7},{7,6},{8,9},{9,8},{10,11... | collective-permute-start | bytes 651272 | tf_op jit(solution)/shard_map/ppermute | solution.py:842
  454.4 17.7 %collective-permute-start.86 = (bf16[800,128]{1,0:T(8,128)(2,1)}, bf16[800,128]{1,0:T(8,128)(2,1)S(1)}, u32[]{:S(2)}, u32[]{:S(2)}) collective-permute-start(bf16[800,128]{1,0:T(8,128)(2,1)} %get-tuple-element.350), channel_id=1, source_target_pairs={{0,1},{1,0},{2,3},{3,2},{4,5},{5,4},{6,7},{7,6},{8,9},{9,8},{10,11... | collective-permute-start | bytes 614408 | tf_op jit(solution)/shard_map/ppermute | solution.py:842
  455.1 19.9 %collective-permute-start.80 = (bf16[832,128]{1,0:T(8,128)(2,1)}, bf16[832,128]{1,0:T(8,128)(2,1)S(1)}, u32[]{:S(2)}, u32[]{:S(2)}) collective-permute-start(bf16[832,128]{1,0:T(8,128)(2,1)} %get-tuple-element.342), channel_id=1, source_target_pairs={{0,1},{1,0},{2,3},{3,2},{4,5},{5,4},{6,7},{7,6},{8,9},{9,8},{10,11... | collective-permute-start | bytes 638984 | tf_op jit(solution)/shard_map/ppermute | solution.py:842
  456.4 19.5 %collective-permute-start.83 = (bf16[1056,128]{1,0:T(8,128)(2,1)}, bf16[1056,128]{1,0:T(8,128)(2,1)S(1)}, u32[]{:S(2)}, u32[]{:S(2)}) collective-permute-start(bf16[1056,128]{1,0:T(8,128)(2,1)} %get-tuple-element.345), channel_id=1, source_target_pairs={{0,2},{2,0},{1,3},{3,1},{4,6},{6,4},{5,7},{7,5},{8,10},{10,8},{9,1... | collective-permute-start | bytes 811016 | tf_op jit(solution)/shard_map/ppermute | solution.py:842
  (99 other events, 702.7 us)
Sparse Core Ops, SparseCore 0:
  10.3 108.1 all-gather.1

commit v4 on v3

--- a/solution.py
+++ b/solution.py
@@ -803,6 +803,7 @@
 
         def rows_of(prefix, first, count):
             low, high = ins[prefix]
+            first = first + sources[prefix][3]
             half = low.shape[0]
             if first + count <= half:
                 return low[first : first + count, :].astype(F32)
@@ -942,6 +943,13 @@
         rows = total.shape[0] // 2
         low, high = total[:rows], total[rows:]
         self.keep, self.payload = jnp.where(self.odd, high, low), [jnp.where(self.odd, low, high)]
+
+    @staticmethod
+    def joined(a, b):
+        both = Sum(a.sizes, None, None, N.direct, a.odd)
+        both.steps = both.steps[-3:]
+        both.level_in(jnp.concatenate([a.plane_total, b.plane_total], axis=0))
+        return both
 
     def trade(self, sent):
         self.payload = [add(self.keep, along(sent[0], [(0, 1), (1, 0), (2, 3), (3, 2)]))]
@@ -1369,6 +1377,10 @@
                 if fast:
                     sums[m] = Sum(s, v[N.keep(m)], v[N.send(m)], modes[m], odd)
 
+        def join(m, a, b):
+            if fast:
+                sums[m] = Sum.joined(sums[a], sums[b])
+
         def open_kv(l):
             if fast:
                 sums[N.dkv(l)] = Sum(s, v[N.dkvkeep(l)], v[N.dkvsend(l)], N.direct)
@@ -1468,7 +1480,8 @@
             weights=wts((N.qkv, N.bq, N.aqkv), 0),
             micros=5.8,
         )
-        phase([N.dkv0, N.g3, N.g4], [N.rawq_low0], [N.g1, N.g2])
+        join(N.g12, N.g1, N.g2)
+        phase([N.dkv0, N.g3, N.g4], [N.rawq_low0], [N.g12])
         grads(
             [N.rb],
             fill([N.ho, N.omid, N.blow, N.omg, N.mid, N.rawq_low, N.attn_in, N.midgq], 0)
@@ -1476,7 +1489,7 @@
             7,
         )
         open_sum(N.rb)
-        phase([N.g3, N.g4, N.rb, N.g1, N.g2], [N.agrad0, N.stream2], [N.dkv0])
+        phase([N.g3, N.g4, N.rb, N.g12], [N.agrad0, N.stream2], [N.dkv0])
         close_kv(0)
         mixed = unsort_rows(s, rank, v[N.stream2])
         v[N.mixed] = mixed
@@ -1498,15 +1511,17 @@
         open_sum(N.ra)
         tokens_grad = unsort_rows(s, rank, v[N.sgrad0])
         v[N.tokens_grad] = tokens_grad
-        phase([N.g3, N.g4, N.ra, N.la], [], [N.mixed, N.tokens_grad, N.g1, N.g2])
-        phase([N.rb, N.g1, N.g2], [], [N.g3, N.g4, N.ra])
-        phase([N.ra, N.g3, N.g4], [], [N.rb, N.g1, N.g2])
-        phase([N.ra, N.rb, N.g3, N.g4, N.g1])
-        phase([N.ra, N.rb, N.g3, N.g4, N.g2])
+        phase([N.g3, N.g4, N.ra, N.la], [], [N.mixed, N.tokens_grad, N.g12])
+        join(N.g34, N.g3, N.g4)
+        phase([N.rb, N.g12], [], [N.g34, N.ra])
+        phase([N.ra, N.g34], [], [N.rb, N.g12])
+        phase([N.ra, N.rb, N.g34, N.g12])
+        phase([N.ra, N.rb, N.g34])
         phase([N.ra, N.rb])
-        for m in sums:
-            assert m in (N.dkv0, N.dkv1) or not sums[m].steps
-        finished = {m: sums[m].payload for m in plans if fast}
+        finished = {}
+        for m in plans if fast else ():
+            pair, first = {N.g1: (N.g12, 0), N.g2: (N.g12, N.g1), N.g3: (N.g34, 0), N.g4: (N.g34, N.g3)}.get(m, (m, 0))
+            finished[m] = (*sums[pair].payload, layouts[m], layouts[first].total if first else 0)
 
         HB, RB = s.HB, s.RB
         two = (0, 1)
@@ -1543,7 +1558,7 @@
             for which, last in ((early, []), (late, ends)):
                 chosen = [plan[i] for i in which] + last
                 used = sorted({part[1] for _, parts in chosen for part in parts})
-                results = unpack(s, chosen, {m: (*finished[m], layouts[m]) for m in used})
+                results = unpack(s, chosen, {m: finished[m] for m in used})
                 for i, value in zip(which, results):
                     made[i] = value
             grads, (norm_grad, heads_grad) = made, results[-2:]

time: 505 us -> 503 us (level)
  waiting for transfers between devices: 156 us -> 163 us
  other arithmetic: 74.1 us -> 67.3 us
    ppermute x21 -> x15, waiting for transfers between devices: 51.4 us -> 58.1 us  [along(): return lax.ppermute(value, 'dp', pairs)]
    convert_element_type x36 -> x32, other arithmetic: 56.4 us -> 52.9 us  [add(): return total.astype(BF)]
    ppermute x21 -> x15, starting transfers between devices: 22.5 us -> 19.2 us  [along(): return lax.ppermute(value, 'dp', pairs)]
  transfers between devices with their start and end apart: 89 -> 83, of which waited for: 32 -> 33; matrix products, arithmetic and copies ran while one was open for 12% -> 11% of each run, Pallas kernels for 26% -> 26%
where the time goes in v4:
time: 503 us; the launch traced here: 493 us
  waiting for transfers between devices  163 us (32%)
  Pallas kernels  160 us (32%)
  starting transfers between devices  71.4 us (14%)
  other arithmetic  67.3 us (13%)
  between operations  16.8 us (3%)
  local copies, waits for them, and re-layouts  14.5 us (3%)
    pallas_call x14, Pallas kernels, run_kernel(): pl.pallas_call(kernel, name=name, out_shape=[jax.ShapeDtypeStruct(*outs[k...  137 us
    ppermute x67, waiting for transfers between devices, swap(): return lax.ppermute(value, 'own', [(i, i ^ bit) for i in range(sizes.n)])  104 us
    ppermute x15, waiting for transfers between devices, along(): return lax.ppermute(value, 'dp', pairs)  58.1 us
    convert_element_type x32, other arithmetic, add(): return total.astype(BF)  52.9 us
    ppermute x67, starting transfers between devices, swap(): return lax.ppermute(value, 'own', [(i, i ^ bit) for i in range(sizes.n)])  52.2 us
    ppermute x15, starting transfers between devices, along(): return lax.ppermute(value, 'dp', pairs)  19.2 us
    unnamed x120, local copies, waits for them, and re-layouts  10.4 us
  transfers between devices with their start and end apart: 83, of which 33 were waited for; matrix products, arithmetic and copies ran while one was open for 11% of the time, Pallas kernels for 26%

profile of v4, /device:TPU:0, one launch (start us, length us, event | category | flops | bytes accessed | tf_op | source)
XLA Modules:
  0.0 493.1 jit_solution(14934819932071197696)
XLA Ops:
  7.3 2.9 pack.6.refs_3_
  13.0 2.9 collective-permute-start
  27.5 4.1 collective-permute-done.refs_0_
  38.9 13.3 %collective-permute-done.1.refs_1_.refs_7_.refs_33_.refs_10_.refs_18_.refs_9_.refs_13_ = bf16[1840,128]{1,0:T(8,128)(2,1)S(1)} collective-permute-done((bf16[1840,128]{1,0:T(8,128)(2,1)}, bf16[1840,128]{1,0:T(8,128)(2,1)S(1)}, u32[]{:S(2)}, u32[]{:S(2)}) %collective-permute-start.1) | collective-permute-done | bytes 471072 | tf_op jit(solution)/shard_map/ppermute | solution.py:839
  53.3 15.3 %collective-permute-done.2.refs_6_.refs_32_.refs_9_.refs_17_.refs_8_.refs_12_ = bf16[1840,128]{1,0:T(8,128)(2,1)S(1)} collective-permute-done((bf16[1840,128]{1,0:T(8,128)(2,1)S(1)}, bf16[1840,128]{1,0:T(8,128)(2,1)S(1)}, u32[]{:S(2)}, u32[]{:S(2)}) %collective-permute-start.2) | collective-permute-done | bytes 471072 | tf_op jit(solution)/shard_map/ppermute | solution.py:839
  73.4 6.4 %qkv0.1 = (f32[16,640]{1,0:T(8,128)}, f32[16,256]{1,0:T(8,128)}, bf16[256,640]{1,0:T(8,128)(2,1)}, bf16[3,256,256]{2,1,0:T(8,128)(2,1)}, f32[5,256,256]{2,1,0:T(...) custom-call(s32[8]{0:T(128)} %stack.47.refs_0_.refs_1_.refs_3_.refs_2_, ...), custom_call_target="tpu_custom_call" | custom-call | flops 6500000 | tf_op jit(solution)/shard_map/qkv0/pallas_call | solution.py:192
  81.3 11.2 %collective-permute-done.15.refs_23_.refs_21_.refs_17_.refs_25_.refs_6_ = bf16[1920,128]{1,0:T(8,128)(2,1)} collective-permute-done((bf16[1920,128]{1,0:T(8,128)(2,1)}, bf16[1920,128]{1,0:T(8,128)(2,1)}, u32[]{:S(2)}, u32[]{:S(2)}) %collective-permute-start.15) | collective-permute-done | bytes 491552 | tf_op jit(solution)/shard_map/ppermute | solution.py:839
  92.5 2.7 collective-permute-start.16
  97.0 13.0 %collective-permute-done.7.refs_14_.refs_9_ = bf16[256,512]{1,0:T(8,128)(2,1)S(1)} collective-permute-done((bf16[256,512]{1,0:T(8,128)(2,1)}, bf16[256,512]{1,0:T(8,128)(2,1)S(1)}, u32[]{:S(2)}, u32[]{:S(2)}) %collective-permute-start.7) | collective-permute-done | bytes 262176 | tf_op jit(solution)/shard_map/ppermute | solution.py:839
  119.0 18.8 %loop0.1 = (f32[4,256,256]{2,1,0:T(8,128)}, f32[4,256,128]{2,1,0:T(8,128)}, bf16[4,256,256]{2,1,0:T(8,128)(2,1)}, bf16[256,256]{1,0:T(8,128)(2,1)}, f32[256,640]...) custom-call(s32[4]{0:T(128)} %and_select_fusion.2.refs_0_, ...), custom_call_target="tpu_custom_call" | custom-call | flops 20000000 | tf_op jit(solution)/shard_map/loop0/pallas_call | solution.py:192
  141.4 5.9 %collective-permute-done.21.refs_12_ = bf16[256,512]{1,0:T(8,128)(2,1)} collective-permute-done((bf16[256,512]{1,0:T(8,128)(2,1)}, bf16[256,512]{1,0:T(8,128)(2,1)}, u32[]{:S(2)}, u32[]{:S(2)}) %collective-permute-start.21) | collective-permute-done | bytes 262176 | tf_op jit(solution)/shard_map/ppermute | solution.py:839
  148.7 4.5 collective-permute-done.22.refs_13_
  155.6 2.7 collective-permute-done.26.refs_17_
  161.6 27.3 %loop1.1 = (f32[256,640]{1,0:T(8,128)}, f32[256,640]{1,0:T(8,128)}, bf16[4,256,256]{2,1,0:T(8,128)(2,1)}, bf16[256,256]{1,0:T(8,128)(2,1)}, bf16[256,640]{1,0:T(...) custom-call(s32[4]{0:T(128)} %and_select_fusion.2.refs_0_, ...), custom_call_target="tpu_custom_call" | custom-call | flops 35000000 | tf_op jit(solution)/shard_map/loop1/pallas_call | solution.py:192
  189.8 6.5 %gradsla.1 = (bf16[4,2432,128]{2,1,0:T(8,128)(2,1)}, bf16[4,2432,128]{2,1,0:T(8,128)(2,1)}) custom-call(s32[2]{0:T(128)} %pad_add_fusion.refs_0_, bf16[256,640]{1,0:T(8,128)(2,1)} %get-tuple-element.204.refs_1_.refs_3_, bf16[2,256,256]{2,1,0:T(8,128)(2,1)} %get-tuple-element.205.refs_2_, bf16[16,256,256]{2,1,0:T(8,128)(2,1)} %get-tuple-element.206.refs_3_.refs_4_, ...), custom_call_target="tpu_custom_call" | custom-call | flops 8600000 | tf_op jit(solution)/shard_map/gradsla/pallas_call | solution.py:192
  198.7 2.5 collective-permute-start.38
  201.3 5.9 %q_back1.1 = (bf16[4,256,256]{2,1,0:T(8,128)(2,1)}, bf16[256,256]{1,0:T(8,128)(2,1)}, f32[256,640]{1,0:T(8,128)}, f32[1,256]{1,0:T(1,128)}) custom-call(s32[8]{0:T(128)} %stack.47.refs_0_.refs_1_.refs_3_.refs_2_, s32[8]{0:T(128)} %stack.47.refs_0_.refs_1_.refs_3_.refs_2_, f32[256,128]{1,0:T(8,128)} %get-tuple-element.387.refs_2_.refs_8_.refs_3_.refs_1_, ...), custom_call_target="tpu_custom_call" | custom-call | flops 5800000 | tf_op jit(solution)/shard_map/q_back1/pallas_call | solution.py:192
  207.2 5.6 %collective-permute-done.37 = bf16[256,512]{1,0:T(8,128)(2,1)S(1)} collective-permute-done((bf16[256,512]{1,0:T(8,128)(2,1)}, bf16[256,512]{1,0:T(8,128)(2,1)S(1)}, u32[]{:S(2)}, u32[]{:S(2)}) %collective-permute-start.37) | collective-permute-done | bytes 262176 | tf_op jit(solution)/shard_map/ppermute | solution.py:839
  214.7 3.0 fusion.18
  221.8 17.2 %kv_back1.1 = (f32[1,256]{1,0:T(1,128)}, bf16[2,256,256]{2,1,0:T(8,128)(2,1)}, bf16[2,256,256]{2,1,0:T(8,128)(2,1)}, f32[1,640]{1,0:T(1,128)}, f32[1,640]{1,0:T(...) custom-call(s32[8]{0:T(128)} %stack.47.refs_0_.refs_1_.refs_3_.refs_, ...), custom_call_target="tpu_custom_call" | custom-call | flops 17000000 | tf_op jit(solution)/shard_map/kv_back1/pallas_call | solution.py:192
  239.0 9.7 %gradsg1.1 = (bf16[4,1760,128]{2,1,0:T(8,128)(2,1)}, bf16[4,1760,128]{2,1,0:T(8,128)(2,1)}, bf16[4,1664,128]{2,1,0:T(8,128)(2,1)}, bf16[4,1664,128]{2,1,0:T(8,128)(2,1)}) custom-call(s32[2]{0:T(128)} %pad_add_fusion.refs_0_, bf16[256,640]{1,0:T(8,128)(2,1)} %get-tuple-element.190.refs_1_, bf16[16,256,256]{2,1,0:T(8,128)(2,1)} %get-tuple-element.231.refs_2_.refs_3_, ...), custom_call_target="tpu_custom_call" | custom-call | flops 9700000 | tf_op jit(solution)/shard_map/gradsg1/pallas_call | solution.py:192
  252.9 4.8 out_back0.1
  258.4 3.4 add_convert_fusion.4
  263.0 2.9 add_convert_fusion
  269.1 8.2 %gradsg3.1 = (bf16[4,1600,128]{2,1,0:T(8,128)(2,1)}, bf16[4,1600,128]{2,1,0:T(8,128)(2,1)}, bf16[4,1696,128]{2,1,0:T(8,128)(2,1)}, bf16[4,1696,128]{2,1,0:T(8,128)(2,1)}) custom-call(s32[2]{0:T(128)} %pad_add_fusion.refs_0_, bf16[256,640]{1,0:T(8,128)(2,1)} %get-tuple-element.190.refs_1_, bf16[2,256,256]{2,1,0:T(8,128)(2,1)} %get-tuple-element.191.refs_2_, ...), custom_call_target="tpu_custom_call" | custom-call | flops 8500000 | tf_op jit(solution)/shard_map/gradsg3/pallas_call | solution.py:192
  277.3 9.3 %attend_back0.1 = (f32[4,256,256]{2,1,0:T(8,128)}, bf16[4,256,512]{2,1,0:T(8,128)(2,1)}, bf16[4,256,512]{2,1,0:T(8,128)(2,1)}) custom-call(s32[4]{0:T(128)} %and_select_fusion.2.refs_0_, bf16[4,256,256]{2,1,0:T(8,128)(2,1)} %after.32.refs_1_, bf16[4,256,256]{2,1,0:T(8,128)(2,1)} %get-tuple-element.186.refs_5_.refs_2_, ...), custom_call_target="tpu_custom_call" | custom-call | flops 13000000 | tf_op jit(solution)/shard_map/attend_back0/pallas_call | solution.py:192
  293.7 5.7 %q_back0.1 = (bf16[4,256,256]{2,1,0:T(8,128)(2,1)}, bf16[256,256]{1,0:T(8,128)(2,1)}, f32[256,640]{1,0:T(8,128)}, f32[1,256]{1,0:T(1,128)}) custom-call(s32[8]{0:T(128)} %stack.47.refs_0_.refs_1_.refs_3_.refs_2_, f32[256,128]{1,0:T(8,128)} %get-tuple-element.387.refs_2_.refs_8_.refs_3_.refs_1_, ...), custom_call_target="tpu_custom_call" | custom-call | flops 5800000 | tf_op jit(solution)/shard_map/q_back0/pallas_call | solution.py:192
  299.4 3.2 collective-permute-done.50
  311.1 6.6 %gradsrb.1 = (bf16[4,2112,128]{2,1,0:T(8,128)(2,1)}, bf16[4,2112,128]{2,1,0:T(8,128)(2,1)}) custom-call(s32[2]{0:T(128)} %pad_add_fusion.refs_0_, bf16[4,256,256]{2,1,0:T(8,128)(2,1)} %get-tuple-element.279.refs_1_, bf16[256,256]{1,0:T(8,128)(2,1)} %get-tuple-element.280.refs_2_, bf16[256,640]{1,0:T(8,128)(2,1)} %get-tuple-element.256.refs_5_.refs_3_, ...), custom_call_target="tpu_custom_call" | custom-call | flops 7000000 | tf_op jit(solution)/shard_map/gradsrb/pallas_call | solution.py:192
  324.4 3.2 add_convert_fusion.6
  327.5 2.9 add_convert_fusion.2
  337.4 6.2 %kv_back0.1 = (f32[1,256]{1,0:T(1,128)}, bf16[2,256,256]{2,1,0:T(8,128)(2,1)}, bf16[2,256,256]{2,1,0:T(8,128)(2,1)}, f32[1,640]{1,0:T(1,128)}, f32[256,640]{1,0:T(8,128)}) custom-call(s32[8]{0:T(128)} %stack.47.refs_0_.refs_1_.refs_3_.refs_2_, f32[256,128]{1,0:T(8,128)} %get-tuple-element.387.refs_2_.refs_8_.refs_3_.refs_1_, ...), custom_call_target="tpu_custom_call" | custom-call | flops 6200000 | tf_op jit(solution)/shard_map/kv_back0/pallas_call | solution.py:192
  347.9 3.9 gradsra.1
  353.8 4.3 collective-permute-done.57
  362.3 9.0 %collective-permute-done.61 = bf16[1600,128]{1,0:T(8,128)(2,1)S(1)} collective-permute-done((bf16[1600,128]{1,0:T(8,128)(2,1)}, bf16[1600,128]{1,0:T(8,128)(2,1)S(1)}, u32[]{:S(2)}, u32[]{:S(2)}) %collective-permute-start.61) | collective-permute-done | bytes 409632 | tf_op jit(solution)/shard_map/ppermute | solution.py:839
  376.1 2.8 fusion.23
  382.5 17.2 %collective-permute-done.67 = bf16[1712,128]{1,0:T(8,128)(2,1)S(1)} collective-permute-done((bf16[1712,128]{1,0:T(8,128)(2,1)}, bf16[1712,128]{1,0:T(8,128)(2,1)S(1)}, u32[]{:S(2)}, u32[]{:S(2)}) %collective-permute-start.67) | collective-permute-done | bytes 438304 | tf_op jit(solution)/shard_map/ppermute | solution.py:843
  410.1 2.7 collective-permute-start.71
  413.6 2.8 collective-permute-done.69
  425.0 6.4 %collective-permute-done.74 = bf16[392,128]{1,0:T(8,128)(2,1)S(1)} collective-permute-done((bf16[392,128]{1,0:T(8,128)(2,1)}, bf16[392,128]{1,0:T(8,128)(2,1)S(1)}, u32[]{:S(2)}, u32[]{:S(2)}) %collective-permute-start.74) | collective-permute-done | bytes 100384 | tf_op jit(solution)/shard_map/ppermute | solution.py:843
  432.1 7.9 %collective-permute-done.75 = bf16[1056,128]{1,0:T(8,128)(2,1)S(1)} collective-permute-done((bf16[1056,128]{1,0:T(8,128)(2,1)}, bf16[1056,128]{1,0:T(8,128)(2,1)S(1)}, u32[]{:S(2)}, u32[]{:S(2)}) %collective-permute-start.75) | collective-permute-done | bytes 270368 | tf_op jit(solution)/shard_map/ppermute | solution.py:843
  440.8 2.6 collective-permute-done.76
  444.3 3.3 collective-permute-start.78
  450.6 9.8 %collective-permute-done.77 = bf16[392,128]{1,0:T(8,128)(2,1)S(1)} collective-permute-done((bf16[392,128]{1,0:T(8,128)(2,1)}, bf16[392,128]{1,0:T(8,128)(2,1)S(1)}, u32[]{:S(2)}, u32[]{:S(2)}) %collective-permute-start.77) | collective-permute-done | bytes 100384 | tf_op jit(solution)/shard_map/ppermute | solution.py:843
  462.8 3.7 collective-permute-done.72
  469.6 6.6 %collective-permute-done.79 = bf16[392,128]{1,0:T(8,128)(2,1)S(1)} collective-permute-done((bf16[392,128]{1,0:T(8,128)(2,1)}, bf16[392,128]{1,0:T(8,128)(2,1)S(1)}, u32[]{:S(2)}, u32[]{:S(2)}) %collective-permute-start.79) | collective-permute-done | bytes 100384 | tf_op jit(solution)/shard_map/ppermute | solution.py:843
  477.9 4.1 unpack.3
  482.8 3.2 unpack.2
  (355 shorter events, 148.2 us)
Async XLA Ops:
  7.2 111.3 %all-gather.2.cloned.1.call-start = ((), (), s32[]{:S(2)}) async-start(), calls=%async_computation | async-start | bytes 13492224 | tf_op jit(solution)/shard_map/all_gather | solution.py:1134
  13.0 18.6 %collective-permute-start = (bf16[1840,128]{1,0:T(8,128)(2,1)}, bf16[1840,128]{1,0:T(8,128)(2,1)S(1)}, u32[]{:S(2)}, u32[]{:S(2)}) collective-permute-start(bf16[1840,128]{1,0:T(8,128)(2,1)} %pack.5.refs_4_.refs_30_.refs_7_.refs_15_.refs_6_.refs_10_), channel_id=1, source_target_pairs={{0,8},{4,12},{8,0},{12,4},{16,24},{20,28},{24,16},{28,20},{1,9},{5... | collective-permute-start | bytes 1413128 | tf_op jit(solution)/shard_map/ppermute | solution.py:839
  32.4 19.8 %collective-permute-start.1 = (bf16[1840,128]{1,0:T(8,128)(2,1)}, bf16[1840,128]{1,0:T(8,128)(2,1)S(1)}, u32[]{:S(2)}, u32[]{:S(2)}) collective-permute-start(bf16[1840,128]{1,0:T(8,128)(2,1)} %after.21.refs_1_.refs_5_.refs_31_.refs_8_.refs_16_.refs_7_.refs_11_), channel_id=1, source_target_pairs={{0,16},{4,20},{8,24},{12,28},{16,0},{20,4},{24,8},{28,12},{1,17},{... | collective-permute-start | bytes 1413128 | tf_op jit(solution)/shard_map/ppermute | solution.py:839
  33.7 34.8 %collective-permute-start.2 = (bf16[1840,128]{1,0:T(8,128)(2,1)S(1)}, bf16[1840,128]{1,0:T(8,128)(2,1)S(1)}, u32[]{:S(2)}, u32[]{:S(2)}) collective-permute-start(bf16[1840,128]{1,0:T(8,128)(2,1)S(1)} %copy-done.3), channel_id=1, source_target_pairs={{0,16},{4,20},{8,24},{12,28},{16,0},{20,4},{24,8},{28,12},{1,17},{... | collective-permute-start | bytes 1413128 | tf_op jit(solution)/shard_map/ppermute | solution.py:839
  34.7 33.8 %collective-permute-start.3 = (bf16[1840,128]{1,0:T(8,128)(2,1)S(1)}, bf16[1840,128]{1,0:T(8,128)(2,1)S(1)}, u32[]{:S(2)}, u32[]{:S(2)}) collective-permute-start(bf16[1840,128]{1,0:T(8,128)(2,1)S(1)} %copy-done.3), channel_id=1, source_target_pairs={{0,4},{4,0},{8,12},{12,8},{16,20},{20,16},{24,28},{28,24},{1,5},{5... | collective-permute-start | bytes 1413128 | tf_op jit(solution)/shard_map/ppermute | solution.py:839
  35.5 33.6 %collective-permute-start.14 = (bf16[1920,128]{1,0:T(8,128)(2,1)}, bf16[1920,128]{1,0:T(8,128)(2,1)}, u32[]{:S(2)}, u32[]{:S(2)}) collective-permute-start(bf16[1920,128]{1,0:T(8,128)(2,1)} %after.22.refs_1_), channel_id=1, source_target_pairs={{0,8},{4,12},{8,0},{12,4},{16,24},{20,28},{24,16},{28,20},{1,9},{5... | collective-permute-start | bytes 1474568 | tf_op jit(solution)/shard_map/ppermute | solution.py:839
  37.9 31.1 %collective-permute-start.4 = (bf16[1840,128]{1,0:T(8,128)(2,1)S(1)}, bf16[1840,128]{1,0:T(8,128)(2,1)S(1)}, u32[]{:S(2)}, u32[]{:S(2)}) collective-permute-start(bf16[1840,128]{1,0:T(8,128)(2,1)S(1)} %copy-done.2), channel_id=1, source_target_pairs={{0,4},{4,0},{8,12},{12,8},{16,20},{20,16},{24,28},{28,24},{1,5},{5... | collective-permute-start | bytes 1413128 | tf_op jit(solution)/shard_map/ppermute | solution.py:839
  53.0 39.5 %collective-permute-start.15 = (bf16[1920,128]{1,0:T(8,128)(2,1)}, bf16[1920,128]{1,0:T(8,128)(2,1)}, u32[]{:S(2)}, u32[]{:S(2)}) collective-permute-start(bf16[1920,128]{1,0:T(8,128)(2,1)} %after.23.refs_2_), channel_id=1, source_target_pairs={{0,16},{4,20},{8,24},{12,28},{16,0},{20,4},{24,8},{28,12},{1,17},{... | collective-permute-start | bytes 1474568 | tf_op jit(solution)/shard_map/ppermute | solution.py:839
  69.1 26.3 %collective-permute-start.17 = (bf16[1920,128]{1,0:T(8,128)(2,1)S(1)}, bf16[1920,128]{1,0:T(8,128)(2,1)}, u32[]{:S(2)}, u32[]{:S(2)}) collective-permute-start(bf16[1920,128]{1,0:T(8,128)(2,1)S(1)} %copy-done), channel_id=1, source_target_pairs={{0,4},{4,0},{8,12},{12,8},{16,20},{20,16},{24,28},{28,24},{1,5},{5... | collective-permute-start | bytes 1474568 | tf_op jit(solution)/shard_map/ppermute | solution.py:839
  69.1 26.3 %collective-permute-start.18 = (bf16[1920,128]{1,0:T(8,128)(2,1)}, bf16[1920,128]{1,0:T(8,128)(2,1)}, u32[]{:S(2)}, u32[]{:S(2)}) collective-permute-start(bf16[1920,128]{1,0:T(8,128)(2,1)} %collective-permute-done.14.refs_22_.refs_20_.refs_16_.refs_24_.refs_5_), channel_id=1, source_target_pairs={{0,4},{4,0},{8,12},{12,8},{16,20},{20,16},{24,28},{28,24},{1,5},{5... | collective-permute-start | bytes 1474568 | tf_op jit(solution)/shard_map/ppermute | solution.py:839
  79.8 16.4 %collective-permute-start.9 = (bf16[256,512]{1,0:T(8,128)(2,1)}, bf16[256,512]{1,0:T(8,128)(2,1)S(1)}, u32[]{:S(2)}, u32[]{:S(2)}) collective-permute-start(bf16[256,512]{1,0:T(8,128)(2,1)} %get-tuple-element.189.refs_13_.refs_8_), channel_id=1, source_target_pairs={{0,24},{4,28},{8,16},{12,20},{16,8},{20,12},{24,0},{28,4},{1,25},{... | collective-permute-start | bytes 786440 | tf_op jit(solution)/shard_map/ppermute | solution.py:839
  92.5 19.4 %collective-permute-start.16 = (bf16[1920,128]{1,0:T(8,128)(2,1)}, bf16[1920,128]{1,0:T(8,128)(2,1)S(1)}, u32[]{:S(2)}, u32[]{:S(2)}) collective-permute-start(bf16[1920,128]{1,0:T(8,128)(2,1)} %collective-permute-done.15.refs_23_.refs_21_.refs_17_.refs_25_.refs_6_), channel_id=1, source_target_pairs={{0,8},{4,12},{8,0},{12,4},{16,24},{20,28},{24,16},{28,20},{1,9},{5... | collective-permute-start | bytes 1474568 | tf_op jit(solution)/shard_map/ppermute | solution.py:839
  95.1 17.4 %collective-permute-start.19 = (bf16[1920,128]{1,0:T(8,128)(2,1)}, bf16[1920,128]{1,0:T(8,128)(2,1)S(1)}, u32[]{:S(2)}, u32[]{:S(2)}) collective-permute-start(bf16[1920,128]{1,0:T(8,128)(2,1)} %collective-permute-done.15.refs_23_.refs_21_.refs_17_.refs_25_.refs_6_), channel_id=1, source_target_pairs={{0,4},{4,0},{8,12},{12,8},{16,20},{20,16},{24,28},{28,24},{1,5},{5... | collective-permute-start | bytes 1474568 | tf_op jit(solution)/shard_map/ppermute | solution.py:839
  95.3 14.7 %collective-permute-start.7 = (bf16[256,512]{1,0:T(8,128)(2,1)}, bf16[256,512]{1,0:T(8,128)(2,1)S(1)}, u32[]{:S(2)}, u32[]{:S(2)}) collective-permute-start(bf16[256,512]{1,0:T(8,128)(2,1)} %get-tuple-element.189.refs_13_.refs_8_), channel_id=1, source_target_pairs={{0,8},{4,12},{8,0},{12,4},{16,24},{20,28},{24,16},{28,20},{1,9},{5... | collective-permute-start | bytes 786440 | tf_op jit(solution)/shard_map/ppermute | solution.py:839
  95.4 14.9 %collective-permute-start.8 = (bf16[256,512]{1,0:T(8,128)(2,1)}, bf16[256,512]{1,0:T(8,128)(2,1)S(1)}, u32[]{:S(2)}, u32[]{:S(2)}) collective-permute-start(bf16[256,512]{1,0:T(8,128)(2,1)} %get-tuple-element.189.refs_13_.refs_8_), channel_id=1, source_target_pairs={{0,16},{4,20},{8,24},{12,28},{16,0},{20,4},{24,8},{28,12},{1,17},{... | collective-permute-start | bytes 786440 | tf_op jit(solution)/shard_map/ppermute | solution.py:839
  96.3 15.6 %collective-permute-start.10 = (bf16[256,512]{1,0:T(8,128)(2,1)}, bf16[256,512]{1,0:T(8,128)(2,1)S(1)}, u32[]{:S(2)}, u32[]{:S(2)}) collective-permute-start(bf16[256,512]{1,0:T(8,128)(2,1)} %get-tuple-element.189.refs_13_.refs_8_), channel_id=1, source_target_pairs={{0,4},{4,0},{8,12},{12,8},{16,20},{20,16},{24,28},{28,24},{1,5},{5... | collective-permute-start | bytes 786440 | tf_op jit(solution)/shard_map/ppermute | solution.py:839
  110.0 29.4 %collective-permute-start.28 = (bf16[2432,128]{1,0:T(8,128)(2,1)}, bf16[2432,128]{1,0:T(8,128)(2,1)S(1)}, u32[]{:S(2)}, u32[]{:S(2)}) collective-permute-start(bf16[2432,128]{1,0:T(8,128)(2,1)} %after.25.refs_0_), channel_id=1, source_target_pairs={{0,8},{4,12},{8,0},{12,4},{16,24},{20,28},{24,16},{28,20},{1,9},{5... | collective-permute-start | bytes 1867784 | tf_op jit(solution)/shard_map/ppermute | solution.py:839
  110.3 31.1 %collective-permute-start.29 = (bf16[2432,128]{1,0:T(8,128)(2,1)}, bf16[2432,128]{1,0:T(8,128)(2,1)S(1)}, u32[]{:S(2)}, u32[]{:S(2)}) collective-permute-start(bf16[2432,128]{1,0:T(8,128)(2,1)} %after.25.refs_0_), channel_id=1, source_target_pairs={{0,16},{4,20},{8,24},{12,28},{16,0},{20,4},{24,8},{28,12},{1,17},{... | collective-permute-start | bytes 1867784 | tf_op jit(solution)/shard_map/ppermute | solution.py:839
  115.4 32.0 %collective-permute-start.30 = (bf16[2432,128]{1,0:T(8,128)(2,1)}, bf16[2432,128]{1,0:T(8,128)(2,1)S(1)}, u32[]{:S(2)}, u32[]{:S(2)}) collective-permute-start(bf16[2432,128]{1,0:T(8,128)(2,1)} %after.25.refs_0_), channel_id=1, source_target_pairs={{0,24},{4,28},{8,16},{12,20},{16,8},{20,12},{24,0},{28,4},{1,25},{... | collective-permute-start | bytes 1867784 | tf_op jit(solution)/shard_map/ppermute | solution.py:839
  139.2 14.0 %collective-permute-start.22 = (bf16[256,512]{1,0:T(8,128)(2,1)}, bf16[256,512]{1,0:T(8,128)(2,1)S(1)}, u32[]{:S(2)}, u32[]{:S(2)}) collective-permute-start(bf16[256,512]{1,0:T(8,128)(2,1)} %get-tuple-element.195.refs_11_), channel_id=1, source_target_pairs={{0,16},{4,20},{8,24},{12,28},{16,0},{20,4},{24,8},{28,12},{1,17},{... | collective-permute-start | bytes 786440 | tf_op jit(solution)/shard_map/ppermute | solution.py:839
  139.4 14.5 %collective-permute-start.23 = (bf16[256,512]{1,0:T(8,128)(2,1)}, bf16[256,512]{1,0:T(8,128)(2,1)S(1)}, u32[]{:S(2)}, u32[]{:S(2)}) collective-permute-start(bf16[256,512]{1,0:T(8,128)(2,1)} %get-tuple-element.195.refs_11_), channel_id=1, source_target_pairs={{0,24},{4,28},{8,16},{12,20},{16,8},{20,12},{24,0},{28,4},{1,25},{... | collective-permute-start | bytes 786440 | tf_op jit(solution)/shard_map/ppermute | solution.py:839
  197.6 17.1 %collective-permute-start.39 = (bf16[4,2432,128]{2,1,0:T(8,128)(2,1)}, bf16[4,2432,128]{2,1,0:T(8,128)(2,1)}, u32[]{:S(2)}, u32[]{:S(2)}) collective-permute-start(bf16[4,2432,128]{2,1,0:T(8,128)(2,1)} %get-tuple-element.223), channel_id=1, source_target_pairs={{0,4},{4,0},{8,12},{12,8},{16,20},{20,16},{24,28},{28,24},{1,5},{5... | collective-permute-start | bytes 7471112 | tf_op jit(solution)/shard_map/ppermute | solution.py:839
  198.7 14.1 %collective-permute-start.37 = (bf16[256,512]{1,0:T(8,128)(2,1)}, bf16[256,512]{1,0:T(8,128)(2,1)S(1)}, u32[]{:S(2)}, u32[]{:S(2)}) collective-permute-start(bf16[256,512]{1,0:T(8,128)(2,1)} %get-tuple-element.219), channel_id=1, source_target_pairs={{0,16},{4,20},{8,24},{12,28},{16,0},{20,4},{24,8},{28,12},{1,17},{... | collective-permute-start | bytes 786440 | tf_op jit(solution)/shard_map/ppermute | solution.py:839
  198.7 14.1 %collective-permute-start.38 = (bf16[256,512]{1,0:T(8,128)(2,1)}, bf16[256,512]{1,0:T(8,128)(2,1)S(1)}, u32[]{:S(2)}, u32[]{:S(2)}) collective-permute-start(bf16[256,512]{1,0:T(8,128)(2,1)} %get-tuple-element.220), channel_id=1, source_target_pairs={{0,24},{4,28},{8,16},{12,20},{16,8},{20,12},{24,0},{28,4},{1,25},{... | collective-permute-start | bytes 786440 | tf_op jit(solution)/shard_map/ppermute | solution.py:839
  217.7 31.0 %collective-permute-start.40 = (bf16[2432,128]{1,0:T(8,128)(2,1)}, bf16[2432,128]{1,0:T(8,128)(2,1)S(1)}, u32[]{:S(2)}, u32[]{:S(2)}) collective-permute-start(bf16[2432,128]{1,0:T(8,128)(2,1)} %get-tuple-element.246), channel_id=1, source_target_pairs={{0,8},{4,12},{8,0},{12,4},{16,24},{20,28},{24,16},{28,20},{1,9},{5... | collective-permute-start | bytes 1867784 | tf_op jit(solution)/shard_map/ppermute | solution.py:839
  218.8 30.0 %collective-permute-start.41 = (bf16[2432,128]{1,0:T(8,128)(2,1)}, bf16[2432,128]{1,0:T(8,128)(2,1)}, u32[]{:S(2)}, u32[]{:S(2)}) collective-permute-start(bf16[2432,128]{1,0:T(8,128)(2,1)} %get-tuple-element.247), channel_id=1, source_target_pairs={{0,16},{4,20},{8,24},{12,28},{16,0},{20,4},{24,8},{28,12},{1,17},{... | collective-permute-start | bytes 1867784 | tf_op jit(solution)/shard_map/ppermute | solution.py:839
  219.5 30.1 %collective-permute-start.42 = (bf16[2432,128]{1,0:T(8,128)(2,1)}, bf16[2432,128]{1,0:T(8,128)(2,1)}, u32[]{:S(2)}, u32[]{:S(2)}) collective-permute-start(bf16[2432,128]{1,0:T(8,128)(2,1)} %get-tuple-element.248), channel_id=1, source_target_pairs={{0,24},{4,28},{8,16},{12,20},{16,8},{20,12},{24,0},{28,4},{1,25},{... | collective-permute-start | bytes 1867784 | tf_op jit(solution)/shard_map/ppermute | solution.py:839
  265.9 22.5 %collective-permute-start.46 = (bf16[2,1664,128]{2,1,0:T(8,128)(2,1)}, bf16[2,1664,128]{2,1,0:T(8,128)(2,1)}, u32[]{:S(2)}, u32[]{:S(2)}) collective-permute-start(bf16[2,1664,128]{2,1,0:T(8,128)(2,1)} %get-tuple-element.265), channel_id=1, source_target_pairs={{0,16},{4,20},{8,24},{12,28},{16,0},{20,4},{24,8},{28,12},{1,17},{... | collective-permute-start | bytes 2555912 | tf_op jit(solution)/shard_map/ppermute | solution.py:839
  266.7 19.8 %collective-permute-start.47 = (bf16[1216,128]{1,0:T(8,128)(2,1)}, bf16[1216,128]{1,0:T(8,128)(2,1)}, u32[]{:S(2)}, u32[]{:S(2)}) collective-permute-start(bf16[1216,128]{1,0:T(8,128)(2,1)} %get-tuple-element.266), channel_id=1, source_target_pairs={{0,1},{1,0},{2,3},{3,2},{4,5},{5,4},{6,7},{7,6},{8,9},{9,8},{10,11... | collective-permute-start | bytes 933896 | tf_op jit(solution)/shard_map/ppermute | solution.py:843
  268.2 22.1 %collective-permute-start.45 = (bf16[2,1760,128]{2,1,0:T(8,128)(2,1)}, bf16[2,1760,128]{2,1,0:T(8,128)(2,1)S(1)}, u32[]{:S(2)}, u32[]{:S(2)}) collective-permute-start(bf16[2,1760,128]{2,1,0:T(8,128)(2,1)} %get-tuple-element.264), channel_id=1, source_target_pairs={{0,8},{4,12},{8,0},{12,4},{16,24},{20,28},{24,16},{28,20},{1,9},{5... | collective-permute-start | bytes 2703368 | tf_op jit(solution)/shard_map/ppermute | solution.py:839
  307.1 17.3 %collective-permute-start.51 = (bf16[4,1600,128]{2,1,0:T(8,128)(2,1)}, bf16[4,1600,128]{2,1,0:T(8,128)(2,1)}, u32[]{:S(2)}, u32[]{:S(2)}) collective-permute-start(bf16[4,1600,128]{2,1,0:T(8,128)(2,1)} %get-tuple-element.276), channel_id=1, source_target_pairs={{0,4},{4,0},{8,12},{12,8},{16,20},{20,16},{24,28},{28,24},{1,5},{5... | collective-permute-start | bytes 4915208 | tf_op jit(solution)/shard_map/ppermute | solution.py:839
  307.1 20.4 %collective-permute-start.52 = (bf16[4,1696,128]{2,1,0:T(8,128)(2,1)}, bf16[4,1696,128]{2,1,0:T(8,128)(2,1)}, u32[]{:S(2)}, u32[]{:S(2)}) collective-permute-start(bf16[4,1696,128]{2,1,0:T(8,128)(2,1)} %get-tuple-element.278), channel_id=1, source_target_pairs={{0,4},{4,0},{8,12},{12,8},{16,20},{20,16},{24,28},{28,24},{1,5},{5... | collective-permute-start | bytes 5210120 | tf_op jit(solution)/shard_map/ppermute | solution.py:839
  317.7 16.5 %collective-permute-start.58 = (bf16[1216,128]{1,0:T(8,128)(2,1)}, bf16[1216,128]{1,0:T(8,128)(2,1)}, u32[]{:S(2)}, u32[]{:S(2)}) collective-permute-start(bf16[1216,128]{1,0:T(8,128)(2,1)} %get-tuple-element.313), channel_id=1, source_target_pairs={{0,2},{2,0},{1,3},{3,1},{4,6},{6,4},{5,7},{7,5},{8,10},{10,8},{9,1... | collective-permute-start | bytes 933896 | tf_op jit(solution)/shard_map/ppermute | solution.py:843
  330.4 21.4 %collective-permute-start.59 = (bf16[1712,128]{1,0:T(8,128)(2,1)}, bf16[1712,128]{1,0:T(8,128)(2,1)S(1)}, u32[]{:S(2)}, u32[]{:S(2)}) collective-permute-start(bf16[1712,128]{1,0:T(8,128)(2,1)} %get-tuple-element.314), channel_id=1, source_target_pairs={{0,1},{1,0},{2,3},{3,2},{4,5},{5,4},{6,7},{7,6},{8,9},{9,8},{10,11... | collective-permute-start | bytes 1314824 | tf_op jit(solution)/shard_map/ppermute | solution.py:843
  330.9 21.8 %collective-permute-start.56 = (bf16[2,1600,128]{2,1,0:T(8,128)(2,1)}, bf16[2,1600,128]{2,1,0:T(8,128)(2,1)S(1)}, u32[]{:S(2)}, u32[]{:S(2)}) collective-permute-start(bf16[2,1600,128]{2,1,0:T(8,128)(2,1)} %get-tuple-element.310), channel_id=1, source_target_pairs={{0,8},{4,12},{8,0},{12,4},{16,24},{20,28},{24,16},{28,20},{1,9},{5... | collective-permute-start | bytes 2457608 | tf_op jit(solution)/shard_map/ppermute | solution.py:839
  336.0 40.1 %collective-permute-start.63 = (bf16[4,2112,128]{2,1,0:T(8,128)(2,1)}, bf16[4,2112,128]{2,1,0:T(8,128)(2,1)}, u32[]{:S(2)}, u32[]{:S(2)}) collective-permute-start(bf16[4,2112,128]{2,1,0:T(8,128)(2,1)} %get-tuple-element.319), channel_id=1, source_target_pairs={{0,4},{4,0},{8,12},{12,8},{16,20},{20,16},{24,28},{28,24},{1,5},{5... | collective-permute-start | bytes 6488072 | tf_op jit(solution)/shard_map/ppermute | solution.py:839
  336.1 22.0 %collective-permute-start.57 = (bf16[2,1696,128]{2,1,0:T(8,128)(2,1)}, bf16[2,1696,128]{2,1,0:T(8,128)(2,1)}, u32[]{:S(2)}, u32[]{:S(2)}) collective-permute-start(bf16[2,1696,128]{2,1,0:T(8,128)(2,1)} %get-tuple-element.311), channel_id=1, source_target_pairs={{0,16},{4,20},{8,24},{12,28},{16,0},{20,4},{24,8},{28,12},{1,17},{... | collective-permute-start | bytes 2605064 | tf_op jit(solution)/shard_map/ppermute | solution.py:839
  378.9 20.9 %collective-permute-start.67 = (bf16[1712,128]{1,0:T(8,128)(2,1)}, bf16[1712,128]{1,0:T(8,128)(2,1)S(1)}, u32[]{:S(2)}, u32[]{:S(2)}) collective-permute-start(bf16[1712,128]{1,0:T(8,128)(2,1)} %get-tuple-element.323), channel_id=1, source_target_pairs={{0,2},{2,0},{1,3},{3,1},{4,6},{6,4},{5,7},{7,5},{8,10},{10,8},{9,1... | collective-permute-start | bytes 1314824 | tf_op jit(solution)/shard_map/ppermute | solution.py:843
  379.1 22.6 %collective-permute-start.64 = (bf16[2112,128]{1,0:T(8,128)(2,1)}, bf16[2112,128]{1,0:T(8,128)(2,1)S(1)}, u32[]{:S(2)}, u32[]{:S(2)}) collective-permute-start(bf16[2112,128]{1,0:T(8,128)(2,1)} %get-tuple-element.320), channel_id=1, source_target_pairs={{0,8},{4,12},{8,0},{12,4},{16,24},{20,28},{24,16},{28,20},{1,9},{5... | collective-permute-start | bytes 1622024 | tf_op jit(solution)/shard_map/ppermute | solution.py:839
  380.0 23.1 %collective-permute-start.65 = (bf16[2112,128]{1,0:T(8,128)(2,1)}, bf16[2112,128]{1,0:T(8,128)(2,1)S(1)}, u32[]{:S(2)}, u32[]{:S(2)}) collective-permute-start(bf16[2112,128]{1,0:T(8,128)(2,1)} %get-tuple-element.321), channel_id=1, source_target_pairs={{0,16},{4,20},{8,24},{12,28},{16,0},{20,4},{24,8},{28,12},{1,17},{... | collective-permute-start | bytes 1622024 | tf_op jit(solution)/shard_map/ppermute | solution.py:839
  381.0 23.2 %collective-permute-start.66 = (bf16[2112,128]{1,0:T(8,128)(2,1)}, bf16[2112,128]{1,0:T(8,128)(2,1)S(1)}, u32[]{:S(2)}, u32[]{:S(2)}) collective-permute-start(bf16[2112,128]{1,0:T(8,128)(2,1)} %get-tuple-element.322), channel_id=1, source_target_pairs={{0,24},{4,28},{8,16},{12,20},{16,8},{20,12},{24,0},{28,4},{1,25},{... | collective-permute-start | bytes 1622024 | tf_op jit(solution)/shard_map/ppermute | solution.py:839
  422.7 17.3 %collective-permute-start.75 = (bf16[1056,128]{1,0:T(8,128)(2,1)}, bf16[1056,128]{1,0:T(8,128)(2,1)S(1)}, u32[]{:S(2)}, u32[]{:S(2)}) collective-permute-start(bf16[1056,128]{1,0:T(8,128)(2,1)} %get-tuple-element.331), channel_id=1, source_target_pairs={{0,1},{1,0},{2,3},{3,2},{4,5},{5,4},{6,7},{7,6},{8,9},{9,8},{10,11... | collective-permute-start | bytes 811016 | tf_op jit(solution)/shard_map/ppermute | solution.py:843
  422.7 25.0 %collective-permute-start.73 = (bf16[1216,128]{1,0:T(8,128)(2,1)S(1)}, bf16[1216,128]{1,0:T(8,128)(2,1)S(1)}, u32[]{:S(2)}, u32[]{:S(2)}) collective-permute-start(bf16[1216,128]{1,0:T(8,128)(2,1)S(1)} %copy-done.19), channel_id=1, source_target_pairs={{0,1},{1,0},{2,3},{3,2},{4,5},{5,4},{6,7},{7,6},{8,9},{9,8},{10,11... | collective-permute-start | bytes 933896 | tf_op jit(solution)/shard_map/ppermute | solution.py:843
  424.7 18.7 %collective-permute-start.76 = (bf16[1648,128]{1,0:T(8,128)(2,1)}, bf16[1648,128]{1,0:T(8,128)(2,1)S(1)}, u32[]{:S(2)}, u32[]{:S(2)}) collective-permute-start(bf16[1648,128]{1,0:T(8,128)(2,1)} %get-tuple-element.332), channel_id=1, source_target_pairs={{0,2},{2,0},{1,3},{3,1},{4,6},{6,4},{5,7},{7,5},{8,10},{10,8},{9,1... | collective-permute-start | bytes 1265672 | tf_op jit(solution)/shard_map/ppermute | solution.py:843
  444.3 17.7 %collective-permute-start.78 = (bf16[1056,128]{1,0:T(8,128)(2,1)}, bf16[1056,128]{1,0:T(8,128)(2,1)S(1)}, u32[]{:S(2)}, u32[]{:S(2)}) collective-permute-start(bf16[1056,128]{1,0:T(8,128)(2,1)} %get-tuple-element.334), channel_id=1, source_target_pairs={{0,2},{2,0},{1,3},{3,1},{4,6},{6,4},{5,7},{7,5},{8,10},{10,8},{9,1... | collective-permute-start | bytes 811016 | tf_op jit(solution)/shard_map/ppermute | solution.py:843
  448.6 17.9 %collective-permute-start.72 = (bf16[1712,128]{1,0:T(8,128)(2,1)S(1)}, bf16[1712,128]{1,0:T(8,128)(2,1)S(1)}, u32[]{:S(2)}, u32[]{:S(2)}) collective-permute-start(bf16[1712,128]{1,0:T(8,128)(2,1)S(1)} %copy-done.13), channel_id=1, source_target_pairs={{0,1},{1,0},{2,3},{3,2},{4,5},{5,4},{6,7},{7,6},{8,9},{9,8},{10,11... | collective-permute-start | bytes 1314824 | tf_op jit(solution)/shard_map/ppermute | solution.py:843
  450.5 26.5 %collective-permute-start.81 = (bf16[1648,128]{1,0:T(8,128)(2,1)}, bf16[1648,128]{1,0:T(8,128)(2,1)S(1)}, u32[]{:S(2)}, u32[]{:S(2)}) collective-permute-start(bf16[1648,128]{1,0:T(8,128)(2,1)} %get-tuple-element.339), channel_id=1, source_target_pairs={{0,1},{1,0},{2,3},{3,2},{4,5},{5,4},{6,7},{7,6},{8,9},{9,8},{10,11... | collective-permute-start | bytes 1265672 | tf_op jit(solution)/shard_map/ppermute | solution.py:843
  467.5 14.5 %collective-permute-start.80 = (bf16[1056,128]{1,0:T(8,128)(2,1)S(1)}, bf16[1056,128]{1,0:T(8,128)(2,1)S(1)}, u32[]{:S(2)}, u32[]{:S(2)}) collective-permute-start(bf16[1056,128]{1,0:T(8,128)(2,1)S(1)} %copy-done.25), channel_id=1, source_target_pairs={{0,1},{1,0},{2,3},{3,2},{4,5},{5,4},{6,7},{7,6},{8,9},{9,8},{10,11... | collective-permute-start | bytes 811016 | tf_op jit(solution)/shard_map/ppermute | solution.py:843
  (93 other events, 578.4 us)
Sparse Core Ops, SparseCore 0:
  10.3 108.1 all-gather.1
